TPU v7x, 256 devices: a whole 4x4x8 slice. The times are simulated.
256 devices in a mesh: ka: 64 (over x, z, y_lo), ga: 4 (over y_hi, core).
Axes of the slice: x: 4, y: 4 (y_hi: 2, y_lo: 2; y = y_hi * 2 + y_lo), z: 8, core: 2. Of those that a mesh axis runs over, the one named last changes fastest.
Arguments:
- bloch_samples: bfloat16 [384, 2, 8, 1024], P('ka'), may hold values from -6 to 6
- zeta_vectors: bfloat16 [1024, 2, 1024], P(None, None, 'ga'), may hold values from -0.01171875 to 0.01171875
- screened: bfloat16 [22, 2, 1024, 1024], P(None, None, ('ga', 'ka')), may hold values from -1 to 9, as said below
- pair_slots: int32 [384, 2, 6], P('ka'), may hold values from 0 to 21
Outputs:
- kernel: float32 [384, 4, 2, 1536], P('ka', None, None, 'ga')
Inputs may be any that keep to these rules, and one draw needn't show every extreme that they name: pair_slots[k, o, j2] is the slot in the first dimension of screened used for the pair of k-point k and the j2-th k-point of the block o + 1 blocks after the block of k, blocks taken cyclically; slots may be assigned arbitrarily. Every screened[s] is Hermitian: screened[s, 0] is symmetric and screened[s, 1] antisymmetric.
All inputs are finite; a program needn't handle non-finite values.
Results may differ from a plain program's by a relative error of at most 0.0051.
Values may be sent and summed in bfloat16 or wider, within the bound.
No kernel may reach another device: no remote copies, remote signals or barrier semaphores. Data moves between devices by JAX's collectives and lax.ppermute only.
A program may use at most 128 MiB of HBM per device.

v0:
```python
import jax
import jax.numpy as jnp
from jax import lax
from jax.sharding import PartitionSpec as P

NV = 4
NC = 4
NG = 1024


group_size = 8


def from_behind(x, axis, by):
    count = lax.axis_size(axis)
    return lax.ppermute(x, axis, [(i, (i + by) % count) for i in range(count)])


def pair_products(left_bands, right_bands):
    left_real = left_bands[:, 0].astype(jnp.float32)[:, None, :, None, :]
    left_imag = left_bands[:, 1].astype(jnp.float32)[:, None, :, None, :]
    right_real = right_bands[:, 0].astype(jnp.float32)[None, :, None, :, :]
    right_imag = right_bands[:, 1].astype(jnp.float32)[None, :, None, :, :]
    real_part = left_real * right_real + left_imag * right_imag
    imag_part = left_real * right_imag - left_imag * right_real
    return (real_part.astype(jnp.bfloat16), imag_part.astype(jnp.bfloat16))


def products_for(bloch_samples, partners, band_low, band_high):
    real_parts = []
    imag_parts = []
    for partner in partners:
        real_part, imag_part = pair_products(
            bloch_samples[:, :, band_low:band_high], partner[:, :, band_low:band_high]
        )
        real_parts.append(real_part.reshape(-1, real_part.shape[-1]))
        imag_parts.append(imag_part.reshape(-1, imag_part.shape[-1]))
    return (jnp.concatenate(real_parts, axis=0), jnp.concatenate(imag_parts, axis=0))


def local_densities(flat_real, flat_imag, zeta_vectors):
    points = zeta_vectors.shape[0]
    slice_width = zeta_vectors.shape[2]
    vectors = zeta_vectors.reshape(points, 2 * slice_width)
    from_real = jnp.dot(flat_real, vectors, preferred_element_type=jnp.float32)
    from_imag = jnp.dot(flat_imag, vectors, preferred_element_type=jnp.float32)
    density_real = from_real[:, :slice_width] - from_imag[:, slice_width:]
    density_imag = from_real[:, slice_width:] + from_imag[:, :slice_width]
    return jnp.stack([density_real, density_imag], axis=1).astype(jnp.bfloat16)


def arranged(values, block_points):
    shaped = values.reshape(2, block_points, block_points, 2, NC, NC, NV, NV)
    length = block_points * NV * NC * NV * NC
    own_rows = jnp.transpose(shaped, (1, 0, 3, 2, 6, 4, 7, 5)).reshape(block_points, 2, 2, length)
    mirror = jnp.transpose(shaped, (2, 0, 3, 1, 7, 5, 6, 4)).reshape(block_points, 2, 2, length)
    mirror = mirror * jnp.array([1.0, -1.0], dtype=jnp.float32).reshape(1, 1, 2, 1)
    return (own_rows, mirror)


def by_groups(compute, slot_list, operands):
    count = slot_list.shape[0] // group_size

    def one_group(index):
        pieces = tuple(
            (lax.dynamic_slice_in_dim(item, index * group_size, group_size, 0) for item in operands)
        )
        slots = lax.dynamic_slice_in_dim(slot_list, index * group_size, group_size, 0)
        return compute(slots, pieces)

    results = lax.map(one_group, jnp.arange(count, dtype=jnp.int32))
    return results.reshape((count * group_size,) + results.shape[2:])


def forward_parts(applied):
    shaped = applied.reshape(applied.shape[0], 2, applied.shape[2], applied.shape[3] // 2, 2)
    screened_real = shaped[:, 0, :, :, 0] - shaped[:, 1, :, :, 1]
    screened_imag = shaped[:, 0, :, :, 1] + shaped[:, 1, :, :, 0]
    return (screened_real, screened_imag)


def contract(left, screened_real, screened_imag):
    bands = left.shape[1]
    lefts = jnp.concatenate([left[:, :, 0], left[:, :, 1]], axis=1).astype(jnp.float32)
    rights = jnp.concatenate([screened_real, screened_imag], axis=2)
    product = jnp.einsum("pag,pgb->pab", lefts, rights, precision=lax.Precision.HIGHEST)
    kernel_real = product[:, :bands, :bands] + product[:, bands:, bands:]
    kernel_imag = product[:, :bands, bands:] - product[:, bands:, :bands]
    return jnp.stack([kernel_real, kernel_imag], axis=1)


def body(bloch_samples, zeta_vectors, screened, pair_slots):
    block_points = bloch_samples.shape[0]
    pair_count = 2 * block_points * block_points
    slice_width = zeta_vectors.shape[2]
    ga_count = lax.axis_size("ga")
    ga_index = lax.axis_index("ga")
    partners = []
    for offset in (1, 2):
        partners.append(from_behind(bloch_samples, "ka", -offset))
    cond_real, cond_imag = products_for(bloch_samples, partners, NV, NV + NC)
    val_real, val_imag = products_for(bloch_samples, partners, 0, NV)
    pair_slot_list = jnp.transpose(pair_slots, (1, 0, 2)).reshape(pair_count)
    conduction = local_densities(cond_real, cond_imag, zeta_vectors).reshape(
        pair_count, NC * NC, 2, slice_width
    )
    valence_local = local_densities(val_real, val_imag, zeta_vectors).reshape(
        pair_count, NV * NV, 2, slice_width
    )
    valence = lax.all_gather(valence_local, "ga", axis=3, tiled=True)
    valence_columns = valence.reshape(pair_count, NV * NV * 2, NG)
    row_piece = lax.all_gather(screened, "ka", axis=2, tiled=True)

    def compute(slots, groups):
        chosen = jnp.take(row_piece, slots, axis=0)
        return jnp.einsum("prgh,pch->prgc", chosen, groups[0], preferred_element_type=jnp.float32)

    applied = by_groups(compute, pair_slot_list, (valence_columns,))
    screened_real, screened_imag = forward_parts(applied)
    direct = contract(conduction, screened_real, screened_imag)
    summed = lax.psum(direct, "ga")
    own_rows, mirror = arranged(summed, block_points)
    share_width = own_rows.shape[3] // ga_count
    lower_edge = ga_index * share_width
    own_part = lax.dynamic_slice_in_dim(own_rows, lower_edge, share_width, 3)
    back_part = lax.dynamic_slice_in_dim(mirror, lower_edge, share_width, 3)
    returned = []
    for offset in (1, 2):
        returned.append(from_behind(back_part[:, offset - 1], "ka", offset))
    return jnp.concatenate([own_part, returned[0][:, None], returned[1][:, None]], axis=1)


def solution(mesh):
    in_specs = (
        P("ka", None, None, None),
        P(None, None, "ga"),
        P(None, None, ("ga", "ka"), None),
        P("ka", None, None),
    )
    out_specs = P("ka", None, None, "ga")
    return jax.shard_map(body, mesh=mesh, in_specs=in_specs, out_specs=out_specs, check_vma=False)
```

profile of v0, /device:TPU:40, one launch (start us, length us, event | category | flops | bytes accessed | tf_op | source)
XLA Modules:
  0.0 973.5 jit_solution(12113033588784206750)
XLA Ops:
  13.7 4.0 collective-permute-done
  17.8 6.8 add_convert_fusion.1
  37.2 3.5 fusion.23
  57.1 34.7 %all-gather.5.cloned.1.call-done = bf16[72,16,2,1024]{3,1,0,2:T(8,128)(2,1)} async-done(((bf16[72,16,2,256]{3,1,0,2:T(8,128)(2,1)}), bf16[72,16,2,1024]{3,1,0,2:T(8,128)(2,1)}) %all-gather.5.cloned.1.call-update) | async-done | bytes 4718608 | tf_op jit(solution)/shard_map/all_gather | solution.py:110
  91.8 9.5 copy.25
  101.3 8.1 reshape.204
  109.4 487.1 %all-gather.3.cloned.1.call-done = bf16[22,2,256,1024]{3,1,0,2:T(2,128)(2,1)} async-done(((bf16[22,2,4,1024]{3,1,0,2:T(2,128)(2,1)}), bf16[22,2,256,1024]{3,1,0,2:T(2,128)(2,1)}) %all-gather.3.cloned.1.call-update) | async-done | bytes 23068688 | tf_op jit(solution)/shard_map/all_gather | solution.py:112
  596.5 24.2 %copy.26 = bf16[22,2,256,1024]{3,2,1,0:T(8,128)(2,1)} copy(bf16[22,2,256,1024]{3,1,0,2:T(2,128)(2,1)} %all-gather.3.cloned.1.call-done) | data formatting | bytes 46137344 | tf_op jit(solution)/shard_map/while | solution.py:71
  620.7 188.0 %while.10 = (s32[]{:T(128)}, f32[9,8,2,256,32]{3,1,0,4,2:T(8,128)}, s32[9]{0:T(128)S(1)}, s32[72]{0:T(128)S(1)}, bf16[22,2,256,1024]{3,2,1,0:T(8,128)(2,1)}, /*i...) while((s32[]{:T(128)}, f32[9,8,2,256,32]{3,1,0,4,2:T(8,128)}, ...), condition=%wide.region_1.2_spmd, body=%wide.region_0.1_spmd.sunk | while | flops 272630848 | bytes 27267396 | solution.py:71
  622.0 12.3 %gather_fusion = bf16[8,2,256,1024]{3,2,1,0:T(8,128)(2,1)} fusion(bf16[22,2,256,1024]{3,2,1,0:T(8,128)(2,1)} %get-tuple-element.163, s32[1024]{0:T(1024)S(1)} %pad_clamp_fusion.2), kind=kCustom, calls=%fused_computation.clone.1 | custom fusion | bytes 16777248 | tf_op jit(solution)/shard_map/while/body/eval_jaxpr/jit(_take)/gather | solution.py:115
  634.4 6.1 fusion.66
  642.9 12.3 %gather_fusion = bf16[8,2,256,1024]{3,2,1,0:T(8,128)(2,1)} fusion(bf16[22,2,256,1024]{3,2,1,0:T(8,128)(2,1)} %get-tuple-element.163, s32[1024]{0:T(1024)S(1)} %pad_clamp_fusion.2), kind=kCustom, calls=%fused_computation.clone.1 | custom fusion | bytes 16777248 | tf_op jit(solution)/shard_map/while/body/eval_jaxpr/jit(_take)/gather | solution.py:115
  655.3 6.1 fusion.66
  663.8 12.3 %gather_fusion = bf16[8,2,256,1024]{3,2,1,0:T(8,128)(2,1)} fusion(bf16[22,2,256,1024]{3,2,1,0:T(8,128)(2,1)} %get-tuple-element.163, s32[1024]{0:T(1024)S(1)} %pad_clamp_fusion.2), kind=kCustom, calls=%fused_computation.clone.1 | custom fusion | bytes 16777248 | tf_op jit(solution)/shard_map/while/body/eval_jaxpr/jit(_take)/gather | solution.py:115
  676.2 6.1 fusion.66
  684.8 12.3 %gather_fusion = bf16[8,2,256,1024]{3,2,1,0:T(8,128)(2,1)} fusion(bf16[22,2,256,1024]{3,2,1,0:T(8,128)(2,1)} %get-tuple-element.163, s32[1024]{0:T(1024)S(1)} %pad_clamp_fusion.2), kind=kCustom, calls=%fused_computation.clone.1 | custom fusion | bytes 16777248 | tf_op jit(solution)/shard_map/while/body/eval_jaxpr/jit(_take)/gather | solution.py:115
  697.1 6.1 fusion.66
  705.6 12.3 %gather_fusion = bf16[8,2,256,1024]{3,2,1,0:T(8,128)(2,1)} fusion(bf16[22,2,256,1024]{3,2,1,0:T(8,128)(2,1)} %get-tuple-element.163, s32[1024]{0:T(1024)S(1)} %pad_clamp_fusion.2), kind=kCustom, calls=%fused_computation.clone.1 | custom fusion | bytes 16777248 | tf_op jit(solution)/shard_map/while/body/eval_jaxpr/jit(_take)/gather | solution.py:115
  717.9 6.1 fusion.66
  726.5 12.3 %gather_fusion = bf16[8,2,256,1024]{3,2,1,0:T(8,128)(2,1)} fusion(bf16[22,2,256,1024]{3,2,1,0:T(8,128)(2,1)} %get-tuple-element.163, s32[1024]{0:T(1024)S(1)} %pad_clamp_fusion.2), kind=kCustom, calls=%fused_computation.clone.1 | custom fusion | bytes 16777248 | tf_op jit(solution)/shard_map/while/body/eval_jaxpr/jit(_take)/gather | solution.py:115
  738.8 6.1 fusion.66
  747.4 12.3 %gather_fusion = bf16[8,2,256,1024]{3,2,1,0:T(8,128)(2,1)} fusion(bf16[22,2,256,1024]{3,2,1,0:T(8,128)(2,1)} %get-tuple-element.163, s32[1024]{0:T(1024)S(1)} %pad_clamp_fusion.2), kind=kCustom, calls=%fused_computation.clone.1 | custom fusion | bytes 16777248 | tf_op jit(solution)/shard_map/while/body/eval_jaxpr/jit(_take)/gather | solution.py:115
  759.7 6.1 fusion.66
  768.3 12.3 %gather_fusion = bf16[8,2,256,1024]{3,2,1,0:T(8,128)(2,1)} fusion(bf16[22,2,256,1024]{3,2,1,0:T(8,128)(2,1)} %get-tuple-element.163, s32[1024]{0:T(1024)S(1)} %pad_clamp_fusion.2), kind=kCustom, calls=%fused_computation.clone.1 | custom fusion | bytes 16777248 | tf_op jit(solution)/shard_map/while/body/eval_jaxpr/jit(_take)/gather | solution.py:115
  780.6 6.1 fusion.66
  789.2 12.3 %gather_fusion = bf16[8,2,256,1024]{3,2,1,0:T(8,128)(2,1)} fusion(bf16[22,2,256,1024]{3,2,1,0:T(8,128)(2,1)} %get-tuple-element.163, s32[1024]{0:T(1024)S(1)} %pad_clamp_fusion.2), kind=kCustom, calls=%fused_computation.clone.1 | custom fusion | bytes 16777248 | tf_op jit(solution)/shard_map/while/body/eval_jaxpr/jit(_take)/gather | solution.py:115
  801.5 6.1 fusion.66
  818.2 98.4 %all-reduce.2.cloned.1.call-done = f32[2,6,6,2,4,4,4,4]{2,1,0,7,6,5,4,3:T(8,128)} async-done(((f32[2,6,6,2,4,4,4,4]{2,1,0,7,6,5,4,3:T(8,128)}), f32[2,6,6,2,4,4,4,4]{2,1,0,7,6,5,4,3:T(8,128)}) %all-reduce.2.cloned.1.call-update) | async-done | bytes 147472 | tf_op jit(solution)/shard_map/psum | solution.py:121
  916.6 14.6 %copy.34 = f32[6,2,2,6,4,4,4,4]{7,6,5,4,3,2,1,0:T(4,128)} copy(f32[6,2,2,6,4,4,4,4]{3,0,1,6,4,7,5,2:T(8,128)} %bitcast.102) | data formatting | bytes 294912 | tf_op jit(solution)/shard_map/transpose | solution.py:55
  931.1 7.1 reshape.206
  938.2 14.6 %copy.39 = f32[6,2,2,6,4,4,4,4]{7,6,5,4,3,2,0,1:T(4,128)} copy(f32[6,2,2,6,4,4,4,4]{0,3,1,4,6,5,7,2:T(8,128)} %bitcast.103) | data formatting | bytes 294912 | tf_op jit(solution)/shard_map/reshape | solution.py:56
  952.8 7.1 reshape.230
  (101 shorter events, 69.3 us)
Async XLA Ops:
  6.5 85.3 %all-gather.5.cloned.1.call-start = ((), (), s32[]{:S(2)}) async-start(), calls=%async_computation.1 | async-start | bytes 5898240 | tf_op jit(solution)/shard_map/all_gather | solution.py:110
  6.5 7.0 collective-permute-start.1
  6.6 11.0 %collective-permute-start = (bf16[6,2,8,1024]{3,2,1,0:T(8,128)(2,1)}, bf16[6,2,8,1024]{3,2,1,0:T(8,128)(2,1)S(1)}, u32[]{:S(2)}, u32[]{:S(2)}) collective-permute-start(bf16[6,2,8,1024]{3,2,1,0:T(8,128)(2,1)} %param.7), channel_id=1, source_target_pairs={{0,252},{4,0},{8,4},{12,8},{16,12},{20,16},{24,20},{28,24},{32,28}... | collective-permute-start | bytes 589832 | tf_op jit(solution)/shard_map/ppermute | solution.py:16
  37.2 3.5 copy-start.1
  37.2 3.5 copy-start.3
  37.2 3.5 copy-start.4
  42.6 3.5 copy-start.6
  43.7 552.8 %all-gather.3.cloned.1.call-start = ((), (), s32[]{:S(2)}) async-start(), calls=%async_computation | async-start | bytes 23429120 | tf_op jit(solution)/shard_map/all_gather | solution.py:112
  45.8 870.8 %all-reduce.2.cloned.1.call-start = ((), (), s32[]{:S(2)}) async-start(), calls=%async_computation.2 | async-start | bytes 8388608 | tf_op jit(solution)/shard_map/psum | solution.py:121
  50.5 1.7 copy-start.2
  52.2 3.1 copy-start
  52.2 3.1 copy-start.5
  952.8 7.1 copy-start.7
  960.0 4.1 collective-permute-start.2
  962.6 3.8 collective-permute-start.3
Sparse Core Ops, SparseCore 0:
  43.8 47.9 all-gather.4
  93.6 502.8 all-gather.2
  818.3 98.2 all-reduce.1
where the time goes:
time: 979 us; the launch traced here: 974 us
  waiting for transfers between devices  628 us (64%)
  local copies, waits for them, and re-layouts  241 us (25%)
  matrix products  65.5 us (7%)
  other arithmetic  13.4 us (1%)
  between operations  13.3 us (1%)
    all_gather x1, waiting for transfers between devices, body(): row_piece = lax.all_gather(screened, 'ka', axis=2, tiled=True)  487 us
    gather x9, local copies, waits for them, and re-layouts, compute(): chosen = jnp.take(row_piece, slots, axis=0)  111 us
    psum x1, waiting for transfers between devices, body(): summed = lax.psum(direct, 'ga')  98.4 us
    dot_general x9, matrix products, compute(): jnp.einsum('prgh,pch->prgc', chosen, groups[0], preferred_element_type=jn...  54.8 us
    all_gather x1, waiting for transfers between devices, body(): valence = lax.all_gather(valence_local, 'ga', axis=3, tiled=True)  34.7 us
    while x1, local copies, waits for them, and re-layouts, by_groups(): results = lax.map(one_group, jnp.arange(count, dtype=jnp.int32))  24.2 us
    reshape x2, local copies, waits for them, and re-layouts, arranged(): jnp.transpose(shaped, (2, 0, 3, 1, 7, 5, 6, 4))  21.7 us
  transfers between devices with their start and end apart: 7, of which 6 were waited for; matrix products, arithmetic and copies ran while one was open for 3% of the time, Pallas kernels for 0%

commit v1 on v0

v1 whole, which is shorter than its diff:
```python
import functools
import jax
import jax.numpy as jnp
from jax import lax
from jax.experimental import pallas as pl
from jax.experimental.pallas import tpu as pltpu
from jax.sharding import PartitionSpec as P

f32 = jnp.float32
bf16 = jnp.bfloat16

WIN = 8
KB = 6
PAIRS = 72
TOTAL = WIN * PAIRS
CHUNK = 16
SLOTS = 22
CHUNKS = (TOTAL + SLOTS * (CHUNK - 1)) // CHUNK // 2 * 2 + 2
MSG = 112
VMEM_LIMIT = 50 * 1024 * 1024


def from_behind(x, axis, by):
    count = lax.axis_size(axis)
    return lax.ppermute(x, axis, [(i, (i + by) % count) for i in range(count)])


def half_swap(mask, first, second):
    return jnp.where(mask, first, pltpu.roll(second, 4, 0))


def density_kernel(near_ref, far_ref, zv_ref, zc_ref, *rest):
    mv_ref, mc_ref, left, right, va, ca, vb, cb = rest[-8:]
    step = pl.program_id(0)
    low = lax.broadcasted_iota(jnp.int32, (8, 1024), 0) < 4

    def produce(chunk, v_buf, c_buf):
        block = chunk // 3
        jh = chunk % 3
        for cv, buf in ((0, v_buf), (1, c_buf)):
            for jl in range(2):
                point = block * KB + 2 * jh + jl
                for part in range(4):
                    cols = slice(256 * part, 256 * part + 256)
                    imag_cols = slice(1024 + 256 * part, 1280 + 256 * part)
                    lefts = []
                    for band in range(4):
                        row = 4 * cv + band
                        lr = jnp.broadcast_to(left[point, row : row + 1, cols], (8, 256))
                        li = jnp.broadcast_to(left[point, 8 + row : 9 + row, cols], (8, 256))
                        lefts.append((lr, li))
                    for o in range(2):
                        for p in range(3):
                            rr = right[(block + o) * 3 + p, cv, 0, :, cols]
                            ri = right[(block + o) * 3 + p, cv, 1, :, cols]
                            base = ((jl * 2 + o) * 3 + p) * 32
                            for half in range(2):
                                reals = []
                                imags = []
                                for lr, li in lefts[2 * half : 2 * half + 2]:
                                    reals.append(lr * rr + li * ri)
                                    imags.append(lr * ri - li * rr)
                                rows = slice(base + 16 * half, base + 16 * half + 16)
                                buf[rows, cols] = jnp.concatenate(reals, axis=0).astype(bf16)
                                buf[rows, imag_cols] = jnp.concatenate(imags, axis=0).astype(bf16)
                    yield

    def consume(sub, v_buf, c_buf):
        mask = lax.broadcasted_iota(jnp.int32, (8, 256), 0) < 4
        for buf, z_ref, out_ref in ((v_buf, zv_ref, mv_ref), (c_buf, zc_ref, mc_ref)):
            for tile in range(z_ref.shape[1] // 256):
                cols = slice(256 * tile, 256 * tile + 256)
                for jl in range(2):
                    res = jnp.dot(buf[192 * jl : 192 * jl + 192], z_ref[:, cols], preferred_element_type=f32)
                    for o in range(2):
                        for p in range(3):
                            base = (o * 3 + p) * 32
                            a = [res[base + 8 * c : base + 8 * c + 8] for c in range(4)]
                            first = [half_swap(mask, a[0], a[1]), half_swap(mask, a[2], a[3])]
                            second = [
                                jnp.where(mask, pltpu.roll(a[0], 4, 0), a[1]),
                                jnp.where(mask, pltpu.roll(a[2], 4, 0), a[3]),
                            ]
                            for jj, value in ((0, first), (1, second)):
                                index = sub * 24 + (2 * p + jj) * 4 + jl * 2 + o
                                out_ref[index, :, cols] = jnp.concatenate(value, axis=0).astype(bf16)
                    yield

    def drain(*generators):
        live = list(generators)
        while live:
            live = [g for g in live if next(g, True) is None]

    @pl.when(step == 0)
    def _():
        for b in range(4):
            ref = near_ref if b < 2 else far_ref
            for j in range(KB):
                x = ref[b % 2, 16 * j : 16 * j + 16, :].astype(f32)
                if b < 2:
                    left[b * KB + j] = x
                if b > 0:
                    p = j // 2
                    for r in range(2):
                        half = x[8 * r : 8 * r + 8]
                        if j % 2 == 0:
                            right[(b - 1) * 3 + p, 0, r] = half
                            right[(b - 1) * 3 + p, 1, r] = pltpu.roll(half, 4, 0)
                        else:
                            index = (b - 1) * 3 + p
                            right[index, 0, r] = jnp.where(low, right[index, 0, r], pltpu.roll(half, 4, 0))
                            right[index, 1, r] = jnp.where(low, right[index, 1, r], half)
        drain(produce(0, va, ca))

    drain(consume(0, va, ca), produce(2 * step + 1, vb, cb))
    drain(consume(1, vb, cb), produce(jnp.minimum(2 * step + 2, 5), va, ca))


def densities(call, near, far, zv, zc, previous):
    whole = lambda shape: pl.BlockSpec(shape, lambda n: (0,) * len(shape), pipeline_mode=pl.Buffered(1))
    in_specs = [whole(near.shape), whole(far.shape), whole(zv.shape), whole(zc.shape)]
    operands = [near, far, zv, zc]
    aliases = {}
    if previous is not None:
        in_specs += [pl.BlockSpec(memory_space=pl.ANY)] * 2
        operands += list(previous)
        aliases = {4: 0, 5: 1}
    wv = zv.shape[1]
    wc = zc.shape[1]
    flops = 2 * 2 * PAIRS * 16 * 2048 * (wv + wc)
    return pl.pallas_call(
        density_kernel,
        grid=(3,),
        in_specs=in_specs,
        out_specs=[
            pl.BlockSpec((48, 16, wv), lambda n: (3 * call + n, 0, 0)),
            pl.BlockSpec((48, 16, wc), lambda n: (3 * call + n, 0, 0)),
        ],
        out_shape=[
            jax.ShapeDtypeStruct((TOTAL, 16, wv), bf16),
            jax.ShapeDtypeStruct((TOTAL, 16, wc), bf16),
        ],
        scratch_shapes=[
            pltpu.VMEM((2 * KB, 16, 1024), f32),
            pltpu.VMEM((9, 2, 2, 8, 1024), f32),
            pltpu.VMEM((384, 2048), bf16),
            pltpu.VMEM((384, 2048), bf16),
            pltpu.VMEM((384, 2048), bf16),
            pltpu.VMEM((384, 2048), bf16),
        ],
        input_output_aliases=aliases,
        compiler_params=pltpu.CompilerParams(vmem_limit_bytes=VMEM_LIMIT),
        cost_estimate=pl.CostEstimate(flops=flops, bytes_accessed=8 * 2**20, transcendentals=0),
        name="densities",
    )(*operands)


def quarter_rows():
    own = [[(0, 0, 0, 16)], [(0, 16, 0, 8), (1, 0, 8, 8)], [(1, 8, 0, 16)]]
    own += [[(q + 2, r, s, n) for q, r, s, n in item] for item in own]
    mirror = [[(0, 24)], [(0, 40), (1, 24)], [(1, 40)]]
    mirror += [[(q + 2, r) for q, r in item] for item in mirror]
    return own, mirror


def apply_kernel(order_ref, slot_ref, used_ref, ga_ref, mv_ref, mc_ref, w_ref, out_ref, rhs, xv):
    ga = ga_ref[0]
    lane_group = lax.broadcasted_iota(jnp.int32, (16, 128), 1) >> 5
    spots = [(((q & 1) ^ (ga & 1)) << 1) | ((q >> 1) ^ (ga >> 1)) for q in range(4)]
    own_rows, mirror_rows = quarter_rows()

    def build(slot, carry):
        for x in range(4):
            wr = w_ref[x, slot, 0]
            wi = w_ref[x, slot, 1]
            rhs[slot, 64 * x : 64 * x + 64, 0:128] = wr
            rhs[slot, 64 * x : 64 * x + 64, 128:256] = -wi
            rhs[slot, 256 + 64 * x : 320 + 64 * x, 0:128] = wi
            rhs[slot, 256 + 64 * x : 320 + 64 * x, 128:256] = wr
        return carry

    lax.fori_loop(0, SLOTS, build, 0)

    def chunk(q, carry):
        for u in range(2):
            slot = slot_ref[2 * q + u]
            ids = [order_ref[(2 * q + u) * CHUNK + i] for i in range(CHUNK)]
            sources = [jnp.minimum(i, TOTAL - 1) for i in ids]
            lhs = jnp.concatenate([mv_ref[s] for s in sources], axis=0)
            res = jnp.dot(lhs, rhs[slot], preferred_element_type=f32).astype(bf16)
            for i in range(CHUNK):
                xv[ids[i]] = res[16 * i : 16 * i + 16]
        return carry

    lax.fori_loop(0, (used_ref[0] + 1) >> 1, chunk, 0)

    def contract(t, carry):
        for jh in range(3):
            for h in range(3):
                first = ((t * 3 + jh) * 6 + 2 * h) * 4
                rows = []
                for i in range(8):
                    y = mc_ref[first + i]
                    rows.append(y)
                    rows.append(jnp.concatenate([-y[:, 128:], y[:, :128]], axis=1))
                lhs = jnp.concatenate([xv[first + i] for i in range(8)], axis=0)
                d = lax.dot_general(
                    lhs, jnp.concatenate(rows, axis=0), (((1,), (1,)), ((), ())), preferred_element_type=f32
                )
                blocks = [
                    [d[16 * i : 16 * i + 16, 128 * (i // 4) : 128 * (i // 4) + 128] for i in range(4 * l, 4 * l + 4)]
                    for l in range(2)
                ]
                odd = (lane_group & 1) == 1
                low = lane_group < 2
                mixed = [[jnp.where(odd, b[2 * jl + 1], b[2 * jl]) for jl in range(2)] for b in blocks]
                for l in range(2):
                    own = jnp.where(low, mixed[l][0], mixed[l][1])
                    for q, r, s, n in own_rows[2 * h + l]:
                        out_ref[spots[q], t, jh, r : r + n, :] = own[s : s + n]
                for jl in range(2):
                    if jl == 0:
                        mirror = jnp.where(low, mixed[0][0], pltpu.roll(mixed[1][0], 64, 1))
                    else:
                        mirror = jnp.where(low, pltpu.roll(mixed[0][1], 64, 1), mixed[1][1])
                    for q, r in mirror_rows[2 * jh + jl]:
                        out_ref[spots[q], t, h, r : r + 16, :] = mirror
        return carry

    lax.fori_loop(0, WIN, contract, 0)


def apply_screened(order, slots, used, ga, mv, mc, w):
    smem = pl.BlockSpec(memory_space=pltpu.SMEM)
    vmem = pl.BlockSpec(memory_space=pltpu.VMEM)
    return pl.pallas_call(
        apply_kernel,
        in_specs=[smem] * 4 + [vmem] * 3,
        out_specs=vmem,
        out_shape=jax.ShapeDtypeStruct((4, WIN, 3, 56, 128), f32),
        scratch_shapes=[
            pltpu.VMEM((SLOTS, 512, 256), bf16),
            pltpu.VMEM((TOTAL + 1, 16, 256), bf16),
        ],
        compiler_params=pltpu.CompilerParams(vmem_limit_bytes=VMEM_LIMIT),
        cost_estimate=pl.CostEstimate(flops=6 * 10**9, bytes_accessed=18 * 2**20, transcendentals=0),
        name="apply_screened",
    )(order, slots, used, ga, mv, mc, w)


def split_dot(x, sel):
    high = x.astype(bf16)
    low = (x - high.astype(f32)).astype(bf16)
    return jnp.dot(high, sel, preferred_element_type=f32) + jnp.dot(low, sel, preferred_element_type=f32)


def arrange_kernel(ga_ref, parts_ref, out_ref):
    ga = ga_ref[0]
    src = lax.broadcasted_iota(jnp.int32, (128, 384), 0)
    lane = lax.broadcasted_iota(jnp.int32, (128, 384), 1)
    row = lax.broadcasted_iota(jnp.int32, (32, 384), 0)
    row_lane = lax.broadcasted_iota(jnp.int32, (32, 384), 1)
    start = ga + (ga >> 1)
    outer = row_lane >> 6
    place = 6 * ga + outer
    own = (24, (lane >> 4) & 3, lane & 3, outer * 4 + ((row_lane >> 2) & 3))
    mirror = (32, lane & 3, (lane >> 4) & 3, ((place >> 2) - start) * 16 + ((row_lane >> 2) & 3) * 4 + (place & 3))
    for kind, (count, c, c2, wanted) in enumerate((own, mirror)):
        low = 24 * kind
        x = jnp.concatenate([parts_ref[jh, low : low + count, :] for jh in range(3)], axis=0)
        keep = row[:count] == wanted[:count]
        for combo in range(8):
            sel = (src == combo * 16 + c * 4 + c2).astype(f32).astype(bf16)
            spread = split_dot(x, sel)
            for jh in range(3):
                rows = spread[count * jh : count * jh + count]
                picked = jnp.sum(jnp.where(keep, rows, 0.0), axis=0, keepdims=True)
                if kind == 1 and combo % 2 == 1:
                    picked = -picked
                out_ref[2 * jh + combo // 4, 2 * kind + (combo // 2) % 2, pl.ds(combo % 2, 1), :] = picked


def arrange(ga, parts):
    vmem = pl.BlockSpec(memory_space=pltpu.VMEM)
    return pl.pallas_call(
        arrange_kernel,
        in_specs=[pl.BlockSpec(memory_space=pltpu.SMEM), vmem],
        out_specs=vmem,
        out_shape=jax.ShapeDtypeStruct((KB, 4, 2, 384), f32),
        compiler_params=pltpu.CompilerParams(vmem_limit_bytes=VMEM_LIMIT),
        name="arrange",
    )(ga, parts)


def schedule(slots):
    pair = jnp.arange(TOTAL, dtype=jnp.int32)
    names = jnp.arange(SLOTS, dtype=jnp.int32)
    hot = slots[:, None] == names[None, :]
    needed = (jnp.sum(hot.astype(jnp.int32), axis=0) + CHUNK - 1) // CHUNK
    start = jnp.sum(jnp.where(names[:, None] < names[None, :], needed[:, None], 0), axis=0)
    same = (slots[:, None] == slots[None, :]) & (pair[None, :] < pair[:, None])
    rank = jnp.sum(same.astype(jnp.int32), axis=1)
    place = jnp.sum(jnp.where(hot, start[None, :], 0), axis=1) * CHUNK + rank
    seat = jnp.arange(CHUNKS * CHUNK, dtype=jnp.int32)
    taken = place[None, :] == seat[:, None]
    order = TOTAL + jnp.sum(jnp.where(taken, pair[None, :] - TOTAL, 0), axis=1)
    chunk = jnp.arange(CHUNKS, dtype=jnp.int32)
    ended = (start + needed)[None, :] <= chunk[:, None]
    slot_of = jnp.minimum(jnp.sum(ended.astype(jnp.int32), axis=1), SLOTS - 1)
    return order, slot_of, jnp.sum(needed).reshape(1)


def zeta_matrix(zeta):
    zr = zeta[:, 0]
    zi = zeta[:, 1]
    return jnp.concatenate([jnp.concatenate([zr, zi], axis=1), jnp.concatenate([-zi, zr], axis=1)], axis=0)


def body(bloch_samples, zeta_vectors, screened, pair_slots):
    ka_count = lax.axis_size("ka")
    ka = lax.axis_index("ka")
    ga = lax.axis_index("ga")
    ga_word = ga.reshape(1).astype(jnp.int32)
    part = lax.rem(ka, WIN)
    slots = jnp.transpose(pair_slots.reshape(3, 2, 2, KB), (0, 3, 1, 2)).reshape(1, PAIRS)
    tail = jnp.pad(slots.astype(bf16), ((0, 15), (0, 1024 - PAIRS)))
    message = jnp.concatenate([bloch_samples.reshape(96, 1024), tail], axis=0)
    following = from_behind(message, "ka", -1)
    pieces = jnp.transpose(screened.reshape(SLOTS, 2, 4, WIN, 128), (3, 0, 1, 2, 4))
    pieces = jnp.concatenate([pieces, pieces], axis=0)
    line = 2 * WIN
    near_groups = [[x * line + s for s in range(line)] for x in range(ka_count // line)]
    x_groups = [[x * line + s for x in range(ka_count // line)] for s in range(line)]
    pieces = lax.all_to_all(pieces, "ka", 0, 0, axis_index_groups=near_groups, tiled=True)
    rows = jnp.transpose(pieces, (1, 2, 0, 3, 4)).reshape(SLOTS, 2, 4 * line, 128)
    w = lax.all_gather(rows, "ka", axis_index_groups=x_groups)
    zv = zeta_matrix(zeta_vectors)
    mine = lax.dynamic_slice_in_dim(zeta_vectors, 128 * lax.rem(part, 2), 128, 2)
    mine, following = lax.optimization_barrier((mine, following))
    holders = [(k, (k % WIN) // 2) for k in range(ka_count)]
    over = lax.ppermute(mine, ("ka", "ga"), [(4 * k + h, 4 * k + (h ^ 2)) for k, h in holders])
    held = jnp.where(ga == part // 2, mine, over)
    moves = [(4 * k + h, 4 * k + (h ^ 1)) for k, h in holders]
    moves += [(4 * k + (h ^ 2), 4 * k + (h ^ 3)) for k, h in holders]
    zc = zeta_matrix(held + lax.ppermute(held, ("ka", "ga"), moves))
    here = jnp.stack([message, following])
    ahead = from_behind(here, "ka", -2)
    behind = from_behind(here, "ka", 2)
    ahead2 = from_behind(ahead, "ka", -2)
    behind2 = from_behind(behind, "ka", 2)
    pairs = [behind2, behind, here, ahead, ahead2]
    made = None
    for call in (2, 1, 3, 0):
        made = densities(call, pairs[call], pairs[call + 1], zv, zc, made)
    mv, mc = made
    all_slots = jnp.concatenate([x[:, 96, :PAIRS] for x in pairs[:4]], axis=0).reshape(TOTAL)
    order, slot_of, used = schedule(all_slots.astype(jnp.int32))
    partial = apply_screened(order, slot_of, used, ga_word, mv, mc, w)
    arrived = lax.ppermute(partial[2:].astype(bf16), "ga", [(0, 1), (1, 0), (2, 3), (3, 2)])
    own = partial[0] + arrived[0].astype(f32)
    other = (partial[1] + arrived[1].astype(f32)).astype(bf16)
    own = own + lax.ppermute(other, "ga", [(0, 2), (2, 0), (1, 3), (3, 1)]).astype(f32)
    first_offset = ((lax.broadcasted_iota(jnp.int32, (1, 1, 1, 128), 3) >> 5) & 1) == 0
    spread = lambda x, before, after: jnp.pad(x, ((before, after), (0, 0), (0, 0), (0, 0)))
    mirror = jnp.where(first_offset, spread(own[:, :, 24:], 1, 1), spread(own[:, :, 24:], 2, 0))
    parts = jnp.concatenate([spread(own[:, :, :24], 0, 2), mirror], axis=2)
    send = lambda picks, by: from_behind(jnp.stack([parts[d] for d in picks]).astype(bf16), "ka", by).astype(f32)
    plus_one = send((1, 5, 9), 1)
    plus_two = send((2, 6), 2)
    minus_one = send((3, 7), -1)
    low = parts[0] + plus_one[0] + plus_two[0]
    high = parts[8] + plus_one[2] + minus_one[1]
    total = parts[4] + plus_one[1] + plus_two[1] + minus_one[0]
    total = total + from_behind(low, "ka", -4) + from_behind(high, "ka", 4)
    return arrange(ga_word, total)


def solution(mesh):
    in_specs = (
        P("ka", None, None, None),
        P(None, None, "ga"),
        P(None, None, ("ga", "ka"), None),
        P("ka", None, None),
    )
    out_specs = P("ka", None, None, "ga")
    return jax.shard_map(body, mesh=mesh, in_specs=in_specs, out_specs=out_specs, check_vma=False)
```

time: 979 us -> 181 us (0.18)
  waiting for transfers between devices: 628 us -> 53.7 us
  local copies, waits for them, and re-layouts: 241 us -> 8.7 us
  matrix products: 65.5 us -> 0 us
  Pallas kernels: 0 us -> 64.6 us
  starting transfers between devices: 6.62 us -> 31.3 us
    all_gather x2 -> x1, waiting for transfers between devices: 522 us -> 0.01 us  [body(): w = lax.all_gather(rows, 'ka', axis_index_groups=x_groups)]
    gather x9 -> x0, local copies, waits for them, and re-layouts: 111 us -> none  [compute(): chosen = jnp.take(row_piece, slots, axis=0)]
    psum x1 -> x0, waiting for transfers between devices: 98.4 us -> none  [body(): summed = lax.psum(direct, 'ga')]
    dot_general x14 -> x0, matrix products: 65.5 us -> none  [the longest x9 54.8 us: compute(): jnp.einsum('prgh,pch->prgc', chosen, groups[0], preferred_element_type=jn...]
    pallas_call x0 -> x6, Pallas kernels: none -> 64.6 us  [the longest x4 43.4 us: densities(): pl.pallas_call(density_kernel, grid=(3,), in_specs=in_specs, out_specs=[p...]
    reshape x6 -> x1, local copies, waits for them, and re-layouts: 39.9 us -> 1.12 us  [body(): screened.reshape(SLOTS, 2, 4, WIN, 128)]
    ppermute x4 -> x10, waiting for transfers between devices: 7.35 us -> 42.2 us  [from_behind(): return lax.ppermute(x, axis, [(i, (i + by) % count) for i in range(count)])]
    while x1 -> x0, local copies, waits for them, and re-layouts: 24.2 us -> none  [by_groups(): results = lax.map(one_group, jnp.arange(count, dtype=jnp.int32))]
  transfers between devices with their start and end apart: 7 -> 16, of which waited for: 6 -> 8; matrix products, arithmetic and copies ran while one was open for 3% -> 8% of each run, Pallas kernels for 0% -> 24%
where the time goes in v1:
time: 181 us; the launch traced here: 180 us
  Pallas kernels  64.6 us (36%)
  waiting for transfers between devices  53.7 us (30%)
  starting transfers between devices  31.3 us (17%)
  between operations  13.8 us (8%)
  local copies, waits for them, and re-layouts  8.7 us (5%)
  other arithmetic  8.26 us (5%)
    pallas_call x4, Pallas kernels, densities(): pl.pallas_call(density_kernel, grid=(3,), in_specs=in_specs, out_specs=[p...  43.4 us
    ppermute x10, waiting for transfers between devices, from_behind(): return lax.ppermute(x, axis, [(i, (i + by) % count) for i in range(count)])  42.2 us
    pallas_call x1, Pallas kernels, apply_screened(): pl.pallas_call(apply_kernel, in_specs=[smem] * 4 + [vmem] * 3, out_specs=...  19.6 us
    ppermute x10, starting transfers between devices, from_behind(): return lax.ppermute(x, axis, [(i, (i + by) % count) for i in range(count)])  13.4 us
    all_to_all x1, starting transfers between devices, body(): lax.all_to_all(pieces, 'ka', 0, 0, axis_index_groups=near_groups, tiled=T...  12.6 us
    ppermute x1, waiting for transfers between devices, body(): lax.ppermute(other, 'ga', [(0, 2), (2, 0), (1, 3), (3, 1)]).astype(f32)  9.32 us
  transfers between devices with their start and end apart: 16, of which 8 were waited for; matrix products, arithmetic and copies ran while one was open for 8% of the time, Pallas kernels for 24%

profile of v1, /device:TPU:40, one launch (start us, length us, event | category | flops | bytes accessed | tf_op | source)
XLA Modules:
  0.0 180.4 jit_solution(15437321594404868169)
XLA Ops:
  7.5 1.0 fusion.14
  9.0 1.1 reshape.116
  10.3 1.2 copy.67
  11.4 12.6 %all-to-all-start = ((bf16[16,22,2,4,128]{4,3,2,1,0:T(4,128)(2,1)}), bf16[16,22,2,4,128]{4,3,2,1,0:T(4,128)(2,1)}, u32[]{:S(2)}, u32[]{:S(2)}) async-start(bf16[16,22,2,4,128]{4,3,2,1,0:T(4,128)(2,1)} %copy.67), calls=%async_computation | async-start | bytes 1441792 | tf_op jit(solution)/shard_map/all_to_all | solution.py:334
  24.5 0.9 copy.73
  25.4 1.6 collective-permute-start.1
  27.0 1.5 fusion.18
  29.1 1.4 collective-permute-start.4
  30.7 19.5 %collective-permute-done.1.near_ref.far_ref = bf16[2,112,1024]{2,1,0:T(8,128)(2,1)S(1)} collective-permute-done((bf16[2,112,1024]{2,1,0:T(8,128)(2,1)S(1)}, bf16[2,112,1024]{2,1,0:T(8,128)(2,1)S(1)}, u32[]{:S(2)}, u32[]{:S(2)}) %collective-permute-start.1) | collective-permute-done | bytes 458784 | tf_op jit(solution)/shard_map/ppermute | solution.py:25
  50.2 1.5 collective-permute-start.2
  52.7 1.6 collective-permute-start.6
  54.3 1.9 %broadcast_select_fusion = bf16[1024,2,128]{2,0,1:T(8,128)(2,1)} fusion(bf16[1024,2,128]{2,0,1:T(8,128)(2,1)} %copy.73, bf16[1024,2,128]{2,0,1:T(8,128)(2,1)} %collective-permute-done.4, pred[]{:T(512)S(6)} %eq.62), kind=kLoop, calls=%fused_computation.18 | loop fusion | flops 262144 | bytes 1572865 | tf_op jit(solution)/shard_map/jit(_where)/select_n | solution.py:342
  56.1 1.3 collective-permute-start.5
  57.4 5.7 %collective-permute-done.2.near_ref = bf16[2,112,1024]{2,1,0:T(8,128)(2,1)} collective-permute-done((bf16[2,112,1024]{2,1,0:T(8,128)(2,1)S(1)}, bf16[2,112,1024]{2,1,0:T(8,128)(2,1)}, u32[]{:S(2)}, u32[]{:S(2)}) %collective-permute-start.2) | collective-permute-done | bytes 458784 | tf_op jit(solution)/shard_map/ppermute | solution.py:25
  65.1 2.4 %copy.68 = bf16[22,2,16,4,128]{4,3,2,1,0:T(4,128)(2,1)} copy(bf16[22,2,16,4,128]{4,3,1,0,2:T(4,128)(2,1)} %bitcast.12) | data formatting | bytes 1441792 | tf_op jit(solution)/shard_map/transpose | solution.py:335
  67.9 1.3 add.126
  69.5 10.5 %densities.4 = (bf16[576,16,512]{2,1,0:T(8,128)(2,1)}, bf16[576,16,256]{2,1,0:T(8,128)(2,1)}) custom-call(bf16[2,112,1024]{2,1,0:T(8,128)(2,1)S(1)} %pad_maximum_fusion.1.near_ref.far_ref, bf16[2,112,1024]{2,1,0:T(8,128)(2,1)S(1)} %collective-permute-done.3.far_ref.near_ref, bf16[2048,512]{1,0:T(8,128)(2,1)S(1)} %maximum_maximum_fusion.zv_ref, ...), custom_call_target="tpu_custom_call" | custom-call | flops 7247757312 | bytes 8388608 | tf_op jit(solution)/shard_map/densities/pallas_call | solution.py:131
  80.0 10.2 %densities.5 = (bf16[576,16,512]{2,1,0:T(8,128)(2,1)}, bf16[576,16,256]{2,1,0:T(8,128)(2,1)}) custom-call(bf16[2,112,1024]{2,1,0:T(8,128)(2,1)S(1)} %collective-permute-done.1.near_ref.far_ref, bf16[2,112,1024]{2,1,0:T(8,128)(2,1)S(1)} %pad_maximum_fusion.1.near_ref.far_ref, ...), custom_call_target="tpu_custom_call", output_to_operand_aliasing={{0}: (4, {}), {1}: (5, {})} | custom-call | flops 7247757312 | bytes 8388608 | tf_op jit(solution)/shard_map/densities/pallas_call | solution.py:131
  90.2 11.4 %densities.6 = (bf16[576,16,512]{2,1,0:T(8,128)(2,1)}, bf16[576,16,256]{2,1,0:T(8,128)(2,1)}) custom-call(bf16[2,112,1024]{2,1,0:T(8,128)(2,1)S(1)} %collective-permute-done.3.far_ref.near_ref, bf16[2,112,1024]{2,1,0:T(8,128)(2,1)} %collective-permute-done.6.far_ref, ...), custom_call_target="tpu_custom_call", output_to_operand_aliasing={{0}: (4, {}), {1}: (5, {})} | custom-call | flops 7247757312 | bytes 8388608 | tf_op jit(solution)/shard_map/densities/pallas_call | solution.py:131
  101.6 11.3 %densities.7 = (bf16[576,16,512]{2,1,0:T(8,128)(2,1)}, bf16[576,16,256]{2,1,0:T(8,128)(2,1)}) custom-call(bf16[2,112,1024]{2,1,0:T(8,128)(2,1)} %collective-permute-done.2.near_ref, bf16[2,112,1024]{2,1,0:T(8,128)(2,1)S(1)} %collective-permute-done.1.near_ref.far_ref, ...), custom_call_target="tpu_custom_call", output_to_operand_aliasing={{0}: (4, {}), {1}: (5, {})} | custom-call | flops 7247757312 | bytes 8388608 | tf_op jit(solution)/shard_map/densities/pallas_call | solution.py:131
  112.8 19.6 %apply_screened.1 = f32[4,8,3,56,128]{4,3,2,1,0:T(8,128)S(1)} custom-call(s32[928]{0:T(1024)S(1)} %broadcast_add_fusion.order_ref, s32[58]{0:T(128)S(1)} %broadcast_minimum_fusion.slot_ref, s32[1]{0:T(128)} %bitcast.6.used_ref, s32[1]{0:T(128)} %bitcast.ga_ref, bf16[576,16,512]{2,1,0:T(8,128)(2,1)} %get-tuple-element.23.mv_ref, ...), custom_call_target="tpu_custom_call" | custom-call | flops 6000000000 | bytes 18874368 | tf_op jit(solution)/shard_map/apply_screened/pallas_call | solution.py:236
  132.7 2.1 %collective-permute-done.7 = bf16[2,8,3,56,128]{4,3,2,1,0:T(8,128)(2,1)S(1)} collective-permute-done((bf16[2,8,3,56,128]{4,3,2,1,0:T(8,128)(2,1)S(1)}, bf16[2,8,3,56,128]{4,3,2,1,0:T(8,128)(2,1)S(1)}, u32[]{:S(2)}, u32[]{:S(2)}) %collective-permute-start.7) | collective-permute-done | bytes 688160 | tf_op jit(solution)/shard_map/ppermute | solution.py:359
  134.9 2.4 %collective-permute-start.8 = (bf16[8,3,56,128]{3,2,1,0:T(8,128)(2,1)S(1)}, bf16[8,3,56,128]{3,2,1,0:T(8,128)(2,1)S(1)}, u32[]{:S(2)}, u32[]{:S(2)}) collective-permute-start(bf16[8,3,56,128]{3,2,1,0:T(8,128)(2,1)S(1)} %fusion.5), channel_id=1, source_target_pairs={{0,2},{2,0},{1,3},{3,1},{4,6},{6,4},{5,7},{7,5},{8,10},{10,8},{9,1... | collective-permute-start | bytes 1032200 | tf_op jit(solution)/shard_map/ppermute | solution.py:362
  137.3 9.3 %collective-permute-done.8 = bf16[8,3,56,128]{3,2,1,0:T(8,128)(2,1)S(1)} collective-permute-done((bf16[8,3,56,128]{3,2,1,0:T(8,128)(2,1)S(1)}, bf16[8,3,56,128]{3,2,1,0:T(8,128)(2,1)S(1)}, u32[]{:S(2)}, u32[]{:S(2)}) %collective-permute-start.8) | collective-permute-done | bytes 344096 | tf_op jit(solution)/shard_map/ppermute | solution.py:362
  146.9 0.9 collective-permute-start.11
  147.9 2.1 %collective-permute-start.9 = (bf16[3,3,56,128]{3,2,1,0:T(8,128)(2,1)S(1)}, bf16[3,3,56,128]{3,2,1,0:T(8,128)(2,1)S(1)}, u32[]{:S(2)}, u32[]{:S(2)}) collective-permute-start(bf16[3,3,56,128]{3,2,1,0:T(8,128)(2,1)S(1)} %pad_maximum_fusion.2), channel_id=1, source_target_pairs={{0,4},{4,8},{8,12},{12,16},{16,20},{20,24},{24,28},{28,32},{32,36}... | collective-permute-start | bytes 387080 | tf_op jit(solution)/shard_map/ppermute | solution.py:25
  150.0 1.5 collective-permute-start.10
  152.4 6.8 %collective-permute-done.10 = bf16[2,3,56,128]{3,2,1,0:T(8,128)(2,1)S(1)} collective-permute-done((bf16[2,3,56,128]{3,2,1,0:T(8,128)(2,1)S(1)}, bf16[2,3,56,128]{3,2,1,0:T(8,128)(2,1)S(1)}, u32[]{:S(2)}, u32[]{:S(2)}) %collective-permute-start.10) | collective-permute-done | bytes 86048 | tf_op jit(solution)/shard_map/ppermute | solution.py:25
  159.3 2.8 %collective-permute-start.12 = (f32[3,56,128]{2,1,0:T(8,128)S(1)}, f32[3,56,128]{2,1,0:T(8,128)S(1)}, u32[]{:S(2)}, u32[]{:S(2)}) collective-permute-start(f32[3,56,128]{2,1,0:T(8,128)S(1)} %get-tuple-element.29), channel_id=1, source_target_pairs={{0,240},{4,244},{8,248},{12,252},{16,0},{20,4},{24,8},{28,12},{32,... | collective-permute-start | bytes 258056 | tf_op jit(solution)/shard_map/ppermute | solution.py:25
  162.4 2.6 %collective-permute-done.12 = f32[3,56,128]{2,1,0:T(8,128)S(1)} collective-permute-done((f32[3,56,128]{2,1,0:T(8,128)S(1)}, f32[3,56,128]{2,1,0:T(8,128)S(1)}, u32[]{:S(2)}, u32[]{:S(2)}) %collective-permute-start.12) | collective-permute-done | bytes 86048 | tf_op jit(solution)/shard_map/ppermute | solution.py:25
  164.9 6.9 %collective-permute-done.13 = f32[3,56,128]{2,1,0:T(8,128)S(1)} collective-permute-done((f32[3,56,128]{2,1,0:T(8,128)S(1)}, f32[3,56,128]{2,1,0:T(8,128)S(1)}, u32[]{:S(2)}, u32[]{:S(2)}) %collective-permute-start.13) | collective-permute-done | bytes 86048 | tf_op jit(solution)/shard_map/ppermute | solution.py:25
  171.9 1.6 arrange.1
  (72 shorter events, 8.0 us)
Async XLA Ops:
  8.5 16.9 %copy-start.1 = (bf16[1,112,1024]{2,1,0:T(8,128)(2,1)}, bf16[1,112,1024]{2,1,0:T(8,128)(2,1)S(1)}, u32[]{:S(2)}) copy-start(bf16[1,112,1024]{2,1,0:T(8,128)(2,1)S(1)} %get-tuple-element.42) | copy-start | bytes 688132
  8.5 15.6 %copy-start = (bf16[1024,2,256]{2,1,0:T(2,128)(2,1)S(1)}, bf16[1024,2,256]{2,1,0:T(2,128)(2,1)}, u32[]{:S(2)}) copy-start(bf16[1024,2,256]{2,1,0:T(2,128)(2,1)} %param.5) | copy-start | bytes 3145732
  8.5 16.9 %collective-permute-start = (bf16[112,1024]{1,0:T(8,128)(2,1)S(1)}, bf16[112,1024]{1,0:T(8,128)(2,1)S(1)}, u32[]{:S(2)}, u32[]{:S(2)}) collective-permute-start(bf16[112,1024]{1,0:T(8,128)(2,1)S(1)} %get-tuple-element.43), channel_id=1, source_target_pairs={{0,252},{4,0},{8,4},{12,8},{16,12},{20,16},{24,20},{28,24},{32,28}... | collective-permute-start | bytes 688136 | tf_op jit(solution)/shard_map/ppermute | solution.py:25
  11.4 53.7 %all-to-all-start = ((bf16[16,22,2,4,128]{4,3,2,1,0:T(4,128)(2,1)}), bf16[16,22,2,4,128]{4,3,2,1,0:T(4,128)(2,1)}, u32[]{:S(2)}, u32[]{:S(2)}) async-start(bf16[16,22,2,4,128]{4,3,2,1,0:T(4,128)(2,1)} %copy.67), calls=%async_computation | async-start | bytes 1441792 | tf_op jit(solution)/shard_map/all_to_all | solution.py:334
  24.0 88.8 %all-gather.2.cloned.1.call-start = ((), (), s32[]{:S(2)}) async-start(), calls=%async_computation.1 | async-start | bytes 3604480 | tf_op jit(solution)/shard_map/all_gather | solution.py:336
  25.4 3.1 %copy-start.2 = (bf16[112,1024]{1,0:T(8,128)(2,1)}, bf16[112,1024]{1,0:T(8,128)(2,1)S(1)}, u32[]{:S(2)}) copy-start(bf16[112,1024]{1,0:T(8,128)(2,1)S(1)} %collective-permute-done) | copy-start | bytes 688132
  25.4 24.8 %collective-permute-start.1 = (bf16[2,112,1024]{2,1,0:T(8,128)(2,1)S(1)}, bf16[2,112,1024]{2,1,0:T(8,128)(2,1)S(1)}, u32[]{:S(2)}, u32[]{:S(2)}) collective-permute-start(bf16[2,112,1024]{2,1,0:T(8,128)(2,1)S(1)} %pad_maximum_fusion.1.near_ref.far_ref), channel_id=1, source_target_pairs={{0,8},{4,12},{8,16},{12,20},{16,24},{20,28},{24,32},{28,36},{32,40... | collective-permute-start | bytes 1376264 | tf_op jit(solution)/shard_map/ppermute | solution.py:25
  28.5 24.1 %collective-permute-start.3 = (bf16[2,112,1024]{2,1,0:T(8,128)(2,1)S(1)}, bf16[2,112,1024]{2,1,0:T(8,128)(2,1)S(1)}, u32[]{:S(2)}, u32[]{:S(2)}) collective-permute-start(bf16[2,112,1024]{2,1,0:T(8,128)(2,1)S(1)} %pad_maximum_fusion.1.near_ref.far_ref), channel_id=1, source_target_pairs={{0,248},{4,252},{8,0},{12,4},{16,8},{20,12},{24,16},{28,20},{32,24... | collective-permute-start | bytes 1376264 | tf_op jit(solution)/shard_map/ppermute | solution.py:25
  29.1 25.2 %collective-permute-start.4 = (bf16[1024,2,128]{2,0,1:T(8,128)(2,1)}, bf16[1024,2,128]{2,0,1:T(8,128)(2,1)}, u32[]{:S(2)}, u32[]{:S(2)}) collective-permute-start(bf16[1024,2,128]{2,0,1:T(8,128)(2,1)} %copy.73), channel_id=1, source_target_pairs={{0,2},{4,6},{9,11},{13,15},{18,16},{22,20},{27,25},{31,29},{32,34}... | collective-permute-start | bytes 1572872 | tf_op jit(solution)/shard_map/ppermute | solution.py:341
  50.2 12.9 %collective-permute-start.2 = (bf16[2,112,1024]{2,1,0:T(8,128)(2,1)S(1)}, bf16[2,112,1024]{2,1,0:T(8,128)(2,1)}, u32[]{:S(2)}, u32[]{:S(2)}) collective-permute-start(bf16[2,112,1024]{2,1,0:T(8,128)(2,1)S(1)} %collective-permute-done.1.near_ref.far_ref), channel_id=1, source_target_pairs={{0,8},{4,12},{8,16},{12,20},{16,24},{20,28},{24,32},{28,36},{32,40... | collective-permute-start | bytes 1376264 | tf_op jit(solution)/shard_map/ppermute | solution.py:25
  52.7 37.6 %collective-permute-start.6 = (bf16[2,112,1024]{2,1,0:T(8,128)(2,1)S(1)}, bf16[2,112,1024]{2,1,0:T(8,128)(2,1)}, u32[]{:S(2)}, u32[]{:S(2)}) collective-permute-start(bf16[2,112,1024]{2,1,0:T(8,128)(2,1)S(1)} %collective-permute-done.3.far_ref.near_ref), channel_id=1, source_target_pairs={{0,248},{4,252},{8,0},{12,4},{16,8},{20,12},{24,16},{28,20},{32,24... | collective-permute-start | bytes 1376264 | tf_op jit(solution)/shard_map/ppermute | solution.py:25
  56.1 11.8 %collective-permute-start.5 = (bf16[1024,2,128]{2,0,1:T(8,128)(2,1)}, bf16[1024,2,128]{2,0,1:T(8,128)(2,1)}, u32[]{:S(2)}, u32[]{:S(2)}) collective-permute-start(bf16[1024,2,128]{2,0,1:T(8,128)(2,1)} %broadcast_select_fusion), channel_id=1, source_target_pairs={{0,1},{4,5},{9,8},{13,12},{18,19},{22,23},{27,26},{31,30},{32,33},... | collective-permute-start | bytes 1572872 | tf_op jit(solution)/shard_map/ppermute | solution.py:345
  132.6 2.2 %collective-permute-start.7 = (bf16[2,8,3,56,128]{4,3,2,1,0:T(8,128)(2,1)S(1)}, bf16[2,8,3,56,128]{4,3,2,1,0:T(8,128)(2,1)S(1)}, u32[]{:S(2)}, u32[]{:S(2)}) collective-permute-start(bf16[2,8,3,56,128]{4,3,2,1,0:T(8,128)(2,1)S(1)} %slice.219), channel_id=1, source_target_pairs={{0,1},{1,0},{2,3},{3,2},{4,5},{5,4},{6,7},{7,6},{8,9},{9,8},{10,11... | collective-permute-start | bytes 2064392 | tf_op jit(solution)/shard_map/ppermute | solution.py:359
  134.9 11.7 %collective-permute-start.8 = (bf16[8,3,56,128]{3,2,1,0:T(8,128)(2,1)S(1)}, bf16[8,3,56,128]{3,2,1,0:T(8,128)(2,1)S(1)}, u32[]{:S(2)}, u32[]{:S(2)}) collective-permute-start(bf16[8,3,56,128]{3,2,1,0:T(8,128)(2,1)S(1)} %fusion.5), channel_id=1, source_target_pairs={{0,2},{2,0},{1,3},{3,1},{4,6},{6,4},{5,7},{7,5},{8,10},{10,8},{9,1... | collective-permute-start | bytes 1032200 | tf_op jit(solution)/shard_map/ppermute | solution.py:362
  146.9 5.5 %collective-permute-start.11 = (bf16[2,3,56,128]{3,2,1,0:T(8,128)(2,1)S(1)}, bf16[2,3,56,128]{3,2,1,0:T(8,128)(2,1)S(1)}, u32[]{:S(2)}, u32[]{:S(2)}) collective-permute-start(bf16[2,3,56,128]{3,2,1,0:T(8,128)(2,1)S(1)} %pad_maximum_fusion.4), channel_id=1, source_target_pairs={{0,252},{4,0},{8,4},{12,8},{16,12},{20,16},{24,20},{28,24},{32,28}... | collective-permute-start | bytes 258056 | tf_op jit(solution)/shard_map/ppermute | solution.py:25
  147.9 11.4 %collective-permute-start.9 = (bf16[3,3,56,128]{3,2,1,0:T(8,128)(2,1)S(1)}, bf16[3,3,56,128]{3,2,1,0:T(8,128)(2,1)S(1)}, u32[]{:S(2)}, u32[]{:S(2)}) collective-permute-start(bf16[3,3,56,128]{3,2,1,0:T(8,128)(2,1)S(1)} %pad_maximum_fusion.2), channel_id=1, source_target_pairs={{0,4},{4,8},{8,12},{12,16},{16,20},{20,24},{24,28},{28,32},{32,36}... | collective-permute-start | bytes 387080 | tf_op jit(solution)/shard_map/ppermute | solution.py:25
  150.0 9.2 %collective-permute-start.10 = (bf16[2,3,56,128]{3,2,1,0:T(8,128)(2,1)S(1)}, bf16[2,3,56,128]{3,2,1,0:T(8,128)(2,1)S(1)}, u32[]{:S(2)}, u32[]{:S(2)}) collective-permute-start(bf16[2,3,56,128]{3,2,1,0:T(8,128)(2,1)S(1)} %pad_maximum_fusion.3), channel_id=1, source_target_pairs={{0,8},{4,12},{8,16},{12,20},{16,24},{20,28},{24,32},{28,36},{32,40... | collective-permute-start | bytes 258056 | tf_op jit(solution)/shard_map/ppermute | solution.py:25
  159.3 5.6 %collective-permute-start.12 = (f32[3,56,128]{2,1,0:T(8,128)S(1)}, f32[3,56,128]{2,1,0:T(8,128)S(1)}, u32[]{:S(2)}, u32[]{:S(2)}) collective-permute-start(f32[3,56,128]{2,1,0:T(8,128)S(1)} %get-tuple-element.29), channel_id=1, source_target_pairs={{0,240},{4,244},{8,248},{12,252},{16,0},{20,4},{24,8},{28,12},{32,... | collective-permute-start | bytes 258056 | tf_op jit(solution)/shard_map/ppermute | solution.py:25
  162.2 9.6 %collective-permute-start.13 = (f32[3,56,128]{2,1,0:T(8,128)S(1)}, f32[3,56,128]{2,1,0:T(8,128)S(1)}, u32[]{:S(2)}, u32[]{:S(2)}) collective-permute-start(f32[3,56,128]{2,1,0:T(8,128)S(1)} %get-tuple-element.30), channel_id=1, source_target_pairs={{0,16},{4,20},{8,24},{12,28},{16,32},{20,36},{24,40},{28,44},{32,4... | collective-permute-start | bytes 258056 | tf_op jit(solution)/shard_map/ppermute | solution.py:25
Sparse Core Ops, SparseCore 0:
  67.6 39.0 all-gather.1

commit v2 on v1

--- a/solution.py
+++ b/solution.py
@@ -17,7 +17,7 @@
 SLOTS = 22
 CHUNKS = (TOTAL + SLOTS * (CHUNK - 1)) // CHUNK // 2 * 2 + 2
 MSG = 112
-VMEM_LIMIT = 50 * 1024 * 1024
+VMEM_LIMIT = 36 * 2**20
 
 
 def from_behind(x, axis, by):
@@ -29,14 +29,18 @@
     return jnp.where(mask, first, pltpu.roll(second, 4, 0))
 
 
-def density_kernel(near_ref, far_ref, zv_ref, zc_ref, *rest):
-    mv_ref, mc_ref, left, right, va, ca, vb, cb = rest[-8:]
+def density_kernel(count, ends, steps, *refs):
+    pair_refs = refs[:count]
+    zv_ref, zc_ref = refs[count : count + 2]
+    mv_ref, mc_ref, left, right, va, ca, vb, cb = refs[-8:]
     step = pl.program_id(0)
     low = lax.broadcasted_iota(jnp.int32, (8, 1024), 0) < 4
 
     def produce(chunk, v_buf, c_buf):
         block = chunk // 3
         jh = chunk % 3
+        if ends:
+            block = block + jnp.where(block >= 2, 4, 0)
         for cv, buf in ((0, v_buf), (1, c_buf)):
             for jl in range(2):
                 point = block * KB + 2 * jh + jl
@@ -93,64 +97,63 @@
 
     @pl.when(step == 0)
     def _():
-        for b in range(4):
-            ref = near_ref if b < 2 else far_ref
+        for b in range(2 * count):
             for j in range(KB):
-                x = ref[b % 2, 16 * j : 16 * j + 16, :].astype(f32)
-                if b < 2:
-                    left[b * KB + j] = x
+                x = pair_refs[b // 2][b % 2, 16 * j : 16 * j + 16, :].astype(f32)
+                left[b * KB + j] = x
                 if b > 0:
-                    p = j // 2
+                    index = (b - 1) * 3 + j // 2
                     for r in range(2):
                         half = x[8 * r : 8 * r + 8]
+                        turned = pltpu.roll(half, 4, 0)
                         if j % 2 == 0:
-                            right[(b - 1) * 3 + p, 0, r] = half
-                            right[(b - 1) * 3 + p, 1, r] = pltpu.roll(half, 4, 0)
+                            right[index, 0, r] = half
+                            right[index, 1, r] = turned
                         else:
-                            index = (b - 1) * 3 + p
-                            right[index, 0, r] = jnp.where(low, right[index, 0, r], pltpu.roll(half, 4, 0))
+                            right[index, 0, r] = jnp.where(low, right[index, 0, r], turned)
                             right[index, 1, r] = jnp.where(low, right[index, 1, r], half)
         drain(produce(0, va, ca))
 
     drain(consume(0, va, ca), produce(2 * step + 1, vb, cb))
-    drain(consume(1, vb, cb), produce(jnp.minimum(2 * step + 2, 5), va, ca))
-
-
-def densities(call, near, far, zv, zc, previous):
+    drain(consume(1, vb, cb), produce(jnp.minimum(2 * step + 2, 2 * steps - 1), va, ca))
+
+
+def densities(pairs, ends, zv, zc, previous):
     whole = lambda shape: pl.BlockSpec(shape, lambda n: (0,) * len(shape), pipeline_mode=pl.Buffered(1))
-    in_specs = [whole(near.shape), whole(far.shape), whole(zv.shape), whole(zc.shape)]
-    operands = [near, far, zv, zc]
+    operands = list(pairs) + [zv, zc]
+    in_specs = [whole(x.shape) for x in operands]
     aliases = {}
     if previous is not None:
+        aliases = {len(operands): 0, len(operands) + 1: 1}
         in_specs += [pl.BlockSpec(memory_space=pl.ANY)] * 2
         operands += list(previous)
-        aliases = {4: 0, 5: 1}
+    count = len(pairs)
+    steps = 6
+    place = (lambda n: (n + jnp.where(n >= 3, 6, 0), 0, 0)) if ends else (lambda n: (3 + n, 0, 0))
     wv = zv.shape[1]
     wc = zc.shape[1]
-    flops = 2 * 2 * PAIRS * 16 * 2048 * (wv + wc)
     return pl.pallas_call(
-        density_kernel,
-        grid=(3,),
+        functools.partial(density_kernel, count, ends, steps),
+        grid=(steps,),
         in_specs=in_specs,
-        out_specs=[
-            pl.BlockSpec((48, 16, wv), lambda n: (3 * call + n, 0, 0)),
-            pl.BlockSpec((48, 16, wc), lambda n: (3 * call + n, 0, 0)),
-        ],
+        out_specs=[pl.BlockSpec((48, 16, wv), place), pl.BlockSpec((48, 16, wc), place)],
         out_shape=[
             jax.ShapeDtypeStruct((TOTAL, 16, wv), bf16),
             jax.ShapeDtypeStruct((TOTAL, 16, wc), bf16),
         ],
         scratch_shapes=[
-            pltpu.VMEM((2 * KB, 16, 1024), f32),
-            pltpu.VMEM((9, 2, 2, 8, 1024), f32),
+            pltpu.VMEM((2 * count * KB, 16, 1024), f32),
+            pltpu.VMEM(((2 * count - 1) * 3, 2, 2, 8, 1024), f32),
             pltpu.VMEM((384, 2048), bf16),
             pltpu.VMEM((384, 2048), bf16),
             pltpu.VMEM((384, 2048), bf16),
             pltpu.VMEM((384, 2048), bf16),
         ],
         input_output_aliases=aliases,
-        compiler_params=pltpu.CompilerParams(vmem_limit_bytes=VMEM_LIMIT),
-        cost_estimate=pl.CostEstimate(flops=flops, bytes_accessed=8 * 2**20, transcendentals=0),
+        compiler_params=pltpu.CompilerParams(vmem_limit_bytes=28 * 2**20),
+        cost_estimate=pl.CostEstimate(
+            flops=2 * steps * 48 * 16 * 2048 * (wv + wc), bytes_accessed=steps * 3 * 2**20, transcendentals=0
+        ),
         name="densities",
     )(*operands)
 
@@ -326,19 +329,19 @@
     tail = jnp.pad(slots.astype(bf16), ((0, 15), (0, 1024 - PAIRS)))
     message = jnp.concatenate([bloch_samples.reshape(96, 1024), tail], axis=0)
     following = from_behind(message, "ka", -1)
+    zv = zeta_matrix(zeta_vectors)
+    mine = lax.dynamic_slice_in_dim(zeta_vectors, 128 * lax.rem(part, 2), 128, 2)
+    mine, following = lax.optimization_barrier((mine, following))
+    holders = [(k, (k % WIN) // 2) for k in range(ka_count)]
+    over = lax.ppermute(mine, ("ka", "ga"), [(4 * k + h, 4 * k + (h ^ 2)) for k, h in holders])
     pieces = jnp.transpose(screened.reshape(SLOTS, 2, 4, WIN, 128), (3, 0, 1, 2, 4))
     pieces = jnp.concatenate([pieces, pieces], axis=0)
+    pieces, following = lax.optimization_barrier((pieces, following))
     line = 2 * WIN
     near_groups = [[x * line + s for s in range(line)] for x in range(ka_count // line)]
     x_groups = [[x * line + s for x in range(ka_count // line)] for s in range(line)]
     pieces = lax.all_to_all(pieces, "ka", 0, 0, axis_index_groups=near_groups, tiled=True)
     rows = jnp.transpose(pieces, (1, 2, 0, 3, 4)).reshape(SLOTS, 2, 4 * line, 128)
-    w = lax.all_gather(rows, "ka", axis_index_groups=x_groups)
-    zv = zeta_matrix(zeta_vectors)
-    mine = lax.dynamic_slice_in_dim(zeta_vectors, 128 * lax.rem(part, 2), 128, 2)
-    mine, following = lax.optimization_barrier((mine, following))
-    holders = [(k, (k % WIN) // 2) for k in range(ka_count)]
-    over = lax.ppermute(mine, ("ka", "ga"), [(4 * k + h, 4 * k + (h ^ 2)) for k, h in holders])
     held = jnp.where(ga == part // 2, mine, over)
     moves = [(4 * k + h, 4 * k + (h ^ 1)) for k, h in holders]
     moves += [(4 * k + (h ^ 2), 4 * k + (h ^ 3)) for k, h in holders]
@@ -346,14 +349,14 @@
     here = jnp.stack([message, following])
     ahead = from_behind(here, "ka", -2)
     behind = from_behind(here, "ka", 2)
+    rows, ahead, behind, zv = lax.optimization_barrier((rows, ahead, behind, zv))
+    w = lax.all_gather(rows, "ka", axis_index_groups=x_groups)
     ahead2 = from_behind(ahead, "ka", -2)
     behind2 = from_behind(behind, "ka", 2)
-    pairs = [behind2, behind, here, ahead, ahead2]
-    made = None
-    for call in (2, 1, 3, 0):
-        made = densities(call, pairs[call], pairs[call + 1], zv, zc, made)
-    mv, mc = made
-    all_slots = jnp.concatenate([x[:, 96, :PAIRS] for x in pairs[:4]], axis=0).reshape(TOTAL)
+    made = densities((behind, here, ahead), False, zv, zc, None)
+    made = densities((behind2, behind, here, ahead, ahead2), True, zv, zc, made)
+    mv, mc, *pairs = lax.optimization_barrier((*made, behind2, behind, here, ahead))
+    all_slots = jnp.concatenate([x[:, 96, :PAIRS] for x in pairs], axis=0).reshape(TOTAL)
     order, slot_of, used = schedule(all_slots.astype(jnp.int32))
     partial = apply_screened(order, slot_of, used, ga_word, mv, mc, w)
     arrived = lax.ppermute(partial[2:].astype(bf16), "ga", [(0, 1), (1, 0), (2, 3), (3, 2)])

time: 181 us -> 186 us (1.028)
  local copies, waits for them, and re-layouts: 8.7 us -> 21.6 us
  Pallas kernels: 64.6 us -> 58.2 us
  waiting for transfers between devices: 53.7 us -> 51 us
  starting transfers between devices: 31.3 us -> 33.2 us
    ppermute x10, waiting for transfers between devices: 42.2 us -> 30.5 us  [from_behind(): return lax.ppermute(x, axis, [(i, (i + by) % count) for i in range(count)])]
    unnamed x11 -> x19, local copies, waits for them, and re-layouts: 0.13 us -> 10.9 us
    all_to_all x1, waiting for transfers between devices: 0.01 us -> 9.98 us  [body(): lax.all_to_all(pieces, 'ka', 0, 0, axis_index_groups=near_groups, tiled=T...]
    pallas_call x4 -> x2, Pallas kernels: 43.4 us -> 39.2 us  [densities(): pl.pallas_call(functools.partial(density_kernel, count, ends, steps), gri...]
    pallas_call x1, Pallas kernels: 19.6 us -> 17.4 us  [apply_screened(): pl.pallas_call(apply_kernel, in_specs=[smem] * 4 + [vmem] * 3, out_specs=...]
    slice x3 -> x4, local copies, waits for them, and re-layouts: 0.68 us -> 2.72 us  [body(): x[:, 96, :PAIRS]]
  transfers between devices with their start and end apart: 16 -> 16, of which waited for: 8 -> 9; matrix products, arithmetic and copies ran while one was open for 8% -> 8% of each run, Pallas kernels for 24% -> 21%
where the time goes in v2:
time: 186 us; the launch traced here: 184 us
  Pallas kernels  58.2 us (31%)
  waiting for transfers between devices  51 us (27%)
  starting transfers between devices  33.2 us (18%)
  local copies, waits for them, and re-layouts  21.6 us (12%)
  between operations  13.8 us (7%)
  other arithmetic  6.46 us (3%)
    pallas_call x2, Pallas kernels, densities(): pl.pallas_call(functools.partial(density_kernel, count, ends, steps), gri...  39.2 us
    ppermute x10, waiting for transfers between devices, from_behind(): return lax.ppermute(x, axis, [(i, (i + by) % count) for i in range(count)])  30.5 us
    pallas_call x1, Pallas kernels, apply_screened(): pl.pallas_call(apply_kernel, in_specs=[smem] * 4 + [vmem] * 3, out_specs=...  17.4 us
    all_to_all x1, starting transfers between devices, body(): lax.all_to_all(pieces, 'ka', 0, 0, axis_index_groups=near_groups, tiled=T...  13.8 us
    ppermute x10, starting transfers between devices, from_behind(): return lax.ppermute(x, axis, [(i, (i + by) % count) for i in range(count)])  12.8 us
    unnamed x19, local copies, waits for them, and re-layouts  10.9 us
    all_to_all x1, waiting for transfers between devices, body(): lax.all_to_all(pieces, 'ka', 0, 0, axis_index_groups=near_groups, tiled=T...  9.98 us
    ppermute x1, waiting for transfers between devices, body(): lax.ppermute(other, 'ga', [(0, 2), (2, 0), (1, 3), (3, 1)]).astype(f32)  8.35 us
  transfers between devices with their start and end apart: 16, of which 9 were waited for; matrix products, arithmetic and copies ran while one was open for 8% of the time, Pallas kernels for 21%

profile of v2, /device:TPU:40, one launch (start us, length us, event | category | flops | bytes accessed | tf_op | source)
XLA Modules:
  0.0 184.3 jit_solution(13318807405690532856)
XLA Ops:
  9.1 1.4 constant_dynamic-slice_fusion
  11.3 5.5 %collective-permute-done = bf16[112,1024]{1,0:T(8,128)(2,1)S(1)} collective-permute-done((bf16[112,1024]{1,0:T(8,128)(2,1)S(1)}, bf16[112,1024]{1,0:T(8,128)(2,1)S(1)}, u32[]{:S(2)}, u32[]{:S(2)}) %collective-permute-start) | collective-permute-done | bytes 229408 | tf_op jit(solution)/shard_map/ppermute | solution.py:25
  16.9 1.5 collective-permute-start.5
  18.6 1.5 fusion.17
  20.1 1.2 copy.57
  21.3 13.8 %all-to-all-start = ((bf16[16,22,2,4,128]{4,3,2,1,0:T(4,128)(2,1)}), bf16[16,22,2,4,128]{4,3,2,1,0:T(4,128)(2,1)}, u32[]{:S(2)}, u32[]{:S(2)}) async-start(bf16[16,22,2,4,128]{4,3,2,1,0:T(4,128)(2,1)} %copy.57), calls=%async_computation | async-start | bytes 1441792 | tf_op jit(solution)/shard_map/all_to_all | solution.py:343
  35.2 1.1 broadcast_select_fusion
  36.3 1.3 collective-permute-start.6
  40.1 1.4 collective-permute-start.2
  41.9 10.0 %all-to-all-done = bf16[16,22,2,4,128]{4,3,2,1,0:T(4,128)(2,1)} async-done(((bf16[16,22,2,4,128]{4,3,2,1,0:T(4,128)(2,1)}), bf16[16,22,2,4,128]{4,3,2,1,0:T(4,128)(2,1)}, u32[]{:S(2)}, u32[]{:S(2)}) %all-to-all-start) | async-done | bytes 720928 | tf_op jit(solution)/shard_map/all_to_all | solution.py:343
  51.9 2.4 %copy.58 = bf16[22,2,16,4,128]{4,3,2,1,0:T(4,128)(2,1)} copy(bf16[22,2,16,4,128]{4,3,1,0,2:T(4,128)(2,1)} %bitcast.5) | data formatting | bytes 1441792 | tf_op jit(solution)/shard_map/transpose | solution.py:344
  54.3 5.7 %collective-permute-done.1.refs_2_.refs_3_ = bf16[2,112,1024]{2,1,0:T(8,128)(2,1)} collective-permute-done((bf16[2,112,1024]{2,1,0:T(8,128)(2,1)}, bf16[2,112,1024]{2,1,0:T(8,128)(2,1)}, u32[]{:S(2)}, u32[]{:S(2)}) %collective-permute-start.1) | collective-permute-done | bytes 458784 | tf_op jit(solution)/shard_map/ppermute | solution.py:25
  60.0 1.5 collective-permute-start.3
  61.5 2.4 %collective-permute-start.4 = (bf16[2,112,1024]{2,1,0:T(8,128)(2,1)}, bf16[2,112,1024]{2,1,0:T(8,128)(2,1)}, u32[]{:S(2)}, u32[]{:S(2)}) collective-permute-start(bf16[2,112,1024]{2,1,0:T(8,128)(2,1)} %collective-permute-done.1.refs_2_.refs_3_), channel_id=1, source_target_pairs={{0,248},{4,252},{8,0},{12,4},{16,8},{20,12},{24,16},{28,20},{32,24... | collective-permute-start | bytes 1376264 | tf_op jit(solution)/shard_map/ppermute | solution.py:25
  63.9 19.3 %densities.2 = (bf16[576,16,512]{2,1,0:T(8,128)(2,1)S(1)}, bf16[576,16,256]{2,1,0:T(8,128)(2,1)S(1)}) custom-call(bf16[2,112,1024]{2,1,0:T(8,128)(2,1)} %collective-permute-done.2.refs_0_.refs_1_, bf16[2,112,1024]{2,1,0:T(8,128)(2,1)} %pad_maximum_fusion.1.refs_1_.refs_2_, bf16[2,112,1024]{2,1,0:T(8,128)(2,1)} %collective-permute-done.1.refs_2_.refs_3_, ...), custom_call_target="tpu_custom_call" | custom-call | flops 14495514624 | bytes 18874368 | tf_op jit(solution)/shard_map/densities/pallas_call | solution.py:135
  83.2 19.9 %densities.3 = (bf16[576,16,512]{2,1,0:T(8,128)(2,1)S(1)}, bf16[576,16,256]{2,1,0:T(8,128)(2,1)S(1)}) custom-call(bf16[2,112,1024]{2,1,0:T(8,128)(2,1)} %collective-permute-done.3.refs_0_, bf16[2,112,1024]{2,1,0:T(8,128)(2,1)} %collective-permute-done.2.refs_0_.refs_1_, ...), custom_call_target="tpu_custom_call", output_to_operand_aliasing={{0}: (7, {}), {1}: (8, {})} | custom-call | flops 14495514624 | bytes 18874368 | tf_op jit(solution)/shard_map/densities/pallas_call | solution.py:135
  103.1 3.6 %copy-done.1 = bf16[576,16,512]{2,1,0:T(8,128)(2,1)} copy-done((bf16[576,16,512]{2,1,0:T(8,128)(2,1)}, bf16[576,16,512]{2,1,0:T(8,128)(2,1)S(1)}, u32[]{:S(2)}) %copy-start.1) | copy-done | bytes 9437208
  106.8 2.2 %copy-done.2 = bf16[576,16,256]{2,1,0:T(8,128)(2,1)} copy-done((bf16[576,16,256]{2,1,0:T(8,128)(2,1)}, bf16[576,16,256]{2,1,0:T(8,128)(2,1)S(1)}, u32[]{:S(2)}) %copy-start.2) | copy-done | bytes 4718616
  113.6 1.8 copy-done
  115.4 2.3 %copy-done.3 = bf16[576,16,256]{2,1,0:T(8,128)(2,1)S(1)} copy-done((bf16[576,16,256]{2,1,0:T(8,128)(2,1)S(1)}, bf16[576,16,256]{2,1,0:T(8,128)(2,1)}, u32[]{:S(2)}) %copy-start.3) | copy-done | bytes 4718616
  117.7 17.4 %apply_screened.1 = f32[4,8,3,56,128]{4,3,2,1,0:T(8,128)S(1)} custom-call(s32[928]{0:T(1024)S(1)} %broadcast_add_fusion.order_ref, s32[58]{0:T(128)S(1)} %broadcast_minimum_fusion.slot_ref, s32[1]{0:T(128)} %bitcast.13.used_ref, s32[1]{0:T(128)} %bitcast.ga_ref, bf16[576,16,512]{2,1,0:T(8,128)(2,1)} %copy-done.1, bf16[576,16,256]{2,1,0:T(8,128)(2,1)S(1)} %copy-done.3, ...), custom_call_target="tpu_custom_call" | custom-call | flops 6000000000 | bytes 18874368 | tf_op jit(solution)/shard_map/apply_screened/pallas_call | solution.py:239
  135.3 2.1 %collective-permute-done.7 = bf16[2,8,3,56,128]{4,3,2,1,0:T(8,128)(2,1)S(1)} collective-permute-done((bf16[2,8,3,56,128]{4,3,2,1,0:T(8,128)(2,1)S(1)}, bf16[2,8,3,56,128]{4,3,2,1,0:T(8,128)(2,1)S(1)}, u32[]{:S(2)}, u32[]{:S(2)}) %collective-permute-start.7) | collective-permute-done | bytes 688160 | tf_op jit(solution)/shard_map/ppermute | solution.py:362
  137.5 3.7 %collective-permute-start.8 = (bf16[8,3,56,128]{3,2,1,0:T(8,128)(2,1)S(1)}, bf16[8,3,56,128]{3,2,1,0:T(8,128)(2,1)S(1)}, u32[]{:S(2)}, u32[]{:S(2)}) collective-permute-start(bf16[8,3,56,128]{3,2,1,0:T(8,128)(2,1)S(1)} %fusion.5), channel_id=1, source_target_pairs={{0,2},{2,0},{1,3},{3,1},{4,6},{6,4},{5,7},{7,5},{8,10},{10,8},{9,1... | collective-permute-start | bytes 1032200 | tf_op jit(solution)/shard_map/ppermute | solution.py:365
  141.2 8.4 %collective-permute-done.8 = bf16[8,3,56,128]{3,2,1,0:T(8,128)(2,1)S(1)} collective-permute-done((bf16[8,3,56,128]{3,2,1,0:T(8,128)(2,1)S(1)}, bf16[8,3,56,128]{3,2,1,0:T(8,128)(2,1)S(1)}, u32[]{:S(2)}, u32[]{:S(2)}) %collective-permute-start.8) | collective-permute-done | bytes 344096 | tf_op jit(solution)/shard_map/ppermute | solution.py:365
  149.9 1.3 collective-permute-start.11
  151.2 2.0 %collective-permute-start.9 = (bf16[3,3,56,128]{3,2,1,0:T(8,128)(2,1)S(1)}, bf16[3,3,56,128]{3,2,1,0:T(8,128)(2,1)S(1)}, u32[]{:S(2)}, u32[]{:S(2)}) collective-permute-start(bf16[3,3,56,128]{3,2,1,0:T(8,128)(2,1)S(1)} %pad_maximum_fusion.2), channel_id=1, source_target_pairs={{0,4},{4,8},{8,12},{12,16},{16,20},{20,24},{24,28},{28,32},{32,36}... | collective-permute-start | bytes 387080 | tf_op jit(solution)/shard_map/ppermute | solution.py:25
  153.4 2.0 %collective-permute-done.11 = bf16[2,3,56,128]{3,2,1,0:T(8,128)(2,1)S(1)} collective-permute-done((bf16[2,3,56,128]{3,2,1,0:T(8,128)(2,1)S(1)}, bf16[2,3,56,128]{3,2,1,0:T(8,128)(2,1)S(1)}, u32[]{:S(2)}, u32[]{:S(2)}) %collective-permute-start.11) | collective-permute-done | bytes 86048 | tf_op jit(solution)/shard_map/ppermute | solution.py:25
  155.4 8.1 %collective-permute-done.10 = bf16[2,3,56,128]{3,2,1,0:T(8,128)(2,1)S(1)} collective-permute-done((bf16[2,3,56,128]{3,2,1,0:T(8,128)(2,1)S(1)}, bf16[2,3,56,128]{3,2,1,0:T(8,128)(2,1)S(1)}, u32[]{:S(2)}, u32[]{:S(2)}) %collective-permute-start.10) | collective-permute-done | bytes 86048 | tf_op jit(solution)/shard_map/ppermute | solution.py:25
  163.5 2.5 %collective-permute-start.12 = (f32[3,56,128]{2,1,0:T(8,128)S(1)}, f32[3,56,128]{2,1,0:T(8,128)S(1)}, u32[]{:S(2)}, u32[]{:S(2)}) collective-permute-start(f32[3,56,128]{2,1,0:T(8,128)S(1)} %get-tuple-element.45), channel_id=1, source_target_pairs={{0,240},{4,244},{8,248},{12,252},{16,0},{20,4},{24,8},{28,12},{32,... | collective-permute-start | bytes 258056 | tf_op jit(solution)/shard_map/ppermute | solution.py:25
  166.5 2.6 %collective-permute-done.12 = f32[3,56,128]{2,1,0:T(8,128)S(1)} collective-permute-done((f32[3,56,128]{2,1,0:T(8,128)S(1)}, f32[3,56,128]{2,1,0:T(8,128)S(1)}, u32[]{:S(2)}, u32[]{:S(2)}) %collective-permute-start.12) | collective-permute-done | bytes 86048 | tf_op jit(solution)/shard_map/ppermute | solution.py:25
  169.1 6.6 %collective-permute-done.13 = f32[3,56,128]{2,1,0:T(8,128)S(1)} collective-permute-done((f32[3,56,128]{2,1,0:T(8,128)S(1)}, f32[3,56,128]{2,1,0:T(8,128)S(1)}, u32[]{:S(2)}, u32[]{:S(2)}) %collective-permute-start.13) | collective-permute-done | bytes 86048 | tf_op jit(solution)/shard_map/ppermute | solution.py:25
  175.8 1.6 arrange.1
  (79 shorter events, 12.3 us)
Async XLA Ops:
  6.5 11.8 %copy-start.5 = (bf16[22,2,4,1024]{3,2,1,0:T(4,128)(2,1)S(1)}, bf16[22,2,4,1024]{3,2,1,0:T(4,128)(2,1)}, u32[]{:S(2)}) copy-start(bf16[22,2,4,1024]{3,2,1,0:T(4,128)(2,1)} %param.6) | copy-start | bytes 1081348
  8.5 10.1 %copy-start.4 = (bf16[1024,2,256]{2,1,0:T(2,128)(2,1)S(1)}, bf16[1024,2,256]{2,1,0:T(2,128)(2,1)}, u32[]{:S(2)}) copy-start(bf16[1024,2,256]{2,1,0:T(2,128)(2,1)} %param.5) | copy-start | bytes 3145732
  8.5 8.3 %collective-permute-start = (bf16[112,1024]{1,0:T(8,128)(2,1)S(1)}, bf16[112,1024]{1,0:T(8,128)(2,1)S(1)}, u32[]{:S(2)}, u32[]{:S(2)}) collective-permute-start(bf16[112,1024]{1,0:T(8,128)(2,1)S(1)} %get-tuple-element.59), channel_id=1, source_target_pairs={{0,252},{4,0},{8,4},{12,8},{16,12},{20,16},{24,20},{28,24},{32,28}... | collective-permute-start | bytes 688136 | tf_op jit(solution)/shard_map/ppermute | solution.py:25
  16.9 1.5 copy-start.6
  16.9 18.3 %collective-permute-start.5 = (bf16[1024,2,128]{2,0,1:T(8,128)(2,1)}, bf16[1024,2,128]{2,0,1:T(8,128)(2,1)}, u32[]{:S(2)}, u32[]{:S(2)}) collective-permute-start(bf16[1024,2,128]{2,0,1:T(8,128)(2,1)} %copy.65), channel_id=1, source_target_pairs={{0,2},{4,6},{9,11},{13,15},{18,16},{22,20},{27,25},{31,29},{32,34}... | collective-permute-start | bytes 1572872 | tf_op jit(solution)/shard_map/ppermute | solution.py:336
  21.3 30.6 %all-to-all-start = ((bf16[16,22,2,4,128]{4,3,2,1,0:T(4,128)(2,1)}), bf16[16,22,2,4,128]{4,3,2,1,0:T(4,128)(2,1)}, u32[]{:S(2)}, u32[]{:S(2)}) async-start(bf16[16,22,2,4,128]{4,3,2,1,0:T(4,128)(2,1)} %copy.57), calls=%async_computation | async-start | bytes 1441792 | tf_op jit(solution)/shard_map/all_to_all | solution.py:343
  35.1 78.4 %all-gather.3.cloned.1.call-start = ((), (), s32[]{:S(2)}) async-start(), calls=%async_computation.1 | async-start | bytes 3604480 | tf_op jit(solution)/shard_map/all_gather | solution.py:353
  36.3 5.3 %collective-permute-start.6 = (bf16[1024,2,128]{2,0,1:T(8,128)(2,1)S(1)}, bf16[1024,2,128]{2,0,1:T(8,128)(2,1)S(1)}, u32[]{:S(2)}, u32[]{:S(2)}) collective-permute-start(bf16[1024,2,128]{2,0,1:T(8,128)(2,1)S(1)} %broadcast_select_fusion), channel_id=1, source_target_pairs={{0,1},{4,5},{9,8},{13,12},{18,19},{22,23},{27,26},{31,30},{32,33},... | collective-permute-start | bytes 1572872 | tf_op jit(solution)/shard_map/ppermute | solution.py:348
  37.8 0.9 copy-start.7
  39.5 20.5 %collective-permute-start.1 = (bf16[2,112,1024]{2,1,0:T(8,128)(2,1)}, bf16[2,112,1024]{2,1,0:T(8,128)(2,1)}, u32[]{:S(2)}, u32[]{:S(2)}) collective-permute-start(bf16[2,112,1024]{2,1,0:T(8,128)(2,1)} %pad_maximum_fusion.1.refs_1_.refs_2_), channel_id=1, source_target_pairs={{0,248},{4,252},{8,0},{12,4},{16,8},{20,12},{24,16},{28,20},{32,24... | collective-permute-start | bytes 1376264 | tf_op jit(solution)/shard_map/ppermute | solution.py:25
  40.1 19.9 %collective-permute-start.2 = (bf16[2,112,1024]{2,1,0:T(8,128)(2,1)}, bf16[2,112,1024]{2,1,0:T(8,128)(2,1)}, u32[]{:S(2)}, u32[]{:S(2)}) collective-permute-start(bf16[2,112,1024]{2,1,0:T(8,128)(2,1)} %pad_maximum_fusion.1.refs_1_.refs_2_), channel_id=1, source_target_pairs={{0,8},{4,12},{8,16},{12,20},{16,24},{20,28},{24,32},{28,36},{32,40... | collective-permute-start | bytes 1376264 | tf_op jit(solution)/shard_map/ppermute | solution.py:25
  60.0 23.2 %collective-permute-start.3 = (bf16[2,112,1024]{2,1,0:T(8,128)(2,1)}, bf16[2,112,1024]{2,1,0:T(8,128)(2,1)}, u32[]{:S(2)}, u32[]{:S(2)}) collective-permute-start(bf16[2,112,1024]{2,1,0:T(8,128)(2,1)} %collective-permute-done.2.refs_0_.refs_1_), channel_id=1, source_target_pairs={{0,8},{4,12},{8,16},{12,20},{16,24},{20,28},{24,32},{28,36},{32,40... | collective-permute-start | bytes 1376264 | tf_op jit(solution)/shard_map/ppermute | solution.py:25
  61.5 21.7 %collective-permute-start.4 = (bf16[2,112,1024]{2,1,0:T(8,128)(2,1)}, bf16[2,112,1024]{2,1,0:T(8,128)(2,1)}, u32[]{:S(2)}, u32[]{:S(2)}) collective-permute-start(bf16[2,112,1024]{2,1,0:T(8,128)(2,1)} %collective-permute-done.1.refs_2_.refs_3_), channel_id=1, source_target_pairs={{0,248},{4,252},{8,0},{12,4},{16,8},{20,12},{24,16},{28,20},{32,24... | collective-permute-start | bytes 1376264 | tf_op jit(solution)/shard_map/ppermute | solution.py:25
  103.1 3.6 %copy-start.1 = (bf16[576,16,512]{2,1,0:T(8,128)(2,1)}, bf16[576,16,512]{2,1,0:T(8,128)(2,1)S(1)}, u32[]{:S(2)}) copy-start(bf16[576,16,512]{2,1,0:T(8,128)(2,1)S(1)} %get-tuple-element.38.mv_ref) | copy-start | bytes 28311556
  106.8 2.2 %copy-start.2 = (bf16[576,16,256]{2,1,0:T(8,128)(2,1)}, bf16[576,16,256]{2,1,0:T(8,128)(2,1)S(1)}, u32[]{:S(2)}) copy-start(bf16[576,16,256]{2,1,0:T(8,128)(2,1)S(1)} %get-tuple-element.39.mc_ref) | copy-start | bytes 14155780
  113.5 1.8 copy-start
  115.4 2.3 %copy-start.3 = (bf16[576,16,256]{2,1,0:T(8,128)(2,1)S(1)}, bf16[576,16,256]{2,1,0:T(8,128)(2,1)}, u32[]{:S(2)}) copy-start(bf16[576,16,256]{2,1,0:T(8,128)(2,1)} %copy-done.2) | copy-start | bytes 14155780
  135.2 2.2 %collective-permute-start.7 = (bf16[2,8,3,56,128]{4,3,2,1,0:T(8,128)(2,1)S(1)}, bf16[2,8,3,56,128]{4,3,2,1,0:T(8,128)(2,1)S(1)}, u32[]{:S(2)}, u32[]{:S(2)}) collective-permute-start(bf16[2,8,3,56,128]{4,3,2,1,0:T(8,128)(2,1)S(1)} %slice.208), channel_id=1, source_target_pairs={{0,1},{1,0},{2,3},{3,2},{4,5},{5,4},{6,7},{7,6},{8,9},{9,8},{10,11... | collective-permute-start | bytes 2064392 | tf_op jit(solution)/shard_map/ppermute | solution.py:362
  137.5 12.1 %collective-permute-start.8 = (bf16[8,3,56,128]{3,2,1,0:T(8,128)(2,1)S(1)}, bf16[8,3,56,128]{3,2,1,0:T(8,128)(2,1)S(1)}, u32[]{:S(2)}, u32[]{:S(2)}) collective-permute-start(bf16[8,3,56,128]{3,2,1,0:T(8,128)(2,1)S(1)} %fusion.5), channel_id=1, source_target_pairs={{0,2},{2,0},{1,3},{3,1},{4,6},{6,4},{5,7},{7,5},{8,10},{10,8},{9,1... | collective-permute-start | bytes 1032200 | tf_op jit(solution)/shard_map/ppermute | solution.py:365
  149.9 5.5 %collective-permute-start.11 = (bf16[2,3,56,128]{3,2,1,0:T(8,128)(2,1)S(1)}, bf16[2,3,56,128]{3,2,1,0:T(8,128)(2,1)S(1)}, u32[]{:S(2)}, u32[]{:S(2)}) collective-permute-start(bf16[2,3,56,128]{3,2,1,0:T(8,128)(2,1)S(1)} %pad_maximum_fusion.4), channel_id=1, source_target_pairs={{0,252},{4,0},{8,4},{12,8},{16,12},{20,16},{24,20},{28,24},{32,28}... | collective-permute-start | bytes 258056 | tf_op jit(solution)/shard_map/ppermute | solution.py:25
  151.2 12.3 %collective-permute-start.9 = (bf16[3,3,56,128]{3,2,1,0:T(8,128)(2,1)S(1)}, bf16[3,3,56,128]{3,2,1,0:T(8,128)(2,1)S(1)}, u32[]{:S(2)}, u32[]{:S(2)}) collective-permute-start(bf16[3,3,56,128]{3,2,1,0:T(8,128)(2,1)S(1)} %pad_maximum_fusion.2), channel_id=1, source_target_pairs={{0,4},{4,8},{8,12},{12,16},{16,20},{20,24},{24,28},{28,32},{32,36}... | collective-permute-start | bytes 387080 | tf_op jit(solution)/shard_map/ppermute | solution.py:25
  153.2 10.2 %collective-permute-start.10 = (bf16[2,3,56,128]{3,2,1,0:T(8,128)(2,1)S(1)}, bf16[2,3,56,128]{3,2,1,0:T(8,128)(2,1)S(1)}, u32[]{:S(2)}, u32[]{:S(2)}) collective-permute-start(bf16[2,3,56,128]{3,2,1,0:T(8,128)(2,1)S(1)} %pad_maximum_fusion.3), channel_id=1, source_target_pairs={{0,8},{4,12},{8,16},{12,20},{16,24},{20,28},{24,32},{28,36},{32,40... | collective-permute-start | bytes 258056 | tf_op jit(solution)/shard_map/ppermute | solution.py:25
  163.5 5.6 %collective-permute-start.12 = (f32[3,56,128]{2,1,0:T(8,128)S(1)}, f32[3,56,128]{2,1,0:T(8,128)S(1)}, u32[]{:S(2)}, u32[]{:S(2)}) collective-permute-start(f32[3,56,128]{2,1,0:T(8,128)S(1)} %get-tuple-element.45), channel_id=1, source_target_pairs={{0,240},{4,244},{8,248},{12,252},{16,0},{20,4},{24,8},{28,12},{32,... | collective-permute-start | bytes 258056 | tf_op jit(solution)/shard_map/ppermute | solution.py:25
  166.1 9.6 %collective-permute-start.13 = (f32[3,56,128]{2,1,0:T(8,128)S(1)}, f32[3,56,128]{2,1,0:T(8,128)S(1)}, u32[]{:S(2)}, u32[]{:S(2)}) collective-permute-start(f32[3,56,128]{2,1,0:T(8,128)S(1)} %get-tuple-element.46), channel_id=1, source_target_pairs={{0,16},{4,20},{8,24},{12,28},{16,32},{20,36},{24,40},{28,44},{32,4... | collective-permute-start | bytes 258056 | tf_op jit(solution)/shard_map/ppermute | solution.py:25
Sparse Core Ops, SparseCore 0:
  64.0 40.3 all-gather.2

commit v3 on v2

--- a/solution.py
+++ b/solution.py
@@ -15,9 +15,10 @@
 TOTAL = WIN * PAIRS
 CHUNK = 16
 SLOTS = 22
-CHUNKS = (TOTAL + SLOTS * (CHUNK - 1)) // CHUNK // 2 * 2 + 2
+UNROLL = 4
+CHUNKS = (TOTAL + SLOTS * (CHUNK - 1)) // CHUNK // UNROLL * UNROLL + UNROLL
 MSG = 112
-VMEM_LIMIT = 36 * 2**20
+VMEM_LIMIT = 50 * 2**20
 
 
 def from_behind(x, axis, by):
@@ -29,18 +30,18 @@
     return jnp.where(mask, first, pltpu.roll(second, 4, 0))
 
 
-def density_kernel(count, ends, steps, *refs):
+def density_kernel(count, rest, steps, *refs):
     pair_refs = refs[:count]
     zv_ref, zc_ref = refs[count : count + 2]
-    mv_ref, mc_ref, left, right, va, ca, vb, cb = refs[-8:]
+    mv_ref, mc_ref, slots_ref, left, right, va, ca, vb, cb = refs[-9:]
     step = pl.program_id(0)
     low = lax.broadcasted_iota(jnp.int32, (8, 1024), 0) < 4
 
     def produce(chunk, v_buf, c_buf):
         block = chunk // 3
         jh = chunk % 3
-        if ends:
-            block = block + jnp.where(block >= 2, 4, 0)
+        if rest:
+            block = block + jnp.where(block >= 4, 2, 0)
         for cv, buf in ((0, v_buf), (1, c_buf)):
             for jl in range(2):
                 point = block * KB + 2 * jh + jl
@@ -98,6 +99,9 @@
     @pl.when(step == 0)
     def _():
         for b in range(2 * count):
+            if b < WIN:
+                tail = pair_refs[b // 2][b % 2, 96:112, 0:128].astype(f32)
+                slots_ref[b : b + 1, :] = tail[0:1].astype(jnp.int32)
             for j in range(KB):
                 x = pair_refs[b // 2][b % 2, 16 * j : 16 * j + 16, :].astype(f32)
                 left[b * KB + j] = x
@@ -118,7 +122,7 @@
     drain(consume(1, vb, cb), produce(jnp.minimum(2 * step + 2, 2 * steps - 1), va, ca))
 
 
-def densities(pairs, ends, zv, zc, previous):
+def densities(pairs, rest, zv, zc, previous):
     whole = lambda shape: pl.BlockSpec(shape, lambda n: (0,) * len(shape), pipeline_mode=pl.Buffered(1))
     operands = list(pairs) + [zv, zc]
     in_specs = [whole(x.shape) for x in operands]
@@ -128,18 +132,23 @@
         in_specs += [pl.BlockSpec(memory_space=pl.ANY)] * 2
         operands += list(previous)
     count = len(pairs)
-    steps = 6
-    place = (lambda n: (n + jnp.where(n >= 3, 6, 0), 0, 0)) if ends else (lambda n: (3 + n, 0, 0))
+    steps = 9 if rest else 3
+    place = (lambda n: (n + jnp.where(n >= 6, 3, 0), 0, 0)) if rest else (lambda n: (6 + n, 0, 0))
     wv = zv.shape[1]
     wc = zc.shape[1]
     return pl.pallas_call(
-        functools.partial(density_kernel, count, ends, steps),
+        functools.partial(density_kernel, count, rest, steps),
         grid=(steps,),
         in_specs=in_specs,
-        out_specs=[pl.BlockSpec((48, 16, wv), place), pl.BlockSpec((48, 16, wc), place)],
+        out_specs=[
+            pl.BlockSpec((48, 16, wv), place),
+            pl.BlockSpec((48, 16, wc), place),
+            pl.BlockSpec((min(2 * count, WIN), 128), lambda n: (0, 0)),
+        ],
         out_shape=[
             jax.ShapeDtypeStruct((TOTAL, 16, wv), bf16),
             jax.ShapeDtypeStruct((TOTAL, 16, wc), bf16),
+            jax.ShapeDtypeStruct((min(2 * count, WIN), 128), jnp.int32),
         ],
         scratch_shapes=[
             pltpu.VMEM((2 * count * KB, 16, 1024), f32),
@@ -150,7 +159,7 @@
             pltpu.VMEM((384, 2048), bf16),
         ],
         input_output_aliases=aliases,
-        compiler_params=pltpu.CompilerParams(vmem_limit_bytes=28 * 2**20),
+        compiler_params=pltpu.CompilerParams(vmem_limit_bytes=VMEM_LIMIT),
         cost_estimate=pl.CostEstimate(
             flops=2 * steps * 48 * 16 * 2048 * (wv + wc), bytes_accessed=steps * 3 * 2**20, transcendentals=0
         ),
@@ -166,7 +175,11 @@
     return own, mirror
 
 
-def apply_kernel(order_ref, slot_ref, used_ref, ga_ref, mv_ref, mc_ref, w_ref, out_ref, rhs, xv):
+def apply_kernel(order_ref, slot_ref, used_ref, ga_ref, mv_hbm, mc_hbm, w_ref, out_ref, rhs, xv, mv_ref, mc_ref, done):
+    fetch_v = pltpu.make_async_copy(mv_hbm, mv_ref, done.at[0])
+    fetch_c = pltpu.make_async_copy(mc_hbm, mc_ref, done.at[1])
+    fetch_v.start()
+    fetch_c.start()
     ga = ga_ref[0]
     lane_group = lax.broadcasted_iota(jnp.int32, (16, 128), 1) >> 5
     spots = [(((q & 1) ^ (ga & 1)) << 1) | ((q >> 1) ^ (ga >> 1)) for q in range(4)]
@@ -183,11 +196,12 @@
         return carry
 
     lax.fori_loop(0, SLOTS, build, 0)
+    fetch_v.wait()
 
     def chunk(q, carry):
-        for u in range(2):
-            slot = slot_ref[2 * q + u]
-            ids = [order_ref[(2 * q + u) * CHUNK + i] for i in range(CHUNK)]
+        for u in range(UNROLL):
+            slot = slot_ref[UNROLL * q + u]
+            ids = [order_ref[(UNROLL * q + u) * CHUNK + i] for i in range(CHUNK)]
             sources = [jnp.minimum(i, TOTAL - 1) for i in ids]
             lhs = jnp.concatenate([mv_ref[s] for s in sources], axis=0)
             res = jnp.dot(lhs, rhs[slot], preferred_element_type=f32).astype(bf16)
@@ -195,7 +209,8 @@
                 xv[ids[i]] = res[16 * i : 16 * i + 16]
         return carry
 
-    lax.fori_loop(0, (used_ref[0] + 1) >> 1, chunk, 0)
+    lax.fori_loop(0, (used_ref[0] + UNROLL - 1) >> 2, chunk, 0)
+    fetch_c.wait()
 
     def contract(t, carry):
         for jh in range(3):
@@ -238,12 +253,15 @@
     vmem = pl.BlockSpec(memory_space=pltpu.VMEM)
     return pl.pallas_call(
         apply_kernel,
-        in_specs=[smem] * 4 + [vmem] * 3,
+        in_specs=[smem] * 4 + [pl.BlockSpec(memory_space=pl.ANY)] * 2 + [vmem],
         out_specs=vmem,
         out_shape=jax.ShapeDtypeStruct((4, WIN, 3, 56, 128), f32),
         scratch_shapes=[
             pltpu.VMEM((SLOTS, 512, 256), bf16),
             pltpu.VMEM((TOTAL + 1, 16, 256), bf16),
+            pltpu.VMEM(mv.shape, bf16),
+            pltpu.VMEM(mc.shape, bf16),
+            pltpu.SemaphoreType.DMA((2,)),
         ],
         compiler_params=pltpu.CompilerParams(vmem_limit_bytes=VMEM_LIMIT),
         cost_estimate=pl.CostEstimate(flops=6 * 10**9, bytes_accessed=18 * 2**20, transcendentals=0),
@@ -329,52 +347,44 @@
     tail = jnp.pad(slots.astype(bf16), ((0, 15), (0, 1024 - PAIRS)))
     message = jnp.concatenate([bloch_samples.reshape(96, 1024), tail], axis=0)
     following = from_behind(message, "ka", -1)
+    here = jnp.stack([message, following])
+    ahead = from_behind(here, "ka", -2)
+    behind = from_behind(here, "ka", 2)
     zv = zeta_matrix(zeta_vectors)
     mine = lax.dynamic_slice_in_dim(zeta_vectors, 128 * lax.rem(part, 2), 128, 2)
-    mine, following = lax.optimization_barrier((mine, following))
-    holders = [(k, (k % WIN) // 2) for k in range(ka_count)]
-    over = lax.ppermute(mine, ("ka", "ga"), [(4 * k + h, 4 * k + (h ^ 2)) for k, h in holders])
+    halves = lax.all_gather(mine, "ga")
+    zc = zeta_matrix(lax.dynamic_index_in_dim(halves, part // 2, 0, keepdims=False))
     pieces = jnp.transpose(screened.reshape(SLOTS, 2, 4, WIN, 128), (3, 0, 1, 2, 4))
     pieces = jnp.concatenate([pieces, pieces], axis=0)
-    pieces, following = lax.optimization_barrier((pieces, following))
+    pieces = pieces + following[0, 0] * 0
     line = 2 * WIN
     near_groups = [[x * line + s for s in range(line)] for x in range(ka_count // line)]
     x_groups = [[x * line + s for x in range(ka_count // line)] for s in range(line)]
     pieces = lax.all_to_all(pieces, "ka", 0, 0, axis_index_groups=near_groups, tiled=True)
+    mv, mc, word = densities((here, ahead), False, zv, zc, None)
     rows = jnp.transpose(pieces, (1, 2, 0, 3, 4)).reshape(SLOTS, 2, 4 * line, 128)
-    held = jnp.where(ga == part // 2, mine, over)
-    moves = [(4 * k + h, 4 * k + (h ^ 1)) for k, h in holders]
-    moves += [(4 * k + (h ^ 2), 4 * k + (h ^ 3)) for k, h in holders]
-    zc = zeta_matrix(held + lax.ppermute(held, ("ka", "ga"), moves))
-    here = jnp.stack([message, following])
-    ahead = from_behind(here, "ka", -2)
-    behind = from_behind(here, "ka", 2)
-    rows, ahead, behind, zv = lax.optimization_barrier((rows, ahead, behind, zv))
+    rows = rows + jnp.minimum(word[0, 0], 0).astype(bf16)
     w = lax.all_gather(rows, "ka", axis_index_groups=x_groups)
     ahead2 = from_behind(ahead, "ka", -2)
     behind2 = from_behind(behind, "ka", 2)
-    made = densities((behind, here, ahead), False, zv, zc, None)
-    made = densities((behind2, behind, here, ahead, ahead2), True, zv, zc, made)
-    mv, mc, *pairs = lax.optimization_barrier((*made, behind2, behind, here, ahead))
-    all_slots = jnp.concatenate([x[:, 96, :PAIRS] for x in pairs], axis=0).reshape(TOTAL)
-    order, slot_of, used = schedule(all_slots.astype(jnp.int32))
+    mv, mc, words = densities((behind2, behind, here, ahead, ahead2), True, zv, zc, (mv, mc))
+    order, slot_of, used = schedule(words[:, :PAIRS].reshape(TOTAL))
     partial = apply_screened(order, slot_of, used, ga_word, mv, mc, w)
     arrived = lax.ppermute(partial[2:].astype(bf16), "ga", [(0, 1), (1, 0), (2, 3), (3, 2)])
-    own = partial[0] + arrived[0].astype(f32)
-    other = (partial[1] + arrived[1].astype(f32)).astype(bf16)
-    own = own + lax.ppermute(other, "ga", [(0, 2), (2, 0), (1, 3), (3, 1)]).astype(f32)
-    first_offset = ((lax.broadcasted_iota(jnp.int32, (1, 1, 1, 128), 3) >> 5) & 1) == 0
-    spread = lambda x, before, after: jnp.pad(x, ((before, after), (0, 0), (0, 0), (0, 0)))
-    mirror = jnp.where(first_offset, spread(own[:, :, 24:], 1, 1), spread(own[:, :, 24:], 2, 0))
-    parts = jnp.concatenate([spread(own[:, :, :24], 0, 2), mirror], axis=2)
-    send = lambda picks, by: from_behind(jnp.stack([parts[d] for d in picks]).astype(bf16), "ka", by).astype(f32)
+    both = partial[:2] + arrived.astype(f32)
+    first_offset = ((lax.broadcasted_iota(jnp.int32, (1, 1, 1, 1, 128), 4) >> 5) & 1) == 0
+    spread = lambda x, before, after: jnp.pad(x, ((0, 0), (before, after), (0, 0), (0, 0), (0, 0)))
+    mirror = jnp.where(first_offset, spread(both[:, :, :, 24:], 1, 1), spread(both[:, :, :, 24:], 2, 0))
+    parts = jnp.concatenate([spread(both[:, :, :, :24], 0, 2), mirror], axis=3)
+    send = lambda picks, by: from_behind(jnp.stack([parts[:, d] for d in picks]).astype(bf16), "ka", by).astype(f32)
     plus_one = send((1, 5, 9), 1)
     plus_two = send((2, 6), 2)
     minus_one = send((3, 7), -1)
-    low = parts[0] + plus_one[0] + plus_two[0]
-    high = parts[8] + plus_one[2] + minus_one[1]
-    total = parts[4] + plus_one[1] + plus_two[1] + minus_one[0]
+    low = parts[:, 0] + plus_one[0] + plus_two[0]
+    high = parts[:, 8] + plus_one[2] + minus_one[1]
+    total = parts[:, 4] + plus_one[1] + plus_two[1] + minus_one[0]
     total = total + from_behind(low, "ka", -4) + from_behind(high, "ka", 4)
+    total = total[0] + lax.ppermute(total[1], "ga", [(0, 2), (2, 0), (1, 3), (3, 1)])
     return arrange(ga_word, total)
 
 

time: 186 us -> 183 us (0.984)
  local copies, waits for them, and re-layouts: 21.6 us -> 11.3 us
  waiting for transfers between devices: 51 us -> 53.8 us
  other arithmetic: 6.46 us -> 8.58 us
    ppermute x10, waiting for transfers between devices: 30.5 us -> 43.2 us  [from_behind(): return lax.ppermute(x, axis, [(i, (i + by) % count) for i in range(count)])]
    unnamed x19 -> x7, local copies, waits for them, and re-layouts: 10.9 us -> 0.22 us
    ppermute x10, starting transfers between devices: 12.8 us -> 19.2 us  [from_behind(): return lax.ppermute(x, axis, [(i, (i + by) % count) for i in range(count)])]
    all_to_all x1, waiting for transfers between devices: 9.98 us -> 4.11 us  [body(): lax.all_to_all(pieces, 'ka', 0, 0, axis_index_groups=near_groups, tiled=T...]
    ppermute x3 -> x1, waiting for transfers between devices: 8.36 us -> 3.73 us  [body(): lax.ppermute(total[1], 'ga', [(0, 2), (2, 0), (1, 3), (3, 1)])]
    ppermute x3 -> x1, starting transfers between devices: 6.48 us -> 2.35 us  [body(): lax.ppermute(total[1], 'ga', [(0, 2), (2, 0), (1, 3), (3, 1)])]
    add x0 -> x2, local copies, waits for them, and re-layouts: none -> 2.43 us  [the longest x1 1.26 us: body(): rows = rows + jnp.minimum(word[0, 0], 0).astype(bf16)]
    transpose x1 -> x0, local copies, waits for them, and re-layouts: 2.37 us -> none  [body(): jnp.transpose(pieces, (1, 2, 0, 3, 4)).reshape(SLOTS, 2, 4 * line, 128)]
  transfers between devices with their start and end apart: 16 -> 15, of which waited for: 9 -> 10; matrix products, arithmetic and copies ran while one was open for 8% -> 9% of each run, Pallas kernels for 21% -> 23%
where the time goes in v3:
time: 183 us; the launch traced here: 182 us
  Pallas kernels  59.3 us (32%)
  waiting for transfers between devices  53.8 us (29%)
  starting transfers between devices  34.1 us (19%)
  between operations  15 us (8%)
  local copies, waits for them, and re-layouts  11.3 us (6%)
  other arithmetic  8.58 us (5%)
    ppermute x10, waiting for transfers between devices, from_behind(): return lax.ppermute(x, axis, [(i, (i + by) % count) for i in range(count)])  43.2 us
    pallas_call x2, Pallas kernels, densities(): pl.pallas_call(functools.partial(density_kernel, count, rest, steps), gri...  41.3 us
    ppermute x10, starting transfers between devices, from_behind(): return lax.ppermute(x, axis, [(i, (i + by) % count) for i in range(count)])  19.2 us
    pallas_call x1, Pallas kernels, apply_screened(): pl.pallas_call(apply_kernel, in_specs=[smem] * 4 + [pl.BlockSpec(memory_s...  16.3 us
    all_to_all x1, starting transfers between devices, body(): lax.all_to_all(pieces, 'ka', 0, 0, axis_index_groups=near_groups, tiled=T...  12.4 us
    all_to_all x1, waiting for transfers between devices, body(): lax.all_to_all(pieces, 'ka', 0, 0, axis_index_groups=near_groups, tiled=T...  4.11 us
    ppermute x1, waiting for transfers between devices, body(): lax.ppermute(total[1], 'ga', [(0, 2), (2, 0), (1, 3), (3, 1)])  3.73 us
  transfers between devices with their start and end apart: 15, of which 10 were waited for; matrix products, arithmetic and copies ran while one was open for 9% of the time, Pallas kernels for 23%

profile of v3, /device:TPU:40, one launch (start us, length us, event | category | flops | bytes accessed | tf_op | source)
XLA Modules:
  0.0 182.1 jit_solution(8607091702650287907)
XLA Ops:
  6.5 2.3 %constant_dynamic-slice_fusion.1 = bf16[1024,2,128]{2,1,0:T(2,128)(2,1)} fusion(bf16[1024,2,256]{2,1,0:T(2,128)(2,1)} %param.5, s32[]{:T(128)S(6)} %select_n.41), kind=kLoop, calls=%fused_computation.71 | loop fusion | bytes 1048580 | tf_op jit(solution)/shard_map/dynamic_slice | solution.py:354
  8.9 0.7 convert_element_type.59
  9.8 1.7 fusion.14
  11.9 1.5 fusion.18
  13.5 1.1 reshape.111
  14.9 5.1 %collective-permute-done = bf16[112,1024]{1,0:T(8,128)(2,1)} collective-permute-done((bf16[112,1024]{1,0:T(8,128)(2,1)}, bf16[112,1024]{1,0:T(8,128)(2,1)}, u32[]{:S(2)}, u32[]{:S(2)}) %collective-permute-start) | collective-permute-done | bytes 229408 | tf_op jit(solution)/shard_map/ppermute | solution.py:26
  20.0 1.7 pad_maximum_fusion.refs_0_.refs_2_
  21.9 1.9 %collective-permute-start.1 = (bf16[2,112,1024]{2,1,0:T(8,128)(2,1)}, bf16[2,112,1024]{2,1,0:T(8,128)(2,1)}, u32[]{:S(2)}, u32[]{:S(2)}) collective-permute-start(bf16[2,112,1024]{2,1,0:T(8,128)(2,1)} %pad_maximum_fusion.refs_0_.refs_2_), channel_id=1, source_target_pairs={{0,8},{4,12},{8,16},{12,20},{16,24},{20,28},{24,32},{28,36},{32,40... | collective-permute-start | bytes 1376264 | tf_op jit(solution)/shard_map/ppermute | solution.py:26
  23.8 1.2 slice.131
  25.9 1.2 copy.39
  27.0 12.4 %all-to-all-start = ((bf16[16,22,2,4,128]{4,3,2,1,0:T(4,128)(2,1)}), bf16[16,22,2,4,128]{4,3,2,1,0:T(4,128)(2,1)}, u32[]{:S(2)}, u32[]{:S(2)}) async-start(bf16[16,22,2,4,128]{4,3,2,1,0:T(4,128)(2,1)} %copy.39), calls=%async_computation | async-start | bytes 1441792 | tf_op jit(solution)/shard_map/all_to_all | solution.py:363
  39.5 0.5 all-gather.6.cloned.1.call-done
  40.0 1.4 constant_dynamic-slice_fusion
  41.7 11.5 %densities.2 = (bf16[576,16,512]{2,1,0:T(8,128)(2,1)}, bf16[576,16,256]{2,1,0:T(8,128)(2,1)}, s32[4,128]{1,0:T(4,128)S(1)}) custom-call(bf16[2,112,1024]{2,1,0:T(8,128)(2,1)} %pad_maximum_fusion.refs_0_.refs_2_, bf16[2,112,1024]{2,1,0:T(8,128)(2,1)} %collective-permute-done.3.refs_1_.refs_3_, bf16[2048,512]{1,0:T(8,128)(2,1)S(1)} %maximum_maximum_fusion.refs_2_.refs_5_, ...), custom_call_target="tpu_custom_call" | custom-call | flops 7247757312 | bytes 9437184 | tf_op jit(solution)/shard_map/densities/pallas_call | solution.py:139
  54.4 4.1 %all-to-all-done = bf16[16,22,2,4,128]{4,3,2,1,0:T(4,128)(2,1)} async-done(((bf16[16,22,2,4,128]{4,3,2,1,0:T(4,128)(2,1)}), bf16[16,22,2,4,128]{4,3,2,1,0:T(4,128)(2,1)}, u32[]{:S(2)}, u32[]{:S(2)}) %all-to-all-start) | async-done | bytes 720928 | tf_op jit(solution)/shard_map/all_to_all | solution.py:363
  58.5 1.4 add_bitcast_fusion
  59.9 1.3 copy.40
  61.2 7.3 %collective-permute-start.4 = (bf16[2,112,1024]{2,1,0:T(8,128)(2,1)}, bf16[2,112,1024]{2,1,0:T(8,128)(2,1)S(1)}, u32[]{:S(2)}, u32[]{:S(2)}) collective-permute-start(bf16[2,112,1024]{2,1,0:T(8,128)(2,1)} %collective-permute-done.3.refs_1_.refs_3_), channel_id=1, source_target_pairs={{0,248},{4,252},{8,0},{12,4},{16,8},{20,12},{24,16},{28,20},{32,24... | collective-permute-start | bytes 1376264 | tf_op jit(solution)/shard_map/ppermute | solution.py:26
  68.5 6.3 %collective-permute-done.4.refs_4_ = bf16[2,112,1024]{2,1,0:T(8,128)(2,1)S(1)} collective-permute-done((bf16[2,112,1024]{2,1,0:T(8,128)(2,1)}, bf16[2,112,1024]{2,1,0:T(8,128)(2,1)S(1)}, u32[]{:S(2)}, u32[]{:S(2)}) %collective-permute-start.4) | collective-permute-done | bytes 458784 | tf_op jit(solution)/shard_map/ppermute | solution.py:26
  74.8 7.3 %collective-permute-done.2.refs_0_ = bf16[2,112,1024]{2,1,0:T(8,128)(2,1)S(1)} collective-permute-done((bf16[2,112,1024]{2,1,0:T(8,128)(2,1)}, bf16[2,112,1024]{2,1,0:T(8,128)(2,1)S(1)}, u32[]{:S(2)}, u32[]{:S(2)}) %collective-permute-start.2) | collective-permute-done | bytes 458784 | tf_op jit(solution)/shard_map/ppermute | solution.py:26
  82.1 29.8 %densities.3 = (bf16[576,16,512]{2,1,0:T(8,128)(2,1)}, bf16[576,16,256]{2,1,0:T(8,128)(2,1)}, s32[8,128]{1,0:T(8,128)S(1)}) custom-call(bf16[2,112,1024]{2,1,0:T(8,128)(2,1)S(1)} %collective-permute-done.2.refs_0_, bf16[2,112,1024]{2,1,0:T(8,128)(2,1)} %collective-permute-done.1.refs_1_, ...), custom_call_target="tpu_custom_call", output_to_operand_aliasing={{0}: (7, {}), {1}: (8, {})} | custom-call | flops 21743271936 | bytes 28311552 | tf_op jit(solution)/shard_map/densities/pallas_call | solution.py:139
  112.1 0.6 fusion.16
  113.7 16.3 %apply_screened.1 = f32[4,8,3,56,128]{4,3,2,1,0:T(8,128)S(1)} custom-call(s32[960]{0:T(1024)S(1)} %broadcast_add_fusion.order_ref, s32[60]{0:T(128)S(1)} %broadcast_minimum_fusion.slot_ref, s32[1]{0:T(128)} %bitcast.12.used_ref, s32[1]{0:T(128)} %bitcast.ga_ref, bf16[576,16,512]{2,1,0:T(8,128)(2,1)} %get-tuple-element.14.mv_hbm, ...), custom_call_target="tpu_custom_call" | custom-call | flops 6000000000 | bytes 18874368 | tf_op jit(solution)/shard_map/apply_screened/pallas_call | solution.py:254
  130.3 2.1 %collective-permute-done.5 = bf16[2,8,3,56,128]{4,3,2,0,1:T(8,128)(2,1)S(1)} collective-permute-done((bf16[2,8,3,56,128]{4,3,2,0,1:T(8,128)(2,1)S(1)}, bf16[2,8,3,56,128]{4,3,2,0,1:T(8,128)(2,1)S(1)}, u32[]{:S(2)}, u32[]{:S(2)}) %collective-permute-start.5) | collective-permute-done | bytes 688160 | tf_op jit(solution)/shard_map/ppermute | solution.py:373
  133.2 3.0 %collective-permute-start.6 = (bf16[3,2,3,56,128]{4,3,2,1,0:T(8,128)(2,1)S(1)}, bf16[3,2,3,56,128]{4,3,2,1,0:T(8,128)(2,1)S(1)}, u32[]{:S(2)}, u32[]{:S(2)}) collective-permute-start(bf16[3,2,3,56,128]{4,3,2,1,0:T(8,128)(2,1)S(1)} %pad_maximum_fusion.1), channel_id=1, source_target_pairs={{0,4},{4,8},{8,12},{12,16},{16,20},{20,24},{24,28},{28,32},{32,36}... | collective-permute-start | bytes 774152 | tf_op jit(solution)/shard_map/ppermute | solution.py:26
  136.4 4.0 %collective-permute-done.8 = bf16[2,2,3,56,128]{4,3,2,1,0:T(8,128)(2,1)S(1)} collective-permute-done((bf16[2,2,3,56,128]{4,3,2,1,0:T(8,128)(2,1)S(1)}, bf16[2,2,3,56,128]{4,3,2,1,0:T(8,128)(2,1)S(1)}, u32[]{:S(2)}, u32[]{:S(2)}) %collective-permute-start.8) | collective-permute-done | bytes 172064 | tf_op jit(solution)/shard_map/ppermute | solution.py:26
  140.4 14.7 %collective-permute-done.7 = bf16[2,2,3,56,128]{4,3,2,1,0:T(8,128)(2,1)S(1)} collective-permute-done((bf16[2,2,3,56,128]{4,3,2,1,0:T(8,128)(2,1)S(1)}, bf16[2,2,3,56,128]{4,3,2,1,0:T(8,128)(2,1)S(1)}, u32[]{:S(2)}, u32[]{:S(2)}) %collective-permute-start.7) | collective-permute-done | bytes 172064 | tf_op jit(solution)/shard_map/ppermute | solution.py:26
  155.4 6.2 %collective-permute-start.9 = (f32[2,3,56,128]{3,2,1,0:T(8,128)S(1)}, f32[2,3,56,128]{3,2,1,0:T(8,128)S(1)}, u32[]{:S(2)}, u32[]{:S(2)}) collective-permute-start(f32[2,3,56,128]{3,2,1,0:T(8,128)S(1)} %get-tuple-element.21), channel_id=1, source_target_pairs={{0,240},{4,244},{8,248},{12,252},{16,0},{20,4},{24,8},{28,12},{32,... | collective-permute-start | bytes 516104 | tf_op jit(solution)/shard_map/ppermute | solution.py:26
  161.6 5.8 %collective-permute-done.10 = f32[2,3,56,128]{3,2,1,0:T(8,128)S(1)} collective-permute-done((f32[2,3,56,128]{3,2,1,0:T(8,128)S(1)}, f32[2,3,56,128]{3,2,1,0:T(8,128)S(1)}, u32[]{:S(2)}, u32[]{:S(2)}) %collective-permute-start.10) | collective-permute-done | bytes 172064 | tf_op jit(solution)/shard_map/ppermute | solution.py:26
  167.5 2.3 %collective-permute-start.11 = (f32[3,56,128]{2,1,0:T(8,128)S(1)}, f32[3,56,128]{2,1,0:T(8,128)S(1)}, u32[]{:S(2)}, u32[]{:S(2)}) collective-permute-start(f32[3,56,128]{2,1,0:T(8,128)S(1)} %slice_bitcast_fusion.12), channel_id=1, source_target_pairs={{0,2},{2,0},{1,3},{3,1},{4,6},{6,4},{5,7},{7,5},{8,10},{10,8},{9,1... | collective-permute-start | bytes 258056 | tf_op jit(solution)/shard_map/ppermute | solution.py:387
  169.8 3.7 %collective-permute-done.11 = f32[3,56,128]{2,1,0:T(8,128)S(1)} collective-permute-done((f32[3,56,128]{2,1,0:T(8,128)S(1)}, f32[3,56,128]{2,1,0:T(8,128)S(1)}, u32[]{:S(2)}, u32[]{:S(2)}) %collective-permute-start.11) | collective-permute-done | bytes 86048 | tf_op jit(solution)/shard_map/ppermute | solution.py:387
  173.6 1.7 arrange.1
  (62 shorter events, 4.8 us)
Async XLA Ops:
  6.5 5.4 %copy-start.1 = (bf16[1024,2,256]{2,1,0:T(2,128)(2,1)S(1)}, bf16[1024,2,256]{2,1,0:T(2,128)(2,1)}, u32[]{:S(2)}) copy-start(bf16[1024,2,256]{2,1,0:T(2,128)(2,1)} %param.5) | copy-start | bytes 3145732
  6.5 33.5 %all-gather.6.cloned.1.call-start = ((), (), s32[]{:S(2)}) async-start(), calls=%async_computation.2 | async-start | bytes 2621440 | tf_op jit(solution)/shard_map/all_gather | solution.py:355
  11.5 8.6 %collective-permute-start = (bf16[112,1024]{1,0:T(8,128)(2,1)}, bf16[112,1024]{1,0:T(8,128)(2,1)}, u32[]{:S(2)}, u32[]{:S(2)}) collective-permute-start(bf16[112,1024]{1,0:T(8,128)(2,1)} %get-tuple-element.35), channel_id=1, source_target_pairs={{0,252},{4,0},{8,4},{12,8},{16,12},{20,16},{24,20},{28,24},{32,28}... | collective-permute-start | bytes 688136 | tf_op jit(solution)/shard_map/ppermute | solution.py:26
  14.9 26.8 %copy-start = (bf16[2048,512]{1,0:T(8,128)(2,1)}, bf16[2048,512]{1,0:T(8,128)(2,1)S(1)}, u32[]{:S(2)}) copy-start(bf16[2048,512]{1,0:T(8,128)(2,1)S(1)} %maximum_maximum_fusion.refs_2_.refs_5_) | copy-start | bytes 6291460
  21.8 19.9 %collective-permute-start.3 = (bf16[2,112,1024]{2,1,0:T(8,128)(2,1)}, bf16[2,112,1024]{2,1,0:T(8,128)(2,1)}, u32[]{:S(2)}, u32[]{:S(2)}) collective-permute-start(bf16[2,112,1024]{2,1,0:T(8,128)(2,1)} %pad_maximum_fusion.refs_0_.refs_2_), channel_id=1, source_target_pairs={{0,248},{4,252},{8,0},{12,4},{16,8},{20,12},{24,16},{28,20},{32,24... | collective-permute-start | bytes 1376264 | tf_op jit(solution)/shard_map/ppermute | solution.py:26
  21.9 46.6 %collective-permute-start.1 = (bf16[2,112,1024]{2,1,0:T(8,128)(2,1)}, bf16[2,112,1024]{2,1,0:T(8,128)(2,1)}, u32[]{:S(2)}, u32[]{:S(2)}) collective-permute-start(bf16[2,112,1024]{2,1,0:T(8,128)(2,1)} %pad_maximum_fusion.refs_0_.refs_2_), channel_id=1, source_target_pairs={{0,8},{4,12},{8,16},{12,20},{16,24},{20,28},{24,32},{28,36},{32,40... | collective-permute-start | bytes 1376264 | tf_op jit(solution)/shard_map/ppermute | solution.py:26
  27.0 31.5 %all-to-all-start = ((bf16[16,22,2,4,128]{4,3,2,1,0:T(4,128)(2,1)}), bf16[16,22,2,4,128]{4,3,2,1,0:T(4,128)(2,1)}, u32[]{:S(2)}, u32[]{:S(2)}) async-start(bf16[16,22,2,4,128]{4,3,2,1,0:T(4,128)(2,1)} %copy.39), calls=%async_computation | async-start | bytes 1441792 | tf_op jit(solution)/shard_map/all_to_all | solution.py:363
  39.4 74.2 %all-gather.4.cloned.1.call-start = ((), (), s32[]{:S(2)}) async-start(), calls=%async_computation.1 | async-start | bytes 3604480 | tf_op jit(solution)/shard_map/all_gather | solution.py:367
  61.2 13.6 %collective-permute-start.4 = (bf16[2,112,1024]{2,1,0:T(8,128)(2,1)}, bf16[2,112,1024]{2,1,0:T(8,128)(2,1)S(1)}, u32[]{:S(2)}, u32[]{:S(2)}) collective-permute-start(bf16[2,112,1024]{2,1,0:T(8,128)(2,1)} %collective-permute-done.3.refs_1_.refs_3_), channel_id=1, source_target_pairs={{0,248},{4,252},{8,0},{12,4},{16,8},{20,12},{24,16},{28,20},{32,24... | collective-permute-start | bytes 1376264 | tf_op jit(solution)/shard_map/ppermute | solution.py:26
  68.5 13.6 %collective-permute-start.2 = (bf16[2,112,1024]{2,1,0:T(8,128)(2,1)}, bf16[2,112,1024]{2,1,0:T(8,128)(2,1)S(1)}, u32[]{:S(2)}, u32[]{:S(2)}) collective-permute-start(bf16[2,112,1024]{2,1,0:T(8,128)(2,1)} %collective-permute-done.1.refs_1_), channel_id=1, source_target_pairs={{0,8},{4,12},{8,16},{12,20},{16,24},{20,28},{24,32},{28,36},{32,40... | collective-permute-start | bytes 1376264 | tf_op jit(solution)/shard_map/ppermute | solution.py:26
  130.2 2.2 %collective-permute-start.5 = (bf16[2,8,3,56,128]{4,3,2,0,1:T(8,128)(2,1)S(1)}, bf16[2,8,3,56,128]{4,3,2,0,1:T(8,128)(2,1)S(1)}, u32[]{:S(2)}, u32[]{:S(2)}) collective-permute-start(bf16[2,8,3,56,128]{4,3,2,0,1:T(8,128)(2,1)S(1)} %copy.53), channel_id=1, source_target_pairs={{0,1},{1,0},{2,3},{3,2},{4,5},{5,4},{6,7},{7,6},{8,9},{9,8},{10,11... | collective-permute-start | bytes 2064392 | tf_op jit(solution)/shard_map/ppermute | solution.py:373
  133.0 7.4 %collective-permute-start.8 = (bf16[2,2,3,56,128]{4,3,2,1,0:T(8,128)(2,1)S(1)}, bf16[2,2,3,56,128]{4,3,2,1,0:T(8,128)(2,1)S(1)}, u32[]{:S(2)}, u32[]{:S(2)}) collective-permute-start(bf16[2,2,3,56,128]{4,3,2,1,0:T(8,128)(2,1)S(1)} %pad_maximum_fusion.3), channel_id=1, source_target_pairs={{0,252},{4,0},{8,4},{12,8},{16,12},{20,16},{24,20},{28,24},{32,28}... | collective-permute-start | bytes 516104 | tf_op jit(solution)/shard_map/ppermute | solution.py:26
  133.2 22.0 %collective-permute-start.6 = (bf16[3,2,3,56,128]{4,3,2,1,0:T(8,128)(2,1)S(1)}, bf16[3,2,3,56,128]{4,3,2,1,0:T(8,128)(2,1)S(1)}, u32[]{:S(2)}, u32[]{:S(2)}) collective-permute-start(bf16[3,2,3,56,128]{4,3,2,1,0:T(8,128)(2,1)S(1)} %pad_maximum_fusion.1), channel_id=1, source_target_pairs={{0,4},{4,8},{8,12},{12,16},{16,20},{20,24},{24,28},{28,32},{32,36}... | collective-permute-start | bytes 774152 | tf_op jit(solution)/shard_map/ppermute | solution.py:26
  136.2 19.0 %collective-permute-start.7 = (bf16[2,2,3,56,128]{4,3,2,1,0:T(8,128)(2,1)S(1)}, bf16[2,2,3,56,128]{4,3,2,1,0:T(8,128)(2,1)S(1)}, u32[]{:S(2)}, u32[]{:S(2)}) collective-permute-start(bf16[2,2,3,56,128]{4,3,2,1,0:T(8,128)(2,1)S(1)} %pad_maximum_fusion.2), channel_id=1, source_target_pairs={{0,8},{4,12},{8,16},{12,20},{16,24},{20,28},{24,32},{28,36},{32,40... | collective-permute-start | bytes 516104 | tf_op jit(solution)/shard_map/ppermute | solution.py:26
  155.3 12.1 %collective-permute-start.10 = (f32[2,3,56,128]{3,2,1,0:T(8,128)S(1)}, f32[2,3,56,128]{3,2,1,0:T(8,128)S(1)}, u32[]{:S(2)}, u32[]{:S(2)}) collective-permute-start(f32[2,3,56,128]{3,2,1,0:T(8,128)S(1)} %get-tuple-element.22), channel_id=1, source_target_pairs={{0,16},{4,20},{8,24},{12,28},{16,32},{20,36},{24,40},{28,44},{32,4... | collective-permute-start | bytes 516104 | tf_op jit(solution)/shard_map/ppermute | solution.py:26
  155.4 12.0 %collective-permute-start.9 = (f32[2,3,56,128]{3,2,1,0:T(8,128)S(1)}, f32[2,3,56,128]{3,2,1,0:T(8,128)S(1)}, u32[]{:S(2)}, u32[]{:S(2)}) collective-permute-start(f32[2,3,56,128]{3,2,1,0:T(8,128)S(1)} %get-tuple-element.21), channel_id=1, source_target_pairs={{0,240},{4,244},{8,248},{12,252},{16,0},{20,4},{24,8},{28,12},{32,... | collective-permute-start | bytes 516104 | tf_op jit(solution)/shard_map/ppermute | solution.py:26
  167.5 6.1 %collective-permute-start.11 = (f32[3,56,128]{2,1,0:T(8,128)S(1)}, f32[3,56,128]{2,1,0:T(8,128)S(1)}, u32[]{:S(2)}, u32[]{:S(2)}) collective-permute-start(f32[3,56,128]{2,1,0:T(8,128)S(1)} %slice_bitcast_fusion.12), channel_id=1, source_target_pairs={{0,2},{2,0},{1,3},{3,1},{4,6},{6,4},{5,7},{7,5},{8,10},{10,8},{9,1... | collective-permute-start | bytes 258056 | tf_op jit(solution)/shard_map/ppermute | solution.py:387
Sparse Core Ops, SparseCore 0:
  9.2 30.8 all-gather.5
  61.3 46.6 all-gather.3

commit v4 on v3

--- a/solution.py
+++ b/solution.py
@@ -41,7 +41,7 @@
         block = chunk // 3
         jh = chunk % 3
         if rest:
-            block = block + jnp.where(block >= 4, 2, 0)
+            block = block + jnp.where(block >= 2, 4, 0)
         for cv, buf in ((0, v_buf), (1, c_buf)):
             for jl in range(2):
                 point = block * KB + 2 * jh + jl
@@ -132,8 +132,8 @@
         in_specs += [pl.BlockSpec(memory_space=pl.ANY)] * 2
         operands += list(previous)
     count = len(pairs)
-    steps = 9 if rest else 3
-    place = (lambda n: (n + jnp.where(n >= 6, 3, 0), 0, 0)) if rest else (lambda n: (6 + n, 0, 0))
+    steps = 6
+    place = (lambda n: (n + jnp.where(n >= 3, 6, 0), 0, 0)) if rest else (lambda n: (3 + n, 0, 0))
     wv = zv.shape[1]
     wc = zc.shape[1]
     return pl.pallas_call(
@@ -356,35 +356,34 @@
     zc = zeta_matrix(lax.dynamic_index_in_dim(halves, part // 2, 0, keepdims=False))
     pieces = jnp.transpose(screened.reshape(SLOTS, 2, 4, WIN, 128), (3, 0, 1, 2, 4))
     pieces = jnp.concatenate([pieces, pieces], axis=0)
-    pieces = pieces + following[0, 0] * 0
     line = 2 * WIN
     near_groups = [[x * line + s for s in range(line)] for x in range(ka_count // line)]
     x_groups = [[x * line + s for x in range(ka_count // line)] for s in range(line)]
     pieces = lax.all_to_all(pieces, "ka", 0, 0, axis_index_groups=near_groups, tiled=True)
-    mv, mc, word = densities((here, ahead), False, zv, zc, None)
     rows = jnp.transpose(pieces, (1, 2, 0, 3, 4)).reshape(SLOTS, 2, 4 * line, 128)
-    rows = rows + jnp.minimum(word[0, 0], 0).astype(bf16)
     w = lax.all_gather(rows, "ka", axis_index_groups=x_groups)
     ahead2 = from_behind(ahead, "ka", -2)
     behind2 = from_behind(behind, "ka", 2)
+    mv, mc, _ = densities((behind, here, ahead), False, zv, zc, None)
     mv, mc, words = densities((behind2, behind, here, ahead, ahead2), True, zv, zc, (mv, mc))
     order, slot_of, used = schedule(words[:, :PAIRS].reshape(TOTAL))
     partial = apply_screened(order, slot_of, used, ga_word, mv, mc, w)
     arrived = lax.ppermute(partial[2:].astype(bf16), "ga", [(0, 1), (1, 0), (2, 3), (3, 2)])
-    both = partial[:2] + arrived.astype(f32)
-    first_offset = ((lax.broadcasted_iota(jnp.int32, (1, 1, 1, 1, 128), 4) >> 5) & 1) == 0
-    spread = lambda x, before, after: jnp.pad(x, ((0, 0), (before, after), (0, 0), (0, 0), (0, 0)))
-    mirror = jnp.where(first_offset, spread(both[:, :, :, 24:], 1, 1), spread(both[:, :, :, 24:], 2, 0))
-    parts = jnp.concatenate([spread(both[:, :, :, :24], 0, 2), mirror], axis=3)
-    send = lambda picks, by: from_behind(jnp.stack([parts[:, d] for d in picks]).astype(bf16), "ka", by).astype(f32)
+    own = partial[0] + arrived[0].astype(f32)
+    other = (partial[1] + arrived[1].astype(f32)).astype(bf16)
+    own = own + lax.ppermute(other, "ga", [(0, 2), (2, 0), (1, 3), (3, 1)]).astype(f32)
+    first_offset = ((lax.broadcasted_iota(jnp.int32, (1, 1, 1, 128), 3) >> 5) & 1) == 0
+    spread = lambda x, before, after: jnp.pad(x, ((before, after), (0, 0), (0, 0), (0, 0)))
+    mirror = jnp.where(first_offset, spread(own[:, :, 24:], 1, 1), spread(own[:, :, 24:], 2, 0))
+    parts = jnp.concatenate([spread(own[:, :, :24], 0, 2), mirror], axis=2)
+    send = lambda picks, by: from_behind(jnp.stack([parts[d] for d in picks]).astype(bf16), "ka", by).astype(f32)
     plus_one = send((1, 5, 9), 1)
     plus_two = send((2, 6), 2)
     minus_one = send((3, 7), -1)
-    low = parts[:, 0] + plus_one[0] + plus_two[0]
-    high = parts[:, 8] + plus_one[2] + minus_one[1]
-    total = parts[:, 4] + plus_one[1] + plus_two[1] + minus_one[0]
+    low = parts[0] + plus_one[0] + plus_two[0]
+    high = parts[8] + plus_one[2] + minus_one[1]
+    total = parts[4] + plus_one[1] + plus_two[1] + minus_one[0]
     total = total + from_behind(low, "ka", -4) + from_behind(high, "ka", 4)
-    total = total[0] + lax.ppermute(total[1], "ga", [(0, 2), (2, 0), (1, 3), (3, 1)])
     return arrange(ga_word, total)
 
 

time: 183 us -> 171 us (0.934)
  starting transfers between devices: 34.1 us -> 25.5 us
  other arithmetic: 8.58 us -> 4.75 us
  waiting for transfers between devices: 53.8 us -> 57.2 us
    ppermute x10, starting transfers between devices: 19.2 us -> 13.5 us  [from_behind(): return lax.ppermute(x, axis, [(i, (i + by) % count) for i in range(count)])]
    ppermute x1, waiting for transfers between devices: 3.73 us -> 9.3 us  [body(): lax.ppermute(other, 'ga', [(0, 2), (2, 0), (1, 3), (3, 1)]).astype(f32)]
    all_to_all x1, waiting for transfers between devices: 4.11 us -> 0.01 us  [body(): lax.all_to_all(pieces, 'ka', 0, 0, axis_index_groups=near_groups, tiled=T...]
    all_to_all x1, starting transfers between devices: 12.4 us -> 9.49 us  [body(): lax.all_to_all(pieces, 'ka', 0, 0, axis_index_groups=near_groups, tiled=T...]
    another operation x2, other arithmetic: 3.42 us -> 0.76 us  [body(): here = jnp.stack([message, following])]
    ppermute x10, waiting for transfers between devices: 43.2 us -> 45.7 us  [from_behind(): return lax.ppermute(x, axis, [(i, (i + by) % count) for i in range(count)])]
    add x2 -> x0, local copies, waits for them, and re-layouts: 2.43 us -> none  [the longest x1 1.26 us: body(): rows = rows + jnp.minimum(word[0, 0], 0).astype(bf16)]
  transfers between devices with their start and end apart: 15 -> 15, of which waited for: 10 -> 9; matrix products, arithmetic and copies ran while one was open for 9% -> 7% of each run, Pallas kernels for 23% -> 24%
where the time goes in v4:
time: 171 us
  Pallas kernels  59.4 us (35%)
  waiting for transfers between devices  57.2 us (33%)
  starting transfers between devices  25.5 us (15%)
  between operations  13.7 us (8%)
  local copies, waits for them, and re-layouts  10.1 us (6%)
  other arithmetic  4.75 us (3%)
    ppermute x10, waiting for transfers between devices, from_behind(): return lax.ppermute(x, axis, [(i, (i + by) % count) for i in range(count)])  45.7 us
    pallas_call x2, Pallas kernels, densities(): pl.pallas_call(functools.partial(density_kernel, count, rest, steps), gri...  41.4 us
    pallas_call x1, Pallas kernels, apply_screened(): pl.pallas_call(apply_kernel, in_specs=[smem] * 4 + [pl.BlockSpec(memory_s...  16.3 us
    ppermute x10, starting transfers between devices, from_behind(): return lax.ppermute(x, axis, [(i, (i + by) % count) for i in range(count)])  13.5 us
    all_to_all x1, starting transfers between devices, body(): lax.all_to_all(pieces, 'ka', 0, 0, axis_index_groups=near_groups, tiled=T...  9.49 us
    ppermute x1, waiting for transfers between devices, body(): lax.ppermute(other, 'ga', [(0, 2), (2, 0), (1, 3), (3, 1)]).astype(f32)  9.3 us
  transfers between devices with their start and end apart: 15, of which 9 were waited for; matrix products, arithmetic and copies ran while one was open for 7% of the time, Pallas kernels for 24%

profile of v4, /device:TPU:40, one launch (start us, length us, event | category | flops | bytes accessed | tf_op | source)
XLA Modules:
  0.0 170.7 jit_solution(9513949816073016089)
XLA Ops:
  6.5 2.2 %constant_dynamic-slice_fusion.1 = bf16[1024,2,128]{2,1,0:T(2,128)(2,1)} fusion(bf16[1024,2,256]{2,1,0:T(2,128)(2,1)} %param.5, s32[]{:T(128)S(6)} %select_n.41), kind=kLoop, calls=%fused_computation.58 | loop fusion | bytes 1048580 | tf_op jit(solution)/shard_map/dynamic_slice | solution.py:354
  8.8 1.1 reshape.105
  10.0 1.1 copy.31
  11.2 9.5 %all-to-all-start = ((bf16[16,22,2,4,128]{4,3,2,1,0:T(4,128)(2,1)}), bf16[16,22,2,4,128]{4,3,2,1,0:T(4,128)(2,1)S(1)}, u32[]{:S(2)}, u32[]{:S(2)}) async-start(bf16[16,22,2,4,128]{4,3,2,1,0:T(4,128)(2,1)} %copy.31), calls=%async_computation | async-start | bytes 1441792 | tf_op jit(solution)/shard_map/all_to_all | solution.py:362
  21.0 0.7 fusion.13
  21.7 0.6 collective-permute-start
  22.3 1.5 fusion.17
  23.8 0.9 copy.41
  24.7 18.5 %collective-permute-done = bf16[112,1024]{1,0:T(8,128)(2,1)S(1)} collective-permute-done((bf16[112,1024]{1,0:T(8,128)(2,1)}, bf16[112,1024]{1,0:T(8,128)(2,1)S(1)}, u32[]{:S(2)}, u32[]{:S(2)}) %collective-permute-start) | collective-permute-done | bytes 229408 | tf_op jit(solution)/shard_map/ppermute | solution.py:26
  43.2 1.8 %collective-permute-start.1 = (bf16[2,112,1024]{2,1,0:T(8,128)(2,1)S(1)}, bf16[2,112,1024]{2,1,0:T(8,128)(2,1)S(1)}, u32[]{:S(2)}, u32[]{:S(2)}) collective-permute-start(bf16[2,112,1024]{2,1,0:T(8,128)(2,1)S(1)} %pad_maximum_fusion.1.refs_1_.refs_2_), channel_id=1, source_target_pairs={{0,8},{4,12},{8,16},{12,20},{16,24},{20,28},{24,32},{28,36},{32,40... | collective-permute-start | bytes 1376264 | tf_op jit(solution)/shard_map/ppermute | solution.py:26
  45.4 1.5 maximum_maximum_fusion.refs_3_.refs_5_
  46.9 7.9 %collective-permute-done.1.refs_0_.refs_1_ = bf16[2,112,1024]{2,1,0:T(8,128)(2,1)S(1)} collective-permute-done((bf16[2,112,1024]{2,1,0:T(8,128)(2,1)S(1)}, bf16[2,112,1024]{2,1,0:T(8,128)(2,1)S(1)}, u32[]{:S(2)}, u32[]{:S(2)}) %collective-permute-start.1) | collective-permute-done | bytes 458784 | tf_op jit(solution)/shard_map/ppermute | solution.py:26
  54.8 2.3 %collective-permute-start.2 = (bf16[2,112,1024]{2,1,0:T(8,128)(2,1)S(1)}, bf16[2,112,1024]{2,1,0:T(8,128)(2,1)S(1)}, u32[]{:S(2)}, u32[]{:S(2)}) collective-permute-start(bf16[2,112,1024]{2,1,0:T(8,128)(2,1)S(1)} %collective-permute-done.1.refs_0_.refs_1_), channel_id=1, source_target_pairs={{0,8},{4,12},{8,16},{12,20},{16,24},{20,28},{24,32},{28,36},{32,40... | collective-permute-start | bytes 1376264 | tf_op jit(solution)/shard_map/ppermute | solution.py:26
  57.0 0.5 collective-permute-done.3.refs_2_.refs_3_
  57.5 1.9 %collective-permute-start.4 = (bf16[2,112,1024]{2,1,0:T(8,128)(2,1)S(1)}, bf16[2,112,1024]{2,1,0:T(8,128)(2,1)S(1)}, u32[]{:S(2)}, u32[]{:S(2)}) collective-permute-start(bf16[2,112,1024]{2,1,0:T(8,128)(2,1)S(1)} %collective-permute-done.3.refs_2_.refs_3_), channel_id=1, source_target_pairs={{0,248},{4,252},{8,0},{12,4},{16,8},{20,12},{24,16},{28,20},{32,24... | collective-permute-start | bytes 1376264 | tf_op jit(solution)/shard_map/ppermute | solution.py:26
  59.4 1.3 copy.32
  60.7 1.4 constant_dynamic-slice_fusion
  62.4 20.5 %densities.2 = (bf16[576,16,512]{2,1,0:T(8,128)(2,1)}, bf16[576,16,256]{2,1,0:T(8,128)(2,1)}, s32[6,128]{1,0:T(8,128)}) custom-call(bf16[2,112,1024]{2,1,0:T(8,128)(2,1)S(1)} %collective-permute-done.1.refs_0_.refs_1_, bf16[2,112,1024]{2,1,0:T(8,128)(2,1)S(1)} %pad_maximum_fusion.1.refs_1_.refs_2_, ...), custom_call_target="tpu_custom_call" | custom-call | flops 14495514624 | bytes 18874368 | tf_op jit(solution)/shard_map/densities/pallas_call | solution.py:139
  82.9 20.9 %densities.3 = (bf16[576,16,512]{2,1,0:T(8,128)(2,1)}, bf16[576,16,256]{2,1,0:T(8,128)(2,1)}, s32[8,128]{1,0:T(8,128)S(1)}) custom-call(bf16[2,112,1024]{2,1,0:T(8,128)(2,1)S(1)} %collective-permute-done.2.refs_0_, bf16[2,112,1024]{2,1,0:T(8,128)(2,1)S(1)} %collective-permute-done.1.refs_0_.refs_1_, ...), custom_call_target="tpu_custom_call", output_to_operand_aliasing={{0}: (7, {}), {1}: (8, {})} | custom-call | flops 14495514624 | bytes 18874368 | tf_op jit(solution)/shard_map/densities/pallas_call | solution.py:139
  104.0 0.6 fusion.15
  105.2 0.3 select_reduce_fusion
  105.6 16.3 %apply_screened.1 = f32[4,8,3,56,128]{4,3,2,1,0:T(8,128)S(1)} custom-call(s32[960]{0:T(1024)S(1)} %broadcast_add_fusion.order_ref, s32[60]{0:T(128)S(1)} %broadcast_minimum_fusion.slot_ref, s32[1]{0:T(128)} %bitcast.12.used_ref, s32[1]{0:T(128)} %bitcast.ga_ref, bf16[576,16,512]{2,1,0:T(8,128)(2,1)} %get-tuple-element.13.mv_hbm, ...), custom_call_target="tpu_custom_call" | custom-call | flops 6000000000 | bytes 18874368 | tf_op jit(solution)/shard_map/apply_screened/pallas_call | solution.py:254
  122.1 2.1 %collective-permute-done.5 = bf16[2,8,3,56,128]{4,3,2,1,0:T(8,128)(2,1)S(1)} collective-permute-done((bf16[2,8,3,56,128]{4,3,2,1,0:T(8,128)(2,1)S(1)}, bf16[2,8,3,56,128]{4,3,2,1,0:T(8,128)(2,1)S(1)}, u32[]{:S(2)}, u32[]{:S(2)}) %collective-permute-start.5) | collective-permute-done | bytes 688160 | tf_op jit(solution)/shard_map/ppermute | solution.py:371
  124.3 2.4 %collective-permute-start.6 = (bf16[8,3,56,128]{3,2,1,0:T(8,128)(2,1)S(1)}, bf16[8,3,56,128]{3,2,1,0:T(8,128)(2,1)S(1)}, u32[]{:S(2)}, u32[]{:S(2)}) collective-permute-start(bf16[8,3,56,128]{3,2,1,0:T(8,128)(2,1)S(1)} %fusion.5), channel_id=1, source_target_pairs={{0,2},{2,0},{1,3},{3,1},{4,6},{6,4},{5,7},{7,5},{8,10},{10,8},{9,1... | collective-permute-start | bytes 1032200 | tf_op jit(solution)/shard_map/ppermute | solution.py:374
  126.7 9.3 %collective-permute-done.6 = bf16[8,3,56,128]{3,2,1,0:T(8,128)(2,1)S(1)} collective-permute-done((bf16[8,3,56,128]{3,2,1,0:T(8,128)(2,1)S(1)}, bf16[8,3,56,128]{3,2,1,0:T(8,128)(2,1)S(1)}, u32[]{:S(2)}, u32[]{:S(2)}) %collective-permute-start.6) | collective-permute-done | bytes 344096 | tf_op jit(solution)/shard_map/ppermute | solution.py:374
  136.6 3.0 %collective-permute-start.7 = (bf16[3,3,56,128]{3,2,1,0:T(8,128)(2,1)S(1)}, bf16[3,3,56,128]{3,2,1,0:T(8,128)(2,1)S(1)}, u32[]{:S(2)}, u32[]{:S(2)}) collective-permute-start(bf16[3,3,56,128]{3,2,1,0:T(8,128)(2,1)S(1)} %pad_maximum_fusion.2), channel_id=1, source_target_pairs={{0,4},{4,8},{8,12},{12,16},{16,20},{20,24},{24,28},{28,32},{32,36}... | collective-permute-start | bytes 387080 | tf_op jit(solution)/shard_map/ppermute | solution.py:26
  139.9 2.0 %collective-permute-done.9 = bf16[2,3,56,128]{3,2,1,0:T(8,128)(2,1)S(1)} collective-permute-done((bf16[2,3,56,128]{3,2,1,0:T(8,128)(2,1)S(1)}, bf16[2,3,56,128]{3,2,1,0:T(8,128)(2,1)S(1)}, u32[]{:S(2)}, u32[]{:S(2)}) %collective-permute-start.9) | collective-permute-done | bytes 86048 | tf_op jit(solution)/shard_map/ppermute | solution.py:26
  142.0 7.2 %collective-permute-done.8 = bf16[2,3,56,128]{3,2,1,0:T(8,128)(2,1)S(1)} collective-permute-done((bf16[2,3,56,128]{3,2,1,0:T(8,128)(2,1)S(1)}, bf16[2,3,56,128]{3,2,1,0:T(8,128)(2,1)S(1)}, u32[]{:S(2)}, u32[]{:S(2)}) %collective-permute-start.8) | collective-permute-done | bytes 86048 | tf_op jit(solution)/shard_map/ppermute | solution.py:26
  149.3 3.2 %collective-permute-start.10 = (f32[3,56,128]{2,1,0:T(8,128)S(1)}, f32[3,56,128]{2,1,0:T(8,128)S(1)}, u32[]{:S(2)}, u32[]{:S(2)}) collective-permute-start(f32[3,56,128]{2,1,0:T(8,128)S(1)} %get-tuple-element.19), channel_id=1, source_target_pairs={{0,240},{4,244},{8,248},{12,252},{16,0},{20,4},{24,8},{28,12},{32,... | collective-permute-start | bytes 258056 | tf_op jit(solution)/shard_map/ppermute | solution.py:26
  152.5 2.6 %collective-permute-done.10 = f32[3,56,128]{2,1,0:T(8,128)S(1)} collective-permute-done((f32[3,56,128]{2,1,0:T(8,128)S(1)}, f32[3,56,128]{2,1,0:T(8,128)S(1)}, u32[]{:S(2)}, u32[]{:S(2)}) %collective-permute-start.10) | collective-permute-done | bytes 86048 | tf_op jit(solution)/shard_map/ppermute | solution.py:26
  155.1 7.1 %collective-permute-done.11 = f32[3,56,128]{2,1,0:T(8,128)S(1)} collective-permute-done((f32[3,56,128]{2,1,0:T(8,128)S(1)}, f32[3,56,128]{2,1,0:T(8,128)S(1)}, u32[]{:S(2)}, u32[]{:S(2)}) %collective-permute-start.11) | collective-permute-done | bytes 86048 | tf_op jit(solution)/shard_map/ppermute | solution.py:26
  162.2 1.7 arrange.1
  (61 shorter events, 3.2 us)
Async XLA Ops:
  6.5 54.1 %all-gather.6.cloned.1.call-start = ((), (), s32[]{:S(2)}) async-start(), calls=%async_computation.2 | async-start | bytes 2621440 | tf_op jit(solution)/shard_map/all_gather | solution.py:355
  9.9 10.8 %copy-start.3 = (s32[6,2,6]{2,1,0:T(2,128)S(1)}, s32[6,2,6]{2,1,0:T(2,128)}, u32[]{:S(2)}) copy-start(s32[6,2,6]{2,1,0:T(2,128)} %param.7) | copy-start | bytes 868
  9.9 11.1 %copy-start.2 = (bf16[6,2,8,1024]{3,2,1,0:T(8,128)(2,1)S(1)}, bf16[6,2,8,1024]{3,2,1,0:T(8,128)(2,1)}, u32[]{:S(2)}) copy-start(bf16[6,2,8,1024]{3,2,1,0:T(8,128)(2,1)} %param.4) | copy-start | bytes 589828
  9.9 12.4 %copy-start = (bf16[1024,2,256]{2,1,0:T(2,128)(2,1)S(1)}, bf16[1024,2,256]{2,1,0:T(2,128)(2,1)}, u32[]{:S(2)}) copy-start(bf16[1024,2,256]{2,1,0:T(2,128)(2,1)} %param.5) | copy-start | bytes 3145732
  11.2 48.2 %all-to-all-start = ((bf16[16,22,2,4,128]{4,3,2,1,0:T(4,128)(2,1)}), bf16[16,22,2,4,128]{4,3,2,1,0:T(4,128)(2,1)S(1)}, u32[]{:S(2)}, u32[]{:S(2)}) async-start(bf16[16,22,2,4,128]{4,3,2,1,0:T(4,128)(2,1)} %copy.31), calls=%async_computation | async-start | bytes 1441792 | tf_op jit(solution)/shard_map/all_to_all | solution.py:362
  20.7 84.9 %all-gather.4.cloned.1.call-start = ((), (), s32[]{:S(2)}) async-start(), calls=%async_computation.1 | async-start | bytes 3604480 | tf_op jit(solution)/shard_map/all_gather | solution.py:364
  21.7 21.4 %collective-permute-start = (bf16[112,1024]{1,0:T(8,128)(2,1)}, bf16[112,1024]{1,0:T(8,128)(2,1)S(1)}, u32[]{:S(2)}, u32[]{:S(2)}) collective-permute-start(bf16[112,1024]{1,0:T(8,128)(2,1)} %get-tuple-element.33), channel_id=1, source_target_pairs={{0,252},{4,0},{8,4},{12,8},{16,12},{20,16},{24,20},{28,24},{32,28}... | collective-permute-start | bytes 688136 | tf_op jit(solution)/shard_map/ppermute | solution.py:26
  24.6 20.7 %copy-start.1 = (bf16[1024,1,256]{2,0,1:T(8,128)(2,1)S(1)}, bf16[1024,1,256]{2,0,1:T(8,128)(2,1)}, u32[]{:S(2)}) copy-start(bf16[1024,1,256]{2,0,1:T(8,128)(2,1)} %copy.41) | copy-start | bytes 1572868
  43.2 11.6 %collective-permute-start.1 = (bf16[2,112,1024]{2,1,0:T(8,128)(2,1)S(1)}, bf16[2,112,1024]{2,1,0:T(8,128)(2,1)S(1)}, u32[]{:S(2)}, u32[]{:S(2)}) collective-permute-start(bf16[2,112,1024]{2,1,0:T(8,128)(2,1)S(1)} %pad_maximum_fusion.1.refs_1_.refs_2_), channel_id=1, source_target_pairs={{0,8},{4,12},{8,16},{12,20},{16,24},{20,28},{24,32},{28,36},{32,40... | collective-permute-start | bytes 1376264 | tf_op jit(solution)/shard_map/ppermute | solution.py:26
  45.0 12.5 %collective-permute-start.3 = (bf16[2,112,1024]{2,1,0:T(8,128)(2,1)S(1)}, bf16[2,112,1024]{2,1,0:T(8,128)(2,1)S(1)}, u32[]{:S(2)}, u32[]{:S(2)}) collective-permute-start(bf16[2,112,1024]{2,1,0:T(8,128)(2,1)S(1)} %pad_maximum_fusion.1.refs_1_.refs_2_), channel_id=1, source_target_pairs={{0,248},{4,252},{8,0},{12,4},{16,8},{20,12},{24,16},{28,20},{32,24... | collective-permute-start | bytes 1376264 | tf_op jit(solution)/shard_map/ppermute | solution.py:26
  54.8 28.1 %collective-permute-start.2 = (bf16[2,112,1024]{2,1,0:T(8,128)(2,1)S(1)}, bf16[2,112,1024]{2,1,0:T(8,128)(2,1)S(1)}, u32[]{:S(2)}, u32[]{:S(2)}) collective-permute-start(bf16[2,112,1024]{2,1,0:T(8,128)(2,1)S(1)} %collective-permute-done.1.refs_0_.refs_1_), channel_id=1, source_target_pairs={{0,8},{4,12},{8,16},{12,20},{16,24},{20,28},{24,32},{28,36},{32,40... | collective-permute-start | bytes 1376264 | tf_op jit(solution)/shard_map/ppermute | solution.py:26
  57.5 25.4 %collective-permute-start.4 = (bf16[2,112,1024]{2,1,0:T(8,128)(2,1)S(1)}, bf16[2,112,1024]{2,1,0:T(8,128)(2,1)S(1)}, u32[]{:S(2)}, u32[]{:S(2)}) collective-permute-start(bf16[2,112,1024]{2,1,0:T(8,128)(2,1)S(1)} %collective-permute-done.3.refs_2_.refs_3_), channel_id=1, source_target_pairs={{0,248},{4,252},{8,0},{12,4},{16,8},{20,12},{24,16},{28,20},{32,24... | collective-permute-start | bytes 1376264 | tf_op jit(solution)/shard_map/ppermute | solution.py:26
  122.0 2.2 %collective-permute-start.5 = (bf16[2,8,3,56,128]{4,3,2,1,0:T(8,128)(2,1)S(1)}, bf16[2,8,3,56,128]{4,3,2,1,0:T(8,128)(2,1)S(1)}, u32[]{:S(2)}, u32[]{:S(2)}) collective-permute-start(bf16[2,8,3,56,128]{4,3,2,1,0:T(8,128)(2,1)S(1)} %slice.196), channel_id=1, source_target_pairs={{0,1},{1,0},{2,3},{3,2},{4,5},{5,4},{6,7},{7,6},{8,9},{9,8},{10,11... | collective-permute-start | bytes 2064392 | tf_op jit(solution)/shard_map/ppermute | solution.py:371
  124.3 11.7 %collective-permute-start.6 = (bf16[8,3,56,128]{3,2,1,0:T(8,128)(2,1)S(1)}, bf16[8,3,56,128]{3,2,1,0:T(8,128)(2,1)S(1)}, u32[]{:S(2)}, u32[]{:S(2)}) collective-permute-start(bf16[8,3,56,128]{3,2,1,0:T(8,128)(2,1)S(1)} %fusion.5), channel_id=1, source_target_pairs={{0,2},{2,0},{1,3},{3,1},{4,6},{6,4},{5,7},{7,5},{8,10},{10,8},{9,1... | collective-permute-start | bytes 1032200 | tf_op jit(solution)/shard_map/ppermute | solution.py:374
  136.3 5.7 %collective-permute-start.9 = (bf16[2,3,56,128]{3,2,1,0:T(8,128)(2,1)S(1)}, bf16[2,3,56,128]{3,2,1,0:T(8,128)(2,1)S(1)}, u32[]{:S(2)}, u32[]{:S(2)}) collective-permute-start(bf16[2,3,56,128]{3,2,1,0:T(8,128)(2,1)S(1)} %pad_maximum_fusion.4), channel_id=1, source_target_pairs={{0,252},{4,0},{8,4},{12,8},{16,12},{20,16},{24,20},{28,24},{32,28}... | collective-permute-start | bytes 258056 | tf_op jit(solution)/shard_map/ppermute | solution.py:26
  136.6 12.6 %collective-permute-start.7 = (bf16[3,3,56,128]{3,2,1,0:T(8,128)(2,1)S(1)}, bf16[3,3,56,128]{3,2,1,0:T(8,128)(2,1)S(1)}, u32[]{:S(2)}, u32[]{:S(2)}) collective-permute-start(bf16[3,3,56,128]{3,2,1,0:T(8,128)(2,1)S(1)} %pad_maximum_fusion.2), channel_id=1, source_target_pairs={{0,4},{4,8},{8,12},{12,16},{16,20},{20,24},{24,28},{28,32},{32,36}... | collective-permute-start | bytes 387080 | tf_op jit(solution)/shard_map/ppermute | solution.py:26
  139.6 9.6 %collective-permute-start.8 = (bf16[2,3,56,128]{3,2,1,0:T(8,128)(2,1)S(1)}, bf16[2,3,56,128]{3,2,1,0:T(8,128)(2,1)S(1)}, u32[]{:S(2)}, u32[]{:S(2)}) collective-permute-start(bf16[2,3,56,128]{3,2,1,0:T(8,128)(2,1)S(1)} %pad_maximum_fusion.3), channel_id=1, source_target_pairs={{0,8},{4,12},{8,16},{12,20},{16,24},{20,28},{24,32},{28,36},{32,40... | collective-permute-start | bytes 258056 | tf_op jit(solution)/shard_map/ppermute | solution.py:26
  149.3 5.7 %collective-permute-start.10 = (f32[3,56,128]{2,1,0:T(8,128)S(1)}, f32[3,56,128]{2,1,0:T(8,128)S(1)}, u32[]{:S(2)}, u32[]{:S(2)}) collective-permute-start(f32[3,56,128]{2,1,0:T(8,128)S(1)} %get-tuple-element.19), channel_id=1, source_target_pairs={{0,240},{4,244},{8,248},{12,252},{16,0},{20,4},{24,8},{28,12},{32,... | collective-permute-start | bytes 258056 | tf_op jit(solution)/shard_map/ppermute | solution.py:26
  152.5 9.6 %collective-permute-start.11 = (f32[3,56,128]{2,1,0:T(8,128)S(1)}, f32[3,56,128]{2,1,0:T(8,128)S(1)}, u32[]{:S(2)}, u32[]{:S(2)}) collective-permute-start(f32[3,56,128]{2,1,0:T(8,128)S(1)} %get-tuple-element.20), channel_id=1, source_target_pairs={{0,16},{4,20},{8,24},{12,28},{16,32},{20,36},{24,40},{28,44},{32,4... | collective-permute-start | bytes 258056 | tf_op jit(solution)/shard_map/ppermute | solution.py:26
Sparse Core Ops, SparseCore 0:
  9.2 40.3 all-gather.5
  60.8 40.2 all-gather.3

commit v5 on v4

--- a/solution.py
+++ b/solution.py
@@ -75,26 +75,27 @@
         for buf, z_ref, out_ref in ((v_buf, zv_ref, mv_ref), (c_buf, zc_ref, mc_ref)):
             for tile in range(z_ref.shape[1] // 256):
                 cols = slice(256 * tile, 256 * tile + 256)
-                for jl in range(2):
-                    res = jnp.dot(buf[192 * jl : 192 * jl + 192], z_ref[:, cols], preferred_element_type=f32)
-                    for o in range(2):
-                        for p in range(3):
-                            base = (o * 3 + p) * 32
-                            a = [res[base + 8 * c : base + 8 * c + 8] for c in range(4)]
-                            first = [half_swap(mask, a[0], a[1]), half_swap(mask, a[2], a[3])]
-                            second = [
-                                jnp.where(mask, pltpu.roll(a[0], 4, 0), a[1]),
-                                jnp.where(mask, pltpu.roll(a[2], 4, 0), a[3]),
-                            ]
-                            for jj, value in ((0, first), (1, second)):
-                                index = sub * 24 + (2 * p + jj) * 4 + jl * 2 + o
-                                out_ref[index, :, cols] = jnp.concatenate(value, axis=0).astype(bf16)
-                    yield
-
-    def drain(*generators):
-        live = list(generators)
-        while live:
-            live = [g for g in live if next(g, True) is None]
+                res = jnp.dot(buf[...], z_ref[:, cols], preferred_element_type=f32)
+                yield
+                for group in range(12):
+                    base = group * 32
+                    jl, o, p = group // 6, group // 3 % 2, group % 3
+                    a = [res[base + 8 * c : base + 8 * c + 8] for c in range(4)]
+                    first = [half_swap(mask, a[0], a[1]), half_swap(mask, a[2], a[3])]
+                    second = [
+                        jnp.where(mask, pltpu.roll(a[0], 4, 0), a[1]),
+                        jnp.where(mask, pltpu.roll(a[2], 4, 0), a[3]),
+                    ]
+                    for jj, value in ((0, first), (1, second)):
+                        index = sub * 24 + (2 * p + jj) * 4 + jl * 2 + o
+                        out_ref[index, :, cols] = jnp.concatenate(value, axis=0).astype(bf16)
+
+    def together(matmuls, products):
+        for _ in matmuls:
+            for _ in range(6):
+                next(products, None)
+        for _ in products:
+            pass
 
     @pl.when(step == 0)
     def _():
@@ -116,10 +117,10 @@
                         else:
                             right[index, 0, r] = jnp.where(low, right[index, 0, r], turned)
                             right[index, 1, r] = jnp.where(low, right[index, 1, r], half)
-        drain(produce(0, va, ca))
-
-    drain(consume(0, va, ca), produce(2 * step + 1, vb, cb))
-    drain(consume(1, vb, cb), produce(jnp.minimum(2 * step + 2, 2 * steps - 1), va, ca))
+        together((), produce(0, va, ca))
+
+    together(consume(0, va, ca), produce(2 * step + 1, vb, cb))
+    together(consume(1, vb, cb), produce(jnp.minimum(2 * step + 2, 2 * steps - 1), va, ca))
 
 
 def densities(pairs, rest, zv, zc, previous):
@@ -179,7 +180,6 @@
     fetch_v = pltpu.make_async_copy(mv_hbm, mv_ref, done.at[0])
     fetch_c = pltpu.make_async_copy(mc_hbm, mc_ref, done.at[1])
     fetch_v.start()
-    fetch_c.start()
     ga = ga_ref[0]
     lane_group = lax.broadcasted_iota(jnp.int32, (16, 128), 1) >> 5
     spots = [(((q & 1) ^ (ga & 1)) << 1) | ((q >> 1) ^ (ga >> 1)) for q in range(4)]
@@ -197,6 +197,7 @@
 
     lax.fori_loop(0, SLOTS, build, 0)
     fetch_v.wait()
+    fetch_c.start()
 
     def chunk(q, carry):
         for u in range(UNROLL):
@@ -356,14 +357,16 @@
     zc = zeta_matrix(lax.dynamic_index_in_dim(halves, part // 2, 0, keepdims=False))
     pieces = jnp.transpose(screened.reshape(SLOTS, 2, 4, WIN, 128), (3, 0, 1, 2, 4))
     pieces = jnp.concatenate([pieces, pieces], axis=0)
+    pieces = pieces + message[0, 0] * 0
     line = 2 * WIN
     near_groups = [[x * line + s for s in range(line)] for x in range(ka_count // line)]
     x_groups = [[x * line + s for x in range(ka_count // line)] for s in range(line)]
     pieces = lax.all_to_all(pieces, "ka", 0, 0, axis_index_groups=near_groups, tiled=True)
     rows = jnp.transpose(pieces, (1, 2, 0, 3, 4)).reshape(SLOTS, 2, 4 * line, 128)
     w = lax.all_gather(rows, "ka", axis_index_groups=x_groups)
-    ahead2 = from_behind(ahead, "ka", -2)
-    behind2 = from_behind(behind, "ka", 2)
+    zero = rows[0, 0, 0, 0] * 0
+    ahead2 = from_behind(ahead + zero, "ka", -2)
+    behind2 = from_behind(behind + zero, "ka", 2)
     mv, mc, _ = densities((behind, here, ahead), False, zv, zc, None)
     mv, mc, words = densities((behind2, behind, here, ahead, ahead2), True, zv, zc, (mv, mc))
     order, slot_of, used = schedule(words[:, :PAIRS].reshape(TOTAL))

time: 171 us -> 172 us (level)
  waiting for transfers between devices: 57.2 us -> 54.1 us
  local copies, waits for them, and re-layouts: 10.1 us -> 12.2 us
  other arithmetic: 4.75 us -> 6.82 us
    ppermute x10, waiting for transfers between devices: 45.7 us -> 42.6 us  [from_behind(): return lax.ppermute(x, axis, [(i, (i + by) % count) for i in range(count)])]
    slice x0 -> x2, local copies, waits for them, and re-layouts: none -> 1.74 us  [the longest x1 1.19 us: body(): pieces = pieces + message[0, 0] * 0]
  transfers between devices with their start and end apart: 15 -> 15, of which waited for: 9 -> 9; matrix products, arithmetic and copies ran while one was open for 7% -> 9% of each run, Pallas kernels for 24% -> 23%
where the time goes in v5:
time: 172 us
  Pallas kernels  57.9 us (34%)
  waiting for transfers between devices  54.1 us (31%)
  starting transfers between devices  25.8 us (15%)
  between operations  15.1 us (9%)
  local copies, waits for them, and re-layouts  12.2 us (7%)
  other arithmetic  6.82 us (4%)
    ppermute x10, waiting for transfers between devices, from_behind(): return lax.ppermute(x, axis, [(i, (i + by) % count) for i in range(count)])  42.6 us
    pallas_call x2, Pallas kernels, densities(): pl.pallas_call(functools.partial(density_kernel, count, rest, steps), gri...  39.9 us
    pallas_call x1, Pallas kernels, apply_screened(): pl.pallas_call(apply_kernel, in_specs=[smem] * 4 + [pl.BlockSpec(memory_s...  16.3 us
    ppermute x10, starting transfers between devices, from_behind(): return lax.ppermute(x, axis, [(i, (i + by) % count) for i in range(count)])  13.8 us
    all_to_all x1, starting transfers between devices, body(): lax.all_to_all(pieces, 'ka', 0, 0, axis_index_groups=near_groups, tiled=T...  9.49 us
    ppermute x1, waiting for transfers between devices, body(): lax.ppermute(other, 'ga', [(0, 2), (2, 0), (1, 3), (3, 1)]).astype(f32)  9.31 us
  transfers between devices with their start and end apart: 15, of which 9 were waited for; matrix products, arithmetic and copies ran while one was open for 9% of the time, Pallas kernels for 23%

profile of v5, /device:TPU:40, one launch (start us, length us, event | category | flops | bytes accessed | tf_op | source)
XLA Modules:
  0.0 171.9 jit_solution(1017305577845020728)
XLA Ops:
  6.5 2.2 %constant_dynamic-slice_fusion.1 = bf16[1024,2,128]{2,1,0:T(2,128)(2,1)} fusion(bf16[1024,2,256]{2,1,0:T(2,128)(2,1)} %param.5, s32[]{:T(128)S(6)} %select_n.41), kind=kLoop, calls=%fused_computation.60 | loop fusion | bytes 1048580 | tf_op jit(solution)/shard_map/dynamic_slice | solution.py:355
  8.8 1.2 slice.133
  10.0 1.1 reshape.111
  12.0 1.1 copy.29
  13.2 9.5 %all-to-all-start = ((bf16[16,22,2,4,128]{4,3,2,1,0:T(4,128)(2,1)}), bf16[16,22,2,4,128]{4,3,2,1,0:T(4,128)(2,1)S(1)}, u32[]{:S(2)}, u32[]{:S(2)}) async-start(bf16[16,22,2,4,128]{4,3,2,1,0:T(4,128)(2,1)} %copy.29), calls=%async_computation | async-start | bytes 1441792 | tf_op jit(solution)/shard_map/all_to_all | solution.py:364
  23.0 0.8 fusion.13
  24.4 1.5 fusion.17
  26.0 19.2 %collective-permute-done = bf16[112,1024]{1,0:T(8,128)(2,1)} collective-permute-done((bf16[112,1024]{1,0:T(8,128)(2,1)}, bf16[112,1024]{1,0:T(8,128)(2,1)}, u32[]{:S(2)}, u32[]{:S(2)}) %collective-permute-start) | collective-permute-done | bytes 229408 | tf_op jit(solution)/shard_map/ppermute | solution.py:26
  45.2 1.1 pad_maximum_fusion.refs_1_.refs_2_
  46.3 1.8 %collective-permute-start.1 = (bf16[2,112,1024]{2,1,0:T(8,128)(2,1)S(1)}, bf16[2,112,1024]{2,1,0:T(8,128)(2,1)S(1)}, u32[]{:S(2)}, u32[]{:S(2)}) collective-permute-start(bf16[2,112,1024]{2,1,0:T(8,128)(2,1)S(1)} %pad_maximum_fusion.refs_1_.refs_2_), channel_id=1, source_target_pairs={{0,8},{4,12},{8,16},{12,20},{16,24},{20,28},{24,32},{28,36},{32,40... | collective-permute-start | bytes 1376264 | tf_op jit(solution)/shard_map/ppermute | solution.py:26
  48.6 1.5 maximum_maximum_fusion.refs_3_.refs_5_
  50.1 0.9 copy-done.2
  50.9 1.5 copy.30
  53.7 4.1 %collective-permute-done.1.refs_0_.refs_1_ = bf16[2,112,1024]{2,1,0:T(8,128)(2,1)S(1)} collective-permute-done((bf16[2,112,1024]{2,1,0:T(8,128)(2,1)S(1)}, bf16[2,112,1024]{2,1,0:T(8,128)(2,1)S(1)}, u32[]{:S(2)}, u32[]{:S(2)}) %collective-permute-start.1) | collective-permute-done | bytes 458784 | tf_op jit(solution)/shard_map/ppermute | solution.py:26
  57.8 2.5 %collective-permute-start.2 = (bf16[2,112,1024]{2,1,0:T(8,128)(2,1)S(1)}, bf16[2,112,1024]{2,1,0:T(8,128)(2,1)S(1)}, u32[]{:S(2)}, u32[]{:S(2)}) collective-permute-start(bf16[2,112,1024]{2,1,0:T(8,128)(2,1)S(1)} %broadcast_add_fusion.1), channel_id=1, source_target_pairs={{0,8},{4,12},{8,16},{12,20},{16,24},{20,28},{24,32},{28,36},{32,40... | collective-permute-start | bytes 1376264 | tf_op jit(solution)/shard_map/ppermute | solution.py:26
  60.8 0.8 broadcast_add_fusion
  61.6 1.7 %collective-permute-start.4 = (bf16[2,112,1024]{2,1,0:T(8,128)(2,1)}, bf16[2,112,1024]{2,1,0:T(8,128)(2,1)S(1)}, u32[]{:S(2)}, u32[]{:S(2)}) collective-permute-start(bf16[2,112,1024]{2,1,0:T(8,128)(2,1)} %broadcast_add_fusion), channel_id=1, source_target_pairs={{0,248},{4,252},{8,0},{12,4},{16,8},{20,12},{24,16},{28,20},{32,24... | collective-permute-start | bytes 1376264 | tf_op jit(solution)/shard_map/ppermute | solution.py:26
  63.4 1.4 constant_dynamic-slice_fusion
  65.1 19.8 %densities.2 = (bf16[576,16,512]{2,1,0:T(8,128)(2,1)}, bf16[576,16,256]{2,1,0:T(8,128)(2,1)}, s32[6,128]{1,0:T(8,128)}) custom-call(bf16[2,112,1024]{2,1,0:T(8,128)(2,1)S(1)} %collective-permute-done.1.refs_0_.refs_1_, bf16[2,112,1024]{2,1,0:T(8,128)(2,1)S(1)} %pad_maximum_fusion.refs_1_.refs_2_, ...), custom_call_target="tpu_custom_call" | custom-call | flops 14495514624 | bytes 18874368 | tf_op jit(solution)/shard_map/densities/pallas_call | solution.py:140
  84.9 20.1 %densities.3 = (bf16[576,16,512]{2,1,0:T(8,128)(2,1)}, bf16[576,16,256]{2,1,0:T(8,128)(2,1)}, s32[8,128]{1,0:T(8,128)S(1)}) custom-call(bf16[2,112,1024]{2,1,0:T(8,128)(2,1)S(1)} %collective-permute-done.2.refs_0_, bf16[2,112,1024]{2,1,0:T(8,128)(2,1)S(1)} %collective-permute-done.1.refs_0_.refs_1_, ...), custom_call_target="tpu_custom_call", output_to_operand_aliasing={{0}: (7, {}), {1}: (8, {})} | custom-call | flops 14495514624 | bytes 18874368 | tf_op jit(solution)/shard_map/densities/pallas_call | solution.py:140
  105.2 0.6 fusion.15
  106.8 16.3 %apply_screened.1 = f32[4,8,3,56,128]{4,3,2,1,0:T(8,128)S(1)} custom-call(s32[960]{0:T(1024)S(1)} %broadcast_add_fusion.2.order_ref, s32[60]{0:T(128)S(1)} %broadcast_minimum_fusion.slot_ref, s32[1]{0:T(128)} %bitcast.17.used_ref, s32[1]{0:T(128)} %bitcast.ga_ref, bf16[576,16,512]{2,1,0:T(8,128)(2,1)} %get-tuple-element.13.mv_hbm, ...), custom_call_target="tpu_custom_call" | custom-call | flops 6000000000 | bytes 18874368 | tf_op jit(solution)/shard_map/apply_screened/pallas_call | solution.py:255
  123.3 2.1 %collective-permute-done.5 = bf16[2,8,3,56,128]{4,3,2,1,0:T(8,128)(2,1)S(1)} collective-permute-done((bf16[2,8,3,56,128]{4,3,2,1,0:T(8,128)(2,1)S(1)}, bf16[2,8,3,56,128]{4,3,2,1,0:T(8,128)(2,1)S(1)}, u32[]{:S(2)}, u32[]{:S(2)}) %collective-permute-start.5) | collective-permute-done | bytes 688160 | tf_op jit(solution)/shard_map/ppermute | solution.py:374
  125.5 2.4 %collective-permute-start.6 = (bf16[8,3,56,128]{3,2,1,0:T(8,128)(2,1)S(1)}, bf16[8,3,56,128]{3,2,1,0:T(8,128)(2,1)S(1)}, u32[]{:S(2)}, u32[]{:S(2)}) collective-permute-start(bf16[8,3,56,128]{3,2,1,0:T(8,128)(2,1)S(1)} %fusion.5), channel_id=1, source_target_pairs={{0,2},{2,0},{1,3},{3,1},{4,6},{6,4},{5,7},{7,5},{8,10},{10,8},{9,1... | collective-permute-start | bytes 1032200 | tf_op jit(solution)/shard_map/ppermute | solution.py:377
  127.9 9.3 %collective-permute-done.6 = bf16[8,3,56,128]{3,2,1,0:T(8,128)(2,1)S(1)} collective-permute-done((bf16[8,3,56,128]{3,2,1,0:T(8,128)(2,1)S(1)}, bf16[8,3,56,128]{3,2,1,0:T(8,128)(2,1)S(1)}, u32[]{:S(2)}, u32[]{:S(2)}) %collective-permute-start.6) | collective-permute-done | bytes 344096 | tf_op jit(solution)/shard_map/ppermute | solution.py:377
  137.9 3.0 %collective-permute-start.7 = (bf16[3,3,56,128]{3,2,1,0:T(8,128)(2,1)S(1)}, bf16[3,3,56,128]{3,2,1,0:T(8,128)(2,1)S(1)}, u32[]{:S(2)}, u32[]{:S(2)}) collective-permute-start(bf16[3,3,56,128]{3,2,1,0:T(8,128)(2,1)S(1)} %pad_maximum_fusion.1), channel_id=1, source_target_pairs={{0,4},{4,8},{8,12},{12,16},{16,20},{20,24},{24,28},{28,32},{32,36}... | collective-permute-start | bytes 387080 | tf_op jit(solution)/shard_map/ppermute | solution.py:26
  141.3 1.9 %collective-permute-done.9 = bf16[2,3,56,128]{3,2,1,0:T(8,128)(2,1)S(1)} collective-permute-done((bf16[2,3,56,128]{3,2,1,0:T(8,128)(2,1)S(1)}, bf16[2,3,56,128]{3,2,1,0:T(8,128)(2,1)S(1)}, u32[]{:S(2)}, u32[]{:S(2)}) %collective-permute-start.9) | collective-permute-done | bytes 86048 | tf_op jit(solution)/shard_map/ppermute | solution.py:26
  143.2 7.2 %collective-permute-done.8 = bf16[2,3,56,128]{3,2,1,0:T(8,128)(2,1)S(1)} collective-permute-done((bf16[2,3,56,128]{3,2,1,0:T(8,128)(2,1)S(1)}, bf16[2,3,56,128]{3,2,1,0:T(8,128)(2,1)S(1)}, u32[]{:S(2)}, u32[]{:S(2)}) %collective-permute-start.8) | collective-permute-done | bytes 86048 | tf_op jit(solution)/shard_map/ppermute | solution.py:26
  150.5 3.2 %collective-permute-start.10 = (f32[3,56,128]{2,1,0:T(8,128)S(1)}, f32[3,56,128]{2,1,0:T(8,128)S(1)}, u32[]{:S(2)}, u32[]{:S(2)}) collective-permute-start(f32[3,56,128]{2,1,0:T(8,128)S(1)} %get-tuple-element.19), channel_id=1, source_target_pairs={{0,240},{4,244},{8,248},{12,252},{16,0},{20,4},{24,8},{28,12},{32,... | collective-permute-start | bytes 258056 | tf_op jit(solution)/shard_map/ppermute | solution.py:26
  153.7 2.5 %collective-permute-done.10 = f32[3,56,128]{2,1,0:T(8,128)S(1)} collective-permute-done((f32[3,56,128]{2,1,0:T(8,128)S(1)}, f32[3,56,128]{2,1,0:T(8,128)S(1)}, u32[]{:S(2)}, u32[]{:S(2)}) %collective-permute-start.10) | collective-permute-done | bytes 86048 | tf_op jit(solution)/shard_map/ppermute | solution.py:26
  156.2 7.1 %collective-permute-done.11 = f32[3,56,128]{2,1,0:T(8,128)S(1)} collective-permute-done((f32[3,56,128]{2,1,0:T(8,128)S(1)}, f32[3,56,128]{2,1,0:T(8,128)S(1)}, u32[]{:S(2)}, u32[]{:S(2)}) %collective-permute-start.11) | collective-permute-done | bytes 86048 | tf_op jit(solution)/shard_map/ppermute | solution.py:26
  163.4 1.7 arrange.1
  (67 shorter events, 5.5 us)
Async XLA Ops:
  6.5 56.8 %all-gather.6.cloned.1.call-start = ((), (), s32[]{:S(2)}) async-start(), calls=%async_computation.2 | async-start | bytes 2621440 | tf_op jit(solution)/shard_map/all_gather | solution.py:356
  11.1 11.6 %copy-start.4 = (s32[6,2,6]{2,1,0:T(2,128)S(1)}, s32[6,2,6]{2,1,0:T(2,128)}, u32[]{:S(2)}) copy-start(s32[6,2,6]{2,1,0:T(2,128)} %param.7) | copy-start | bytes 868
  11.1 11.9 %copy-start.3 = (bf16[6,2,8,1024]{3,2,1,0:T(8,128)(2,1)S(1)}, bf16[6,2,8,1024]{3,2,1,0:T(8,128)(2,1)}, u32[]{:S(2)}) copy-start(bf16[6,2,8,1024]{3,2,1,0:T(8,128)(2,1)} %param.4) | copy-start | bytes 589828
  11.8 12.6 %copy-start = (bf16[1024,2,256]{2,1,0:T(2,128)(2,1)S(1)}, bf16[1024,2,256]{2,1,0:T(2,128)(2,1)}, u32[]{:S(2)}) copy-start(bf16[1024,2,256]{2,1,0:T(2,128)(2,1)} %param.5) | copy-start | bytes 3145732
  13.2 36.9 %all-to-all-start = ((bf16[16,22,2,4,128]{4,3,2,1,0:T(4,128)(2,1)}), bf16[16,22,2,4,128]{4,3,2,1,0:T(4,128)(2,1)S(1)}, u32[]{:S(2)}, u32[]{:S(2)}) async-start(bf16[16,22,2,4,128]{4,3,2,1,0:T(4,128)(2,1)} %copy.29), calls=%async_computation | async-start | bytes 1441792 | tf_op jit(solution)/shard_map/all_to_all | solution.py:364
  22.6 84.1 %all-gather.4.cloned.1.call-start = ((), (), s32[]{:S(2)}) async-start(), calls=%async_computation.1 | async-start | bytes 3604480 | tf_op jit(solution)/shard_map/all_gather | solution.py:366
  23.8 21.4 %collective-permute-start = (bf16[112,1024]{1,0:T(8,128)(2,1)}, bf16[112,1024]{1,0:T(8,128)(2,1)}, u32[]{:S(2)}, u32[]{:S(2)}) collective-permute-start(bf16[112,1024]{1,0:T(8,128)(2,1)} %get-tuple-element.33), channel_id=1, source_target_pairs={{0,252},{4,0},{8,4},{12,8},{16,12},{20,16},{24,20},{28,24},{32,28}... | collective-permute-start | bytes 688136 | tf_op jit(solution)/shard_map/ppermute | solution.py:26
  46.3 11.5 %collective-permute-start.1 = (bf16[2,112,1024]{2,1,0:T(8,128)(2,1)S(1)}, bf16[2,112,1024]{2,1,0:T(8,128)(2,1)S(1)}, u32[]{:S(2)}, u32[]{:S(2)}) collective-permute-start(bf16[2,112,1024]{2,1,0:T(8,128)(2,1)S(1)} %pad_maximum_fusion.refs_1_.refs_2_), channel_id=1, source_target_pairs={{0,8},{4,12},{8,16},{12,20},{16,24},{20,28},{24,32},{28,36},{32,40... | collective-permute-start | bytes 1376264 | tf_op jit(solution)/shard_map/ppermute | solution.py:26
  48.2 12.6 %collective-permute-start.3 = (bf16[2,112,1024]{2,1,0:T(8,128)(2,1)S(1)}, bf16[2,112,1024]{2,1,0:T(8,128)(2,1)S(1)}, u32[]{:S(2)}, u32[]{:S(2)}) collective-permute-start(bf16[2,112,1024]{2,1,0:T(8,128)(2,1)S(1)} %pad_maximum_fusion.refs_1_.refs_2_), channel_id=1, source_target_pairs={{0,248},{4,252},{8,0},{12,4},{16,8},{20,12},{24,16},{28,20},{32,24... | collective-permute-start | bytes 1376264 | tf_op jit(solution)/shard_map/ppermute | solution.py:26
  50.1 0.9 copy-start.2
  52.4 10.9 %copy-start.1 = (bf16[22,2,16,4,128]{4,3,2,1,0:T(4,128)(2,1)}, bf16[22,2,16,4,128]{4,3,2,1,0:T(4,128)(2,1)S(1)}, u32[]{:S(2)}) copy-start(bf16[22,2,16,4,128]{4,3,2,1,0:T(4,128)(2,1)S(1)} %copy.30) | copy-start | bytes 2162692
  57.8 27.0 %collective-permute-start.2 = (bf16[2,112,1024]{2,1,0:T(8,128)(2,1)S(1)}, bf16[2,112,1024]{2,1,0:T(8,128)(2,1)S(1)}, u32[]{:S(2)}, u32[]{:S(2)}) collective-permute-start(bf16[2,112,1024]{2,1,0:T(8,128)(2,1)S(1)} %broadcast_add_fusion.1), channel_id=1, source_target_pairs={{0,8},{4,12},{8,16},{12,20},{16,24},{20,28},{24,32},{28,36},{32,40... | collective-permute-start | bytes 1376264 | tf_op jit(solution)/shard_map/ppermute | solution.py:26
  61.6 23.3 %collective-permute-start.4 = (bf16[2,112,1024]{2,1,0:T(8,128)(2,1)}, bf16[2,112,1024]{2,1,0:T(8,128)(2,1)S(1)}, u32[]{:S(2)}, u32[]{:S(2)}) collective-permute-start(bf16[2,112,1024]{2,1,0:T(8,128)(2,1)} %broadcast_add_fusion), channel_id=1, source_target_pairs={{0,248},{4,252},{8,0},{12,4},{16,8},{20,12},{24,16},{28,20},{32,24... | collective-permute-start | bytes 1376264 | tf_op jit(solution)/shard_map/ppermute | solution.py:26
  123.2 2.2 %collective-permute-start.5 = (bf16[2,8,3,56,128]{4,3,2,1,0:T(8,128)(2,1)S(1)}, bf16[2,8,3,56,128]{4,3,2,1,0:T(8,128)(2,1)S(1)}, u32[]{:S(2)}, u32[]{:S(2)}) collective-permute-start(bf16[2,8,3,56,128]{4,3,2,1,0:T(8,128)(2,1)S(1)} %slice.206), channel_id=1, source_target_pairs={{0,1},{1,0},{2,3},{3,2},{4,5},{5,4},{6,7},{7,6},{8,9},{9,8},{10,11... | collective-permute-start | bytes 2064392 | tf_op jit(solution)/shard_map/ppermute | solution.py:374
  125.5 11.7 %collective-permute-start.6 = (bf16[8,3,56,128]{3,2,1,0:T(8,128)(2,1)S(1)}, bf16[8,3,56,128]{3,2,1,0:T(8,128)(2,1)S(1)}, u32[]{:S(2)}, u32[]{:S(2)}) collective-permute-start(bf16[8,3,56,128]{3,2,1,0:T(8,128)(2,1)S(1)} %fusion.5), channel_id=1, source_target_pairs={{0,2},{2,0},{1,3},{3,1},{4,6},{6,4},{5,7},{7,5},{8,10},{10,8},{9,1... | collective-permute-start | bytes 1032200 | tf_op jit(solution)/shard_map/ppermute | solution.py:377
  137.5 5.7 %collective-permute-start.9 = (bf16[2,3,56,128]{3,2,1,0:T(8,128)(2,1)S(1)}, bf16[2,3,56,128]{3,2,1,0:T(8,128)(2,1)S(1)}, u32[]{:S(2)}, u32[]{:S(2)}) collective-permute-start(bf16[2,3,56,128]{3,2,1,0:T(8,128)(2,1)S(1)} %pad_maximum_fusion.3), channel_id=1, source_target_pairs={{0,252},{4,0},{8,4},{12,8},{16,12},{20,16},{24,20},{28,24},{32,28}... | collective-permute-start | bytes 258056 | tf_op jit(solution)/shard_map/ppermute | solution.py:26
  137.9 12.5 %collective-permute-start.7 = (bf16[3,3,56,128]{3,2,1,0:T(8,128)(2,1)S(1)}, bf16[3,3,56,128]{3,2,1,0:T(8,128)(2,1)S(1)}, u32[]{:S(2)}, u32[]{:S(2)}) collective-permute-start(bf16[3,3,56,128]{3,2,1,0:T(8,128)(2,1)S(1)} %pad_maximum_fusion.1), channel_id=1, source_target_pairs={{0,4},{4,8},{8,12},{12,16},{16,20},{20,24},{24,28},{28,32},{32,36}... | collective-permute-start | bytes 387080 | tf_op jit(solution)/shard_map/ppermute | solution.py:26
  140.9 9.5 %collective-permute-start.8 = (bf16[2,3,56,128]{3,2,1,0:T(8,128)(2,1)S(1)}, bf16[2,3,56,128]{3,2,1,0:T(8,128)(2,1)S(1)}, u32[]{:S(2)}, u32[]{:S(2)}) collective-permute-start(bf16[2,3,56,128]{3,2,1,0:T(8,128)(2,1)S(1)} %pad_maximum_fusion.2), channel_id=1, source_target_pairs={{0,8},{4,12},{8,16},{12,20},{16,24},{20,28},{24,32},{28,36},{32,40... | collective-permute-start | bytes 258056 | tf_op jit(solution)/shard_map/ppermute | solution.py:26
  150.5 5.7 %collective-permute-start.10 = (f32[3,56,128]{2,1,0:T(8,128)S(1)}, f32[3,56,128]{2,1,0:T(8,128)S(1)}, u32[]{:S(2)}, u32[]{:S(2)}) collective-permute-start(f32[3,56,128]{2,1,0:T(8,128)S(1)} %get-tuple-element.19), channel_id=1, source_target_pairs={{0,240},{4,244},{8,248},{12,252},{16,0},{20,4},{24,8},{28,12},{32,... | collective-permute-start | bytes 258056 | tf_op jit(solution)/shard_map/ppermute | solution.py:26
  153.7 9.6 %collective-permute-start.11 = (f32[3,56,128]{2,1,0:T(8,128)S(1)}, f32[3,56,128]{2,1,0:T(8,128)S(1)}, u32[]{:S(2)}, u32[]{:S(2)}) collective-permute-start(f32[3,56,128]{2,1,0:T(8,128)S(1)} %get-tuple-element.20), channel_id=1, source_target_pairs={{0,16},{4,20},{8,24},{12,28},{16,32},{20,36},{24,40},{28,44},{32,4... | collective-permute-start | bytes 258056 | tf_op jit(solution)/shard_map/ppermute | solution.py:26
Sparse Core Ops, SparseCore 0:
  9.2 42.3 all-gather.5
  63.5 40.2 all-gather.3

commit v6 on v5

--- a/solution.py
+++ b/solution.py
@@ -30,7 +30,7 @@
     return jnp.where(mask, first, pltpu.roll(second, 4, 0))
 
 
-def density_kernel(count, rest, steps, *refs):
+def density_kernel(count, steps, *refs):
     pair_refs = refs[:count]
     zv_ref, zc_ref = refs[count : count + 2]
     mv_ref, mc_ref, slots_ref, left, right, va, ca, vb, cb = refs[-9:]
@@ -40,8 +40,6 @@
     def produce(chunk, v_buf, c_buf):
         block = chunk // 3
         jh = chunk % 3
-        if rest:
-            block = block + jnp.where(block >= 2, 4, 0)
         for cv, buf in ((0, v_buf), (1, c_buf)):
             for jl in range(2):
                 point = block * KB + 2 * jh + jl
@@ -105,7 +103,8 @@
                 slots_ref[b : b + 1, :] = tail[0:1].astype(jnp.int32)
             for j in range(KB):
                 x = pair_refs[b // 2][b % 2, 16 * j : 16 * j + 16, :].astype(f32)
-                left[b * KB + j] = x
+                if b < WIN:
+                    left[b * KB + j] = x
                 if b > 0:
                     index = (b - 1) * 3 + j // 2
                     for r in range(2):
@@ -123,43 +122,37 @@
     together(consume(1, vb, cb), produce(jnp.minimum(2 * step + 2, 2 * steps - 1), va, ca))
 
 
-def densities(pairs, rest, zv, zc, previous):
+def densities(pairs, zv, zc):
     whole = lambda shape: pl.BlockSpec(shape, lambda n: (0,) * len(shape), pipeline_mode=pl.Buffered(1))
     operands = list(pairs) + [zv, zc]
     in_specs = [whole(x.shape) for x in operands]
-    aliases = {}
-    if previous is not None:
-        aliases = {len(operands): 0, len(operands) + 1: 1}
-        in_specs += [pl.BlockSpec(memory_space=pl.ANY)] * 2
-        operands += list(previous)
     count = len(pairs)
-    steps = 6
-    place = (lambda n: (n + jnp.where(n >= 3, 6, 0), 0, 0)) if rest else (lambda n: (3 + n, 0, 0))
+    steps = 3 * (count - 1)
+    place = lambda n: (n, 0, 0)
     wv = zv.shape[1]
     wc = zc.shape[1]
     return pl.pallas_call(
-        functools.partial(density_kernel, count, rest, steps),
+        functools.partial(density_kernel, count, steps),
         grid=(steps,),
         in_specs=in_specs,
         out_specs=[
             pl.BlockSpec((48, 16, wv), place),
             pl.BlockSpec((48, 16, wc), place),
-            pl.BlockSpec((min(2 * count, WIN), 128), lambda n: (0, 0)),
+            pl.BlockSpec((WIN, 128), lambda n: (0, 0)),
         ],
         out_shape=[
             jax.ShapeDtypeStruct((TOTAL, 16, wv), bf16),
             jax.ShapeDtypeStruct((TOTAL, 16, wc), bf16),
-            jax.ShapeDtypeStruct((min(2 * count, WIN), 128), jnp.int32),
+            jax.ShapeDtypeStruct((WIN, 128), jnp.int32),
         ],
         scratch_shapes=[
-            pltpu.VMEM((2 * count * KB, 16, 1024), f32),
+            pltpu.VMEM((WIN * KB, 16, 1024), f32),
             pltpu.VMEM(((2 * count - 1) * 3, 2, 2, 8, 1024), f32),
             pltpu.VMEM((384, 2048), bf16),
             pltpu.VMEM((384, 2048), bf16),
             pltpu.VMEM((384, 2048), bf16),
             pltpu.VMEM((384, 2048), bf16),
         ],
-        input_output_aliases=aliases,
         compiler_params=pltpu.CompilerParams(vmem_limit_bytes=VMEM_LIMIT),
         cost_estimate=pl.CostEstimate(
             flops=2 * steps * 48 * 16 * 2048 * (wv + wc), bytes_accessed=steps * 3 * 2**20, transcendentals=0
@@ -357,18 +350,16 @@
     zc = zeta_matrix(lax.dynamic_index_in_dim(halves, part // 2, 0, keepdims=False))
     pieces = jnp.transpose(screened.reshape(SLOTS, 2, 4, WIN, 128), (3, 0, 1, 2, 4))
     pieces = jnp.concatenate([pieces, pieces], axis=0)
-    pieces = pieces + message[0, 0] * 0
+    pieces = pieces + following[0, 0] * 0
     line = 2 * WIN
     near_groups = [[x * line + s for s in range(line)] for x in range(ka_count // line)]
     x_groups = [[x * line + s for x in range(ka_count // line)] for s in range(line)]
     pieces = lax.all_to_all(pieces, "ka", 0, 0, axis_index_groups=near_groups, tiled=True)
     rows = jnp.transpose(pieces, (1, 2, 0, 3, 4)).reshape(SLOTS, 2, 4 * line, 128)
     w = lax.all_gather(rows, "ka", axis_index_groups=x_groups)
-    zero = rows[0, 0, 0, 0] * 0
-    ahead2 = from_behind(ahead + zero, "ka", -2)
-    behind2 = from_behind(behind + zero, "ka", 2)
-    mv, mc, _ = densities((behind, here, ahead), False, zv, zc, None)
-    mv, mc, words = densities((behind2, behind, here, ahead, ahead2), True, zv, zc, (mv, mc))
+    ahead2 = from_behind(ahead, "ka", -2)
+    behind2 = from_behind(behind, "ka", 2)
+    mv, mc, words = densities((behind2, behind, here, ahead, ahead2), zv, zc)
     order, slot_of, used = schedule(words[:, :PAIRS].reshape(TOTAL))
     partial = apply_screened(order, slot_of, used, ga_word, mv, mc, w)
     arrived = lax.ppermute(partial[2:].astype(bf16), "ga", [(0, 1), (1, 0), (2, 3), (3, 2)])

time: 172 us -> 181 us (1.052)
  waiting for transfers between devices: 54.1 us -> 63.2 us
  starting transfers between devices: 25.8 us -> 33 us
  Pallas kernels: 57.9 us -> 54.2 us
  local copies, waits for them, and re-layouts: 12.2 us -> 9.75 us
    ppermute x10, waiting for transfers between devices: 42.6 us -> 51.6 us  [from_behind(): return lax.ppermute(x, axis, [(i, (i + by) % count) for i in range(count)])]
    ppermute x10, starting transfers between devices: 13.8 us -> 20.2 us  [from_behind(): return lax.ppermute(x, axis, [(i, (i + by) % count) for i in range(count)])]
    pallas_call x2 -> x1, Pallas kernels: 39.9 us -> 36.2 us  [densities(): pl.pallas_call(functools.partial(density_kernel, count, steps), grid=(ste...]
  transfers between devices with their start and end apart: 15 -> 15, of which waited for: 9 -> 9; matrix products, arithmetic and copies ran while one was open for 9% -> 7% of each run, Pallas kernels for 23% -> 20%
where the time goes in v6:
time: 181 us; the launch traced here: 180 us
  waiting for transfers between devices  63.2 us (35%)
  Pallas kernels  54.2 us (30%)
  starting transfers between devices  33 us (18%)
  between operations  14.4 us (8%)
  local copies, waits for them, and re-layouts  9.75 us (5%)
  other arithmetic  5.77 us (3%)
    ppermute x10, waiting for transfers between devices, from_behind(): return lax.ppermute(x, axis, [(i, (i + by) % count) for i in range(count)])  51.6 us
    pallas_call x1, Pallas kernels, densities(): pl.pallas_call(functools.partial(density_kernel, count, steps), grid=(ste...  36.2 us
    ppermute x10, starting transfers between devices, from_behind(): return lax.ppermute(x, axis, [(i, (i + by) % count) for i in range(count)])  20.2 us
    pallas_call x1, Pallas kernels, apply_screened(): pl.pallas_call(apply_kernel, in_specs=[smem] * 4 + [pl.BlockSpec(memory_s...  16.3 us
    all_to_all x1, starting transfers between devices, body(): lax.all_to_all(pieces, 'ka', 0, 0, axis_index_groups=near_groups, tiled=T...  10.3 us
    ppermute x1, waiting for transfers between devices, body(): lax.ppermute(other, 'ga', [(0, 2), (2, 0), (1, 3), (3, 1)]).astype(f32)  9.3 us
  transfers between devices with their start and end apart: 15, of which 9 were waited for; matrix products, arithmetic and copies ran while one was open for 7% of the time, Pallas kernels for 20%

profile of v6, /device:TPU:40, one launch (start us, length us, event | category | flops | bytes accessed | tf_op | source)
XLA Modules:
  0.0 180.2 jit_solution(7021998702906997398)
XLA Ops:
  6.5 2.2 %constant_dynamic-slice_fusion.1 = bf16[1024,2,128]{2,1,0:T(2,128)(2,1)} fusion(bf16[1024,2,256]{2,1,0:T(2,128)(2,1)} %param.5, s32[]{:T(128)S(6)} %select_n.41), kind=kLoop, calls=%fused_computation.58 | loop fusion | bytes 1048580 | tf_op jit(solution)/shard_map/dynamic_slice | solution.py:348
  8.8 0.7 convert_element_type.67
  9.8 1.0 fusion.13
  11.4 7.6 %collective-permute-done = bf16[112,1024]{1,0:T(8,128)(2,1)S(1)} collective-permute-done((bf16[112,1024]{1,0:T(8,128)(2,1)S(1)}, bf16[112,1024]{1,0:T(8,128)(2,1)S(1)}, u32[]{:S(2)}, u32[]{:S(2)}) %collective-permute-start) | collective-permute-done | bytes 229408 | tf_op jit(solution)/shard_map/ppermute | solution.py:26
  19.1 0.5 slice.131
  20.5 1.1 copy.29
  21.6 10.3 %all-to-all-start = ((bf16[16,22,2,4,128]{4,3,2,1,0:T(4,128)(2,1)}), bf16[16,22,2,4,128]{4,3,2,1,0:T(4,128)(2,1)S(1)}, u32[]{:S(2)}, u32[]{:S(2)}) async-start(bf16[16,22,2,4,128]{4,3,2,1,0:T(4,128)(2,1)} %copy.29), calls=%async_computation | async-start | bytes 1441792 | tf_op jit(solution)/shard_map/all_to_all | solution.py:357
  32.0 1.5 fusion.17
  33.5 0.9 copy.39
  34.4 1.5 collective-permute-start.1
  35.9 0.6 collective-permute-start.3
  36.6 1.5 maximum_maximum_fusion.refs_5_
  38.1 19.0 %collective-permute-done.1.refs_1_ = bf16[2,112,1024]{2,1,0:T(8,128)(2,1)S(1)} collective-permute-done((bf16[2,112,1024]{2,1,0:T(8,128)(2,1)S(1)}, bf16[2,112,1024]{2,1,0:T(8,128)(2,1)S(1)}, u32[]{:S(2)}, u32[]{:S(2)}) %collective-permute-start.1) | collective-permute-done | bytes 458784 | tf_op jit(solution)/shard_map/ppermute | solution.py:26
  57.1 1.5 collective-permute-start.2
  58.7 4.6 %collective-permute-start.4 = (bf16[2,112,1024]{2,1,0:T(8,128)(2,1)S(1)}, bf16[2,112,1024]{2,1,0:T(8,128)(2,1)S(1)}, u32[]{:S(2)}, u32[]{:S(2)}) collective-permute-start(bf16[2,112,1024]{2,1,0:T(8,128)(2,1)S(1)} %collective-permute-done.3.refs_3_), channel_id=1, source_target_pairs={{0,248},{4,252},{8,0},{12,4},{16,8},{20,12},{24,16},{28,20},{32,24... | collective-permute-start | bytes 1376264 | tf_op jit(solution)/shard_map/ppermute | solution.py:26
  63.2 1.3 copy.30
  64.6 1.4 constant_dynamic-slice_fusion
  66.3 6.4 %collective-permute-done.2.refs_0_ = bf16[2,112,1024]{2,1,0:T(8,128)(2,1)S(1)} collective-permute-done((bf16[2,112,1024]{2,1,0:T(8,128)(2,1)S(1)}, bf16[2,112,1024]{2,1,0:T(8,128)(2,1)S(1)}, u32[]{:S(2)}, u32[]{:S(2)}) %collective-permute-start.2) | collective-permute-done | bytes 458784 | tf_op jit(solution)/shard_map/ppermute | solution.py:26
  72.7 36.2 %densities.1 = (bf16[576,16,512]{2,1,0:T(8,128)(2,1)}, bf16[576,16,256]{2,1,0:T(8,128)(2,1)}, s32[8,128]{1,0:T(8,128)S(1)}) custom-call(bf16[2,112,1024]{2,1,0:T(8,128)(2,1)S(1)} %collective-permute-done.2.refs_0_, bf16[2,112,1024]{2,1,0:T(8,128)(2,1)S(1)} %collective-permute-done.1.refs_1_, bf16[2,112,1024]{2,1,0:T(8,128)(2,1)S(1)} %pad_maximum_fusion.refs_2_, ...), custom_call_target="tpu_custom_call" | custom-call | flops 28991029248 | bytes 37748736 | tf_op jit(solution)/shard_map/densities/pallas_call | solution.py:134
  109.1 0.6 fusion.15
  110.7 16.3 %apply_screened.1 = f32[4,8,3,56,128]{4,3,2,1,0:T(8,128)S(1)} custom-call(s32[960]{0:T(1024)S(1)} %broadcast_add_fusion.order_ref, s32[60]{0:T(128)S(1)} %broadcast_minimum_fusion.slot_ref, s32[1]{0:T(128)} %bitcast.12.used_ref, s32[1]{0:T(128)} %bitcast.ga_ref, bf16[576,16,512]{2,1,0:T(8,128)(2,1)} %get-tuple-element.9.mv_hbm, ...), custom_call_target="tpu_custom_call" | custom-call | flops 6000000000 | bytes 18874368 | tf_op jit(solution)/shard_map/apply_screened/pallas_call | solution.py:248
  127.2 2.1 %collective-permute-done.5 = bf16[2,8,3,56,128]{4,3,2,1,0:T(8,128)(2,1)S(1)} collective-permute-done((bf16[2,8,3,56,128]{4,3,2,1,0:T(8,128)(2,1)S(1)}, bf16[2,8,3,56,128]{4,3,2,1,0:T(8,128)(2,1)S(1)}, u32[]{:S(2)}, u32[]{:S(2)}) %collective-permute-start.5) | collective-permute-done | bytes 688160 | tf_op jit(solution)/shard_map/ppermute | solution.py:365
  129.4 2.4 %collective-permute-start.6 = (bf16[8,3,56,128]{3,2,1,0:T(8,128)(2,1)S(1)}, bf16[8,3,56,128]{3,2,1,0:T(8,128)(2,1)S(1)}, u32[]{:S(2)}, u32[]{:S(2)}) collective-permute-start(bf16[8,3,56,128]{3,2,1,0:T(8,128)(2,1)S(1)} %fusion.5), channel_id=1, source_target_pairs={{0,2},{2,0},{1,3},{3,1},{4,6},{6,4},{5,7},{7,5},{8,10},{10,8},{9,1... | collective-permute-start | bytes 1032200 | tf_op jit(solution)/shard_map/ppermute | solution.py:368
  131.8 9.3 %collective-permute-done.6 = bf16[8,3,56,128]{3,2,1,0:T(8,128)(2,1)S(1)} collective-permute-done((bf16[8,3,56,128]{3,2,1,0:T(8,128)(2,1)S(1)}, bf16[8,3,56,128]{3,2,1,0:T(8,128)(2,1)S(1)}, u32[]{:S(2)}, u32[]{:S(2)}) %collective-permute-start.6) | collective-permute-done | bytes 344096 | tf_op jit(solution)/shard_map/ppermute | solution.py:368
  141.4 0.6 collective-permute-start.9
  142.1 2.4 %collective-permute-start.7 = (bf16[3,3,56,128]{3,2,1,0:T(8,128)(2,1)S(1)}, bf16[3,3,56,128]{3,2,1,0:T(8,128)(2,1)S(1)}, u32[]{:S(2)}, u32[]{:S(2)}) collective-permute-start(bf16[3,3,56,128]{3,2,1,0:T(8,128)(2,1)S(1)} %pad_maximum_fusion.1), channel_id=1, source_target_pairs={{0,4},{4,8},{8,12},{12,16},{16,20},{20,24},{24,28},{28,32},{32,36}... | collective-permute-start | bytes 387080 | tf_op jit(solution)/shard_map/ppermute | solution.py:26
  144.7 2.2 %collective-permute-done.9 = bf16[2,3,56,128]{3,2,1,0:T(8,128)(2,1)S(1)} collective-permute-done((bf16[2,3,56,128]{3,2,1,0:T(8,128)(2,1)S(1)}, bf16[2,3,56,128]{3,2,1,0:T(8,128)(2,1)S(1)}, u32[]{:S(2)}, u32[]{:S(2)}) %collective-permute-start.9) | collective-permute-done | bytes 86048 | tf_op jit(solution)/shard_map/ppermute | solution.py:26
  146.9 7.0 %collective-permute-done.8 = bf16[2,3,56,128]{3,2,1,0:T(8,128)(2,1)S(1)} collective-permute-done((bf16[2,3,56,128]{3,2,1,0:T(8,128)(2,1)S(1)}, bf16[2,3,56,128]{3,2,1,0:T(8,128)(2,1)S(1)}, u32[]{:S(2)}, u32[]{:S(2)}) %collective-permute-start.8) | collective-permute-done | bytes 86048 | tf_op jit(solution)/shard_map/ppermute | solution.py:26
  154.0 8.3 %collective-permute-start.10 = (f32[3,56,128]{2,1,0:T(8,128)S(1)}, f32[3,56,128]{2,1,0:T(8,128)S(1)}, u32[]{:S(2)}, u32[]{:S(2)}) collective-permute-start(f32[3,56,128]{2,1,0:T(8,128)S(1)} %get-tuple-element.15), channel_id=1, source_target_pairs={{0,240},{4,244},{8,248},{12,252},{16,0},{20,4},{24,8},{28,12},{32,... | collective-permute-start | bytes 258056 | tf_op jit(solution)/shard_map/ppermute | solution.py:26
  162.3 2.1 %collective-permute-done.10 = f32[3,56,128]{2,1,0:T(8,128)S(1)} collective-permute-done((f32[3,56,128]{2,1,0:T(8,128)S(1)}, f32[3,56,128]{2,1,0:T(8,128)S(1)}, u32[]{:S(2)}, u32[]{:S(2)}) %collective-permute-start.10) | collective-permute-done | bytes 86048 | tf_op jit(solution)/shard_map/ppermute | solution.py:26
  164.4 7.2 %collective-permute-done.11 = f32[3,56,128]{2,1,0:T(8,128)S(1)} collective-permute-done((f32[3,56,128]{2,1,0:T(8,128)S(1)}, f32[3,56,128]{2,1,0:T(8,128)S(1)}, u32[]{:S(2)}, u32[]{:S(2)}) %collective-permute-start.11) | collective-permute-done | bytes 86048 | tf_op jit(solution)/shard_map/ppermute | solution.py:26
  171.7 1.7 arrange.1
  (63 shorter events, 3.6 us)
Async XLA Ops:
  6.5 4.7 %copy-start.2 = (bf16[22,2,4,1024]{3,2,1,0:T(4,128)(2,1)S(1)}, bf16[22,2,4,1024]{3,2,1,0:T(4,128)(2,1)}, u32[]{:S(2)}) copy-start(bf16[22,2,4,1024]{3,2,1,0:T(4,128)(2,1)} %param.6) | copy-start | bytes 1081348
  6.5 58.0 %all-gather.6.cloned.1.call-start = ((), (), s32[]{:S(2)}) async-start(), calls=%async_computation.2 | async-start | bytes 2621440 | tf_op jit(solution)/shard_map/all_gather | solution.py:349
  10.7 8.3 %collective-permute-start = (bf16[112,1024]{1,0:T(8,128)(2,1)S(1)}, bf16[112,1024]{1,0:T(8,128)(2,1)S(1)}, u32[]{:S(2)}, u32[]{:S(2)}) collective-permute-start(bf16[112,1024]{1,0:T(8,128)(2,1)S(1)} %get-tuple-element.29), channel_id=1, source_target_pairs={{0,252},{4,0},{8,4},{12,8},{16,12},{20,16},{24,20},{28,24},{32,28}... | collective-permute-start | bytes 688136 | tf_op jit(solution)/shard_map/ppermute | solution.py:26
  11.4 20.5 %copy-start = (bf16[1024,2,256]{2,1,0:T(2,128)(2,1)S(1)}, bf16[1024,2,256]{2,1,0:T(2,128)(2,1)}, u32[]{:S(2)}) copy-start(bf16[1024,2,256]{2,1,0:T(2,128)(2,1)} %param.5) | copy-start | bytes 3145732
  19.1 12.9 %copy-start.3 = (bf16[112,1024]{1,0:T(8,128)(2,1)}, bf16[112,1024]{1,0:T(8,128)(2,1)S(1)}, u32[]{:S(2)}) copy-start(bf16[112,1024]{1,0:T(8,128)(2,1)S(1)} %collective-permute-done) | copy-start | bytes 688132
  21.6 41.7 %all-to-all-start = ((bf16[16,22,2,4,128]{4,3,2,1,0:T(4,128)(2,1)}), bf16[16,22,2,4,128]{4,3,2,1,0:T(4,128)(2,1)S(1)}, u32[]{:S(2)}, u32[]{:S(2)}) async-start(bf16[16,22,2,4,128]{4,3,2,1,0:T(4,128)(2,1)} %copy.29), calls=%async_computation | async-start | bytes 1441792 | tf_op jit(solution)/shard_map/all_to_all | solution.py:357
  31.9 78.8 %all-gather.4.cloned.1.call-start = ((), (), s32[]{:S(2)}) async-start(), calls=%async_computation.1 | async-start | bytes 3604480 | tf_op jit(solution)/shard_map/all_gather | solution.py:359
  31.9 2.4 %copy-start.4 = (bf16[112,1024]{1,0:T(8,128)(2,1)S(1)}, bf16[112,1024]{1,0:T(8,128)(2,1)}, u32[]{:S(2)}) copy-start(bf16[112,1024]{1,0:T(8,128)(2,1)} %copy-done.3) | copy-start | bytes 688132
  34.3 2.2 %copy-start.1 = (bf16[1024,1,256]{2,0,1:T(8,128)(2,1)S(1)}, bf16[1024,1,256]{2,0,1:T(8,128)(2,1)}, u32[]{:S(2)}) copy-start(bf16[1024,1,256]{2,0,1:T(8,128)(2,1)} %copy.39) | copy-start | bytes 1572868
  34.4 22.7 %collective-permute-start.1 = (bf16[2,112,1024]{2,1,0:T(8,128)(2,1)S(1)}, bf16[2,112,1024]{2,1,0:T(8,128)(2,1)S(1)}, u32[]{:S(2)}, u32[]{:S(2)}) collective-permute-start(bf16[2,112,1024]{2,1,0:T(8,128)(2,1)S(1)} %pad_maximum_fusion.refs_2_), channel_id=1, source_target_pairs={{0,8},{4,12},{8,16},{12,20},{16,24},{20,28},{24,32},{28,36},{32,40... | collective-permute-start | bytes 1376264 | tf_op jit(solution)/shard_map/ppermute | solution.py:26
  35.9 22.7 %collective-permute-start.3 = (bf16[2,112,1024]{2,1,0:T(8,128)(2,1)S(1)}, bf16[2,112,1024]{2,1,0:T(8,128)(2,1)S(1)}, u32[]{:S(2)}, u32[]{:S(2)}) collective-permute-start(bf16[2,112,1024]{2,1,0:T(8,128)(2,1)S(1)} %pad_maximum_fusion.refs_2_), channel_id=1, source_target_pairs={{0,248},{4,252},{8,0},{12,4},{16,8},{20,12},{24,16},{28,20},{32,24... | collective-permute-start | bytes 1376264 | tf_op jit(solution)/shard_map/ppermute | solution.py:26
  57.1 15.5 %collective-permute-start.2 = (bf16[2,112,1024]{2,1,0:T(8,128)(2,1)S(1)}, bf16[2,112,1024]{2,1,0:T(8,128)(2,1)S(1)}, u32[]{:S(2)}, u32[]{:S(2)}) collective-permute-start(bf16[2,112,1024]{2,1,0:T(8,128)(2,1)S(1)} %collective-permute-done.1.refs_1_), channel_id=1, source_target_pairs={{0,8},{4,12},{8,16},{12,20},{16,24},{20,28},{24,32},{28,36},{32,40... | collective-permute-start | bytes 1376264 | tf_op jit(solution)/shard_map/ppermute | solution.py:26
  58.7 14.0 %collective-permute-start.4 = (bf16[2,112,1024]{2,1,0:T(8,128)(2,1)S(1)}, bf16[2,112,1024]{2,1,0:T(8,128)(2,1)S(1)}, u32[]{:S(2)}, u32[]{:S(2)}) collective-permute-start(bf16[2,112,1024]{2,1,0:T(8,128)(2,1)S(1)} %collective-permute-done.3.refs_3_), channel_id=1, source_target_pairs={{0,248},{4,252},{8,0},{12,4},{16,8},{20,12},{24,16},{28,20},{32,24... | collective-permute-start | bytes 1376264 | tf_op jit(solution)/shard_map/ppermute | solution.py:26
  127.1 2.2 %collective-permute-start.5 = (bf16[2,8,3,56,128]{4,3,2,1,0:T(8,128)(2,1)S(1)}, bf16[2,8,3,56,128]{4,3,2,1,0:T(8,128)(2,1)S(1)}, u32[]{:S(2)}, u32[]{:S(2)}) collective-permute-start(bf16[2,8,3,56,128]{4,3,2,1,0:T(8,128)(2,1)S(1)} %slice.201), channel_id=1, source_target_pairs={{0,1},{1,0},{2,3},{3,2},{4,5},{5,4},{6,7},{7,6},{8,9},{9,8},{10,11... | collective-permute-start | bytes 2064392 | tf_op jit(solution)/shard_map/ppermute | solution.py:365
  129.4 11.7 %collective-permute-start.6 = (bf16[8,3,56,128]{3,2,1,0:T(8,128)(2,1)S(1)}, bf16[8,3,56,128]{3,2,1,0:T(8,128)(2,1)S(1)}, u32[]{:S(2)}, u32[]{:S(2)}) collective-permute-start(bf16[8,3,56,128]{3,2,1,0:T(8,128)(2,1)S(1)} %fusion.5), channel_id=1, source_target_pairs={{0,2},{2,0},{1,3},{3,1},{4,6},{6,4},{5,7},{7,5},{8,10},{10,8},{9,1... | collective-permute-start | bytes 1032200 | tf_op jit(solution)/shard_map/ppermute | solution.py:368
  141.4 5.5 %collective-permute-start.9 = (bf16[2,3,56,128]{3,2,1,0:T(8,128)(2,1)S(1)}, bf16[2,3,56,128]{3,2,1,0:T(8,128)(2,1)S(1)}, u32[]{:S(2)}, u32[]{:S(2)}) collective-permute-start(bf16[2,3,56,128]{3,2,1,0:T(8,128)(2,1)S(1)} %pad_maximum_fusion.3), channel_id=1, source_target_pairs={{0,252},{4,0},{8,4},{12,8},{16,12},{20,16},{24,20},{28,24},{32,28}... | collective-permute-start | bytes 258056 | tf_op jit(solution)/shard_map/ppermute | solution.py:26
  142.1 11.8 %collective-permute-start.7 = (bf16[3,3,56,128]{3,2,1,0:T(8,128)(2,1)S(1)}, bf16[3,3,56,128]{3,2,1,0:T(8,128)(2,1)S(1)}, u32[]{:S(2)}, u32[]{:S(2)}) collective-permute-start(bf16[3,3,56,128]{3,2,1,0:T(8,128)(2,1)S(1)} %pad_maximum_fusion.1), channel_id=1, source_target_pairs={{0,4},{4,8},{8,12},{12,16},{16,20},{20,24},{24,28},{28,32},{32,36}... | collective-permute-start | bytes 387080 | tf_op jit(solution)/shard_map/ppermute | solution.py:26
  144.5 9.4 %collective-permute-start.8 = (bf16[2,3,56,128]{3,2,1,0:T(8,128)(2,1)S(1)}, bf16[2,3,56,128]{3,2,1,0:T(8,128)(2,1)S(1)}, u32[]{:S(2)}, u32[]{:S(2)}) collective-permute-start(bf16[2,3,56,128]{3,2,1,0:T(8,128)(2,1)S(1)} %pad_maximum_fusion.2), channel_id=1, source_target_pairs={{0,8},{4,12},{8,16},{12,20},{16,24},{20,28},{24,32},{28,36},{32,40... | collective-permute-start | bytes 258056 | tf_op jit(solution)/shard_map/ppermute | solution.py:26
  154.0 10.4 %collective-permute-start.10 = (f32[3,56,128]{2,1,0:T(8,128)S(1)}, f32[3,56,128]{2,1,0:T(8,128)S(1)}, u32[]{:S(2)}, u32[]{:S(2)}) collective-permute-start(f32[3,56,128]{2,1,0:T(8,128)S(1)} %get-tuple-element.15), channel_id=1, source_target_pairs={{0,240},{4,244},{8,248},{12,252},{16,0},{20,4},{24,8},{28,12},{32,... | collective-permute-start | bytes 258056 | tf_op jit(solution)/shard_map/ppermute | solution.py:26
  162.3 9.3 %collective-permute-start.11 = (f32[3,56,128]{2,1,0:T(8,128)S(1)}, f32[3,56,128]{2,1,0:T(8,128)S(1)}, u32[]{:S(2)}, u32[]{:S(2)}) collective-permute-start(f32[3,56,128]{2,1,0:T(8,128)S(1)} %get-tuple-element.16), channel_id=1, source_target_pairs={{0,16},{4,20},{8,24},{12,28},{16,32},{20,36},{24,40},{28,44},{32,4... | collective-permute-start | bytes 258056 | tf_op jit(solution)/shard_map/ppermute | solution.py:26
Sparse Core Ops, SparseCore 0:
  9.2 32.6 all-gather.5
  64.7 38.9 all-gather.3

commit v7 on v6

--- a/solution.py
+++ b/solution.py
@@ -350,7 +350,7 @@
     zc = zeta_matrix(lax.dynamic_index_in_dim(halves, part // 2, 0, keepdims=False))
     pieces = jnp.transpose(screened.reshape(SLOTS, 2, 4, WIN, 128), (3, 0, 1, 2, 4))
     pieces = jnp.concatenate([pieces, pieces], axis=0)
-    pieces = pieces + following[0, 0] * 0
+    pieces = pieces + (ahead[0, 0, 0] + behind[0, 0, 0]) * 0
     line = 2 * WIN
     near_groups = [[x * line + s for s in range(line)] for x in range(ka_count // line)]
     x_groups = [[x * line + s for x in range(ka_count // line)] for s in range(line)]
@@ -377,7 +377,7 @@
     low = parts[0] + plus_one[0] + plus_two[0]
     high = parts[8] + plus_one[2] + minus_one[1]
     total = parts[4] + plus_one[1] + plus_two[1] + minus_one[0]
-    total = total + from_behind(low, "ka", -4) + from_behind(high, "ka", 4)
+    total = total + from_behind(low.astype(bf16), "ka", -4).astype(f32) + from_behind(high.astype(bf16), "ka", 4).astype(f32)
     return arrange(ga_word, total)
 
 

time: 181 us -> 178 us (0.983)
  starting transfers between devices: 33 us -> 25.3 us
  waiting for transfers between devices: 63.2 us -> 67 us
    all_to_all x1, waiting for transfers between devices: 0.01 us -> 12.9 us  [body(): lax.all_to_all(pieces, 'ka', 0, 0, axis_index_groups=near_groups, tiled=T...]
    ppermute x10, waiting for transfers between devices: 51.6 us -> 42.5 us  [from_behind(): return lax.ppermute(x, axis, [(i, (i + by) % count) for i in range(count)])]
    ppermute x10, starting transfers between devices: 20.2 us -> 15 us  [from_behind(): return lax.ppermute(x, axis, [(i, (i + by) % count) for i in range(count)])]
    all_to_all x1, starting transfers between devices: 10.3 us -> 7.81 us  [body(): lax.all_to_all(pieces, 'ka', 0, 0, axis_index_groups=near_groups, tiled=T...]
  transfers between devices with their start and end apart: 15 -> 15, of which waited for: 9 -> 11; matrix products, arithmetic and copies ran while one was open for 7% -> 8% of each run, Pallas kernels for 20% -> 20%
where the time goes in v7:
time: 178 us
  waiting for transfers between devices  67 us (38%)
  Pallas kernels  54.3 us (31%)
  starting transfers between devices  25.3 us (14%)
  between operations  15.1 us (8%)
  local copies, waits for them, and re-layouts  10.6 us (6%)
  other arithmetic  5.76 us (3%)
    ppermute x10, waiting for transfers between devices, from_behind(): return lax.ppermute(x, axis, [(i, (i + by) % count) for i in range(count)])  42.5 us
    pallas_call x1, Pallas kernels, densities(): pl.pallas_call(functools.partial(density_kernel, count, steps), grid=(ste...  36.2 us
    pallas_call x1, Pallas kernels, apply_screened(): pl.pallas_call(apply_kernel, in_specs=[smem] * 4 + [pl.BlockSpec(memory_s...  16.4 us
    ppermute x10, starting transfers between devices, from_behind(): return lax.ppermute(x, axis, [(i, (i + by) % count) for i in range(count)])  15 us
    all_to_all x1, waiting for transfers between devices, body(): lax.all_to_all(pieces, 'ka', 0, 0, axis_index_groups=near_groups, tiled=T...  12.9 us
    ppermute x1, waiting for transfers between devices, body(): lax.ppermute(other, 'ga', [(0, 2), (2, 0), (1, 3), (3, 1)]).astype(f32)  9.36 us
    all_to_all x1, starting transfers between devices, body(): lax.all_to_all(pieces, 'ka', 0, 0, axis_index_groups=near_groups, tiled=T...  7.81 us
  transfers between devices with their start and end apart: 15, of which 11 were waited for; matrix products, arithmetic and copies ran while one was open for 8% of the time, Pallas kernels for 20%

profile of v7, /device:TPU:40, one launch (start us, length us, event | category | flops | bytes accessed | tf_op | source)
XLA Modules:
  0.0 177.9 jit_solution(14205351219596488621)
XLA Ops:
  6.5 2.2 %constant_dynamic-slice_fusion.1 = bf16[1024,2,128]{2,1,0:T(2,128)(2,1)} fusion(bf16[1024,2,256]{2,1,0:T(2,128)(2,1)} %param.5, s32[]{:T(128)S(6)} %select_n.41), kind=kLoop, calls=%fused_computation.60 | loop fusion | bytes 1048580 | tf_op jit(solution)/shard_map/dynamic_slice | solution.py:348
  8.8 0.7 convert_element_type.85
  9.8 1.0 fusion.15
  11.3 7.8 %collective-permute-done = bf16[112,1024]{1,0:T(8,128)(2,1)S(1)} collective-permute-done((bf16[112,1024]{1,0:T(8,128)(2,1)S(1)}, bf16[112,1024]{1,0:T(8,128)(2,1)S(1)}, u32[]{:S(2)}, u32[]{:S(2)}) %collective-permute-start) | collective-permute-done | bytes 229408 | tf_op jit(solution)/shard_map/ppermute | solution.py:26
  19.3 1.9 %collective-permute-start.1 = (bf16[2,112,1024]{2,1,0:T(8,128)(2,1)S(1)}, bf16[2,112,1024]{2,1,0:T(8,128)(2,1)S(1)}, u32[]{:S(2)}, u32[]{:S(2)}) collective-permute-start(bf16[2,112,1024]{2,1,0:T(8,128)(2,1)S(1)} %pad_maximum_fusion.refs_2_), channel_id=1, source_target_pairs={{0,8},{4,12},{8,16},{12,20},{16,24},{20,28},{24,32},{28,36},{32,40... | collective-permute-start | bytes 1376264 | tf_op jit(solution)/shard_map/ppermute | solution.py:26
  21.4 9.4 %collective-permute-done.3.refs_3_ = bf16[2,112,1024]{2,1,0:T(8,128)(2,1)S(1)} collective-permute-done((bf16[2,112,1024]{2,1,0:T(8,128)(2,1)S(1)}, bf16[2,112,1024]{2,1,0:T(8,128)(2,1)S(1)}, u32[]{:S(2)}, u32[]{:S(2)}) %collective-permute-start.3) | collective-permute-done | bytes 458784 | tf_op jit(solution)/shard_map/ppermute | solution.py:26
  31.3 8.8 %collective-permute-done.1.refs_1_ = bf16[2,112,1024]{2,1,0:T(8,128)(2,1)S(1)} collective-permute-done((bf16[2,112,1024]{2,1,0:T(8,128)(2,1)S(1)}, bf16[2,112,1024]{2,1,0:T(8,128)(2,1)S(1)}, u32[]{:S(2)}, u32[]{:S(2)}) %collective-permute-start.1) | collective-permute-done | bytes 458784 | tf_op jit(solution)/shard_map/ppermute | solution.py:26
  40.0 0.6 slice.136
  42.1 1.1 copy.29
  43.3 7.8 %all-to-all-start = ((bf16[16,22,2,4,128]{4,3,2,1,0:T(4,128)(2,1)}), bf16[16,22,2,4,128]{4,3,2,1,0:T(4,128)(2,1)}, u32[]{:S(2)}, u32[]{:S(2)}) async-start(bf16[16,22,2,4,128]{4,3,2,1,0:T(4,128)(2,1)} %copy.29), calls=%async_computation | async-start | bytes 1441792 | tf_op jit(solution)/shard_map/all_to_all | solution.py:357
  51.2 1.5 fusion.19
  52.9 1.5 maximum_maximum_fusion.refs_5_
  54.4 1.5 collective-permute-start.2
  55.9 0.6 collective-permute-start.4
  56.4 12.9 %all-to-all-done = bf16[16,22,2,4,128]{4,3,2,1,0:T(4,128)(2,1)} async-done(((bf16[16,22,2,4,128]{4,3,2,1,0:T(4,128)(2,1)}), bf16[16,22,2,4,128]{4,3,2,1,0:T(4,128)(2,1)}, u32[]{:S(2)}, u32[]{:S(2)}) %all-to-all-start) | async-done | bytes 720928 | tf_op jit(solution)/shard_map/all_to_all | solution.py:357
  69.3 2.4 %copy.30 = bf16[22,2,16,4,128]{4,3,2,1,0:T(4,128)(2,1)} copy(bf16[22,2,16,4,128]{4,3,1,0,2:T(4,128)(2,1)} %bitcast.15) | data formatting | bytes 1441792 | tf_op jit(solution)/shard_map/transpose | solution.py:358
  71.7 1.4 constant_dynamic-slice_fusion
  73.4 3.1 %collective-permute-done.2.refs_0_ = bf16[2,112,1024]{2,1,0:T(8,128)(2,1)S(1)} collective-permute-done((bf16[2,112,1024]{2,1,0:T(8,128)(2,1)S(1)}, bf16[2,112,1024]{2,1,0:T(8,128)(2,1)S(1)}, u32[]{:S(2)}, u32[]{:S(2)}) %collective-permute-start.2) | collective-permute-done | bytes 458784 | tf_op jit(solution)/shard_map/ppermute | solution.py:26
  76.5 36.2 %densities.1 = (bf16[576,16,512]{2,1,0:T(8,128)(2,1)}, bf16[576,16,256]{2,1,0:T(8,128)(2,1)}, s32[8,128]{1,0:T(8,128)S(1)}) custom-call(bf16[2,112,1024]{2,1,0:T(8,128)(2,1)S(1)} %collective-permute-done.2.refs_0_, bf16[2,112,1024]{2,1,0:T(8,128)(2,1)S(1)} %collective-permute-done.1.refs_1_, bf16[2,112,1024]{2,1,0:T(8,128)(2,1)S(1)} %pad_maximum_fusion.refs_2_, ...), custom_call_target="tpu_custom_call" | custom-call | flops 28991029248 | bytes 37748736 | tf_op jit(solution)/shard_map/densities/pallas_call | solution.py:134
  112.9 0.6 fusion.17
  114.5 16.4 %apply_screened.1 = f32[4,8,3,56,128]{4,3,2,1,0:T(8,128)S(1)} custom-call(s32[960]{0:T(1024)S(1)} %broadcast_add_fusion.order_ref, s32[60]{0:T(128)S(1)} %broadcast_minimum_fusion.slot_ref, s32[1]{0:T(128)} %bitcast.12.used_ref, s32[1]{0:T(128)} %bitcast.ga_ref, bf16[576,16,512]{2,1,0:T(8,128)(2,1)} %get-tuple-element.9.mv_hbm, ...), custom_call_target="tpu_custom_call" | custom-call | flops 6000000000 | bytes 18874368 | tf_op jit(solution)/shard_map/apply_screened/pallas_call | solution.py:248
  131.1 2.1 %collective-permute-done.5 = bf16[2,8,3,56,128]{4,3,2,1,0:T(8,128)(2,1)S(1)} collective-permute-done((bf16[2,8,3,56,128]{4,3,2,1,0:T(8,128)(2,1)S(1)}, bf16[2,8,3,56,128]{4,3,2,1,0:T(8,128)(2,1)S(1)}, u32[]{:S(2)}, u32[]{:S(2)}) %collective-permute-start.5) | collective-permute-done | bytes 688160 | tf_op jit(solution)/shard_map/ppermute | solution.py:365
  133.3 2.3 %collective-permute-start.6 = (bf16[8,3,56,128]{3,2,1,0:T(8,128)(2,1)S(1)}, bf16[8,3,56,128]{3,2,1,0:T(8,128)(2,1)S(1)}, u32[]{:S(2)}, u32[]{:S(2)}) collective-permute-start(bf16[8,3,56,128]{3,2,1,0:T(8,128)(2,1)S(1)} %fusion.5), channel_id=1, source_target_pairs={{0,2},{2,0},{1,3},{3,1},{4,6},{6,4},{5,7},{7,5},{8,10},{10,8},{9,1... | collective-permute-start | bytes 1032200 | tf_op jit(solution)/shard_map/ppermute | solution.py:368
  135.6 9.4 %collective-permute-done.6 = bf16[8,3,56,128]{3,2,1,0:T(8,128)(2,1)S(1)} collective-permute-done((bf16[8,3,56,128]{3,2,1,0:T(8,128)(2,1)S(1)}, bf16[8,3,56,128]{3,2,1,0:T(8,128)(2,1)S(1)}, u32[]{:S(2)}, u32[]{:S(2)}) %collective-permute-start.6) | collective-permute-done | bytes 344096 | tf_op jit(solution)/shard_map/ppermute | solution.py:368
  145.3 0.8 collective-permute-start.7
  146.1 3.1 %collective-permute-start.8 = (bf16[2,3,56,128]{3,2,1,0:T(8,128)(2,1)S(1)}, bf16[2,3,56,128]{3,2,1,0:T(8,128)(2,1)S(1)}, u32[]{:S(2)}, u32[]{:S(2)}) collective-permute-start(bf16[2,3,56,128]{3,2,1,0:T(8,128)(2,1)S(1)} %pad_maximum_fusion.2), channel_id=1, source_target_pairs={{0,8},{4,12},{8,16},{12,20},{16,24},{20,28},{24,32},{28,36},{32,40... | collective-permute-start | bytes 258056 | tf_op jit(solution)/shard_map/ppermute | solution.py:26
  149.4 2.7 %collective-permute-done.8 = bf16[2,3,56,128]{3,2,1,0:T(8,128)(2,1)S(1)} collective-permute-done((bf16[2,3,56,128]{3,2,1,0:T(8,128)(2,1)S(1)}, bf16[2,3,56,128]{3,2,1,0:T(8,128)(2,1)S(1)}, u32[]{:S(2)}, u32[]{:S(2)}) %collective-permute-start.8) | collective-permute-done | bytes 86048 | tf_op jit(solution)/shard_map/ppermute | solution.py:26
  152.0 2.6 %collective-permute-done.9 = bf16[2,3,56,128]{3,2,1,0:T(8,128)(2,1)S(1)} collective-permute-done((bf16[2,3,56,128]{3,2,1,0:T(8,128)(2,1)S(1)}, bf16[2,3,56,128]{3,2,1,0:T(8,128)(2,1)S(1)}, u32[]{:S(2)}, u32[]{:S(2)}) %collective-permute-start.9) | collective-permute-done | bytes 86048 | tf_op jit(solution)/shard_map/ppermute | solution.py:26
  154.8 6.4 %collective-permute-start.10 = (bf16[3,56,128]{2,1,0:T(8,128)(2,1)S(1)}, bf16[3,56,128]{2,1,0:T(8,128)(2,1)S(1)}, u32[]{:S(2)}, u32[]{:S(2)}) collective-permute-start(bf16[3,56,128]{2,1,0:T(8,128)(2,1)S(1)} %get-tuple-element.15), channel_id=1, source_target_pairs={{0,240},{4,244},{8,248},{12,252},{16,0},{20,4},{24,8},{28,12},{32,... | collective-permute-start | bytes 129032 | tf_op jit(solution)/shard_map/ppermute | solution.py:26
  161.2 1.7 collective-permute-done.10
  162.9 6.5 %collective-permute-done.11 = bf16[3,56,128]{2,1,0:T(8,128)(2,1)S(1)} collective-permute-done((bf16[3,56,128]{2,1,0:T(8,128)(2,1)S(1)}, bf16[3,56,128]{2,1,0:T(8,128)(2,1)S(1)}, u32[]{:S(2)}, u32[]{:S(2)}) %collective-permute-start.11) | collective-permute-done | bytes 43040 | tf_op jit(solution)/shard_map/ppermute | solution.py:26
  169.4 1.7 arrange.1
  (58 shorter events, 4.3 us)
Async XLA Ops:
  6.5 14.7 %copy-start.1 = (bf16[22,2,4,1024]{3,2,1,0:T(4,128)(2,1)S(1)}, bf16[22,2,4,1024]{3,2,1,0:T(4,128)(2,1)}, u32[]{:S(2)}) copy-start(bf16[22,2,4,1024]{3,2,1,0:T(4,128)(2,1)} %param.6) | copy-start | bytes 1081348
  6.5 65.2 %all-gather.6.cloned.1.call-start = ((), (), s32[]{:S(2)}) async-start(), calls=%async_computation.2 | async-start | bytes 2621440 | tf_op jit(solution)/shard_map/all_gather | solution.py:349
  10.7 8.3 %collective-permute-start = (bf16[112,1024]{1,0:T(8,128)(2,1)S(1)}, bf16[112,1024]{1,0:T(8,128)(2,1)S(1)}, u32[]{:S(2)}, u32[]{:S(2)}) collective-permute-start(bf16[112,1024]{1,0:T(8,128)(2,1)S(1)} %get-tuple-element.29), channel_id=1, source_target_pairs={{0,252},{4,0},{8,4},{12,8},{16,12},{20,16},{24,20},{28,24},{32,28}... | collective-permute-start | bytes 688136 | tf_op jit(solution)/shard_map/ppermute | solution.py:26
  19.1 11.6 %collective-permute-start.3 = (bf16[2,112,1024]{2,1,0:T(8,128)(2,1)S(1)}, bf16[2,112,1024]{2,1,0:T(8,128)(2,1)S(1)}, u32[]{:S(2)}, u32[]{:S(2)}) collective-permute-start(bf16[2,112,1024]{2,1,0:T(8,128)(2,1)S(1)} %pad_maximum_fusion.refs_2_), channel_id=1, source_target_pairs={{0,248},{4,252},{8,0},{12,4},{16,8},{20,12},{24,16},{28,20},{32,24... | collective-permute-start | bytes 1376264 | tf_op jit(solution)/shard_map/ppermute | solution.py:26
  19.3 20.7 %collective-permute-start.1 = (bf16[2,112,1024]{2,1,0:T(8,128)(2,1)S(1)}, bf16[2,112,1024]{2,1,0:T(8,128)(2,1)S(1)}, u32[]{:S(2)}, u32[]{:S(2)}) collective-permute-start(bf16[2,112,1024]{2,1,0:T(8,128)(2,1)S(1)} %pad_maximum_fusion.refs_2_), channel_id=1, source_target_pairs={{0,8},{4,12},{8,16},{12,20},{16,24},{20,28},{24,32},{28,36},{32,40... | collective-permute-start | bytes 1376264 | tf_op jit(solution)/shard_map/ppermute | solution.py:26
  21.4 29.8 %copy-start = (bf16[1024,2,256]{2,1,0:T(2,128)(2,1)S(1)}, bf16[1024,2,256]{2,1,0:T(2,128)(2,1)}, u32[]{:S(2)}) copy-start(bf16[1024,2,256]{2,1,0:T(2,128)(2,1)} %param.5) | copy-start | bytes 3145732
  43.3 26.0 %all-to-all-start = ((bf16[16,22,2,4,128]{4,3,2,1,0:T(4,128)(2,1)}), bf16[16,22,2,4,128]{4,3,2,1,0:T(4,128)(2,1)}, u32[]{:S(2)}, u32[]{:S(2)}) async-start(bf16[16,22,2,4,128]{4,3,2,1,0:T(4,128)(2,1)} %copy.29), calls=%async_computation | async-start | bytes 1441792 | tf_op jit(solution)/shard_map/all_to_all | solution.py:357
  51.1 63.3 %all-gather.4.cloned.1.call-start = ((), (), s32[]{:S(2)}) async-start(), calls=%async_computation.1 | async-start | bytes 3604480 | tf_op jit(solution)/shard_map/all_gather | solution.py:359
  54.4 22.1 %collective-permute-start.2 = (bf16[2,112,1024]{2,1,0:T(8,128)(2,1)S(1)}, bf16[2,112,1024]{2,1,0:T(8,128)(2,1)S(1)}, u32[]{:S(2)}, u32[]{:S(2)}) collective-permute-start(bf16[2,112,1024]{2,1,0:T(8,128)(2,1)S(1)} %collective-permute-done.1.refs_1_), channel_id=1, source_target_pairs={{0,8},{4,12},{8,16},{12,20},{16,24},{20,28},{24,32},{28,36},{32,40... | collective-permute-start | bytes 1376264 | tf_op jit(solution)/shard_map/ppermute | solution.py:26
  55.9 20.6 %collective-permute-start.4 = (bf16[2,112,1024]{2,1,0:T(8,128)(2,1)S(1)}, bf16[2,112,1024]{2,1,0:T(8,128)(2,1)S(1)}, u32[]{:S(2)}, u32[]{:S(2)}) collective-permute-start(bf16[2,112,1024]{2,1,0:T(8,128)(2,1)S(1)} %collective-permute-done.3.refs_3_), channel_id=1, source_target_pairs={{0,248},{4,252},{8,0},{12,4},{16,8},{20,12},{24,16},{28,20},{32,24... | collective-permute-start | bytes 1376264 | tf_op jit(solution)/shard_map/ppermute | solution.py:26
  131.0 2.2 %collective-permute-start.5 = (bf16[2,8,3,56,128]{4,3,2,1,0:T(8,128)(2,1)S(1)}, bf16[2,8,3,56,128]{4,3,2,1,0:T(8,128)(2,1)S(1)}, u32[]{:S(2)}, u32[]{:S(2)}) collective-permute-start(bf16[2,8,3,56,128]{4,3,2,1,0:T(8,128)(2,1)S(1)} %slice.218), channel_id=1, source_target_pairs={{0,1},{1,0},{2,3},{3,2},{4,5},{5,4},{6,7},{7,6},{8,9},{9,8},{10,11... | collective-permute-start | bytes 2064392 | tf_op jit(solution)/shard_map/ppermute | solution.py:365
  133.3 11.7 %collective-permute-start.6 = (bf16[8,3,56,128]{3,2,1,0:T(8,128)(2,1)S(1)}, bf16[8,3,56,128]{3,2,1,0:T(8,128)(2,1)S(1)}, u32[]{:S(2)}, u32[]{:S(2)}) collective-permute-start(bf16[8,3,56,128]{3,2,1,0:T(8,128)(2,1)S(1)} %fusion.5), channel_id=1, source_target_pairs={{0,2},{2,0},{1,3},{3,1},{4,6},{6,4},{5,7},{7,5},{8,10},{10,8},{9,1... | collective-permute-start | bytes 1032200 | tf_op jit(solution)/shard_map/ppermute | solution.py:368
  145.3 9.4 %collective-permute-start.7 = (bf16[3,3,56,128]{3,2,1,0:T(8,128)(2,1)S(1)}, bf16[3,3,56,128]{3,2,1,0:T(8,128)(2,1)S(1)}, u32[]{:S(2)}, u32[]{:S(2)}) collective-permute-start(bf16[3,3,56,128]{3,2,1,0:T(8,128)(2,1)S(1)} %pad_maximum_fusion.1), channel_id=1, source_target_pairs={{0,4},{4,8},{8,12},{12,16},{16,20},{20,24},{24,28},{28,32},{32,36}... | collective-permute-start | bytes 387080 | tf_op jit(solution)/shard_map/ppermute | solution.py:26
  146.1 5.9 %collective-permute-start.8 = (bf16[2,3,56,128]{3,2,1,0:T(8,128)(2,1)S(1)}, bf16[2,3,56,128]{3,2,1,0:T(8,128)(2,1)S(1)}, u32[]{:S(2)}, u32[]{:S(2)}) collective-permute-start(bf16[2,3,56,128]{3,2,1,0:T(8,128)(2,1)S(1)} %pad_maximum_fusion.2), channel_id=1, source_target_pairs={{0,8},{4,12},{8,16},{12,20},{16,24},{20,28},{24,32},{28,36},{32,40... | collective-permute-start | bytes 258056 | tf_op jit(solution)/shard_map/ppermute | solution.py:26
  149.2 5.5 %collective-permute-start.9 = (bf16[2,3,56,128]{3,2,1,0:T(8,128)(2,1)S(1)}, bf16[2,3,56,128]{3,2,1,0:T(8,128)(2,1)S(1)}, u32[]{:S(2)}, u32[]{:S(2)}) collective-permute-start(bf16[2,3,56,128]{3,2,1,0:T(8,128)(2,1)S(1)} %pad_maximum_fusion.3), channel_id=1, source_target_pairs={{0,252},{4,0},{8,4},{12,8},{16,12},{20,16},{24,20},{28,24},{32,28}... | collective-permute-start | bytes 258056 | tf_op jit(solution)/shard_map/ppermute | solution.py:26
  154.8 8.1 %collective-permute-start.10 = (bf16[3,56,128]{2,1,0:T(8,128)(2,1)S(1)}, bf16[3,56,128]{2,1,0:T(8,128)(2,1)S(1)}, u32[]{:S(2)}, u32[]{:S(2)}) collective-permute-start(bf16[3,56,128]{2,1,0:T(8,128)(2,1)S(1)} %get-tuple-element.15), channel_id=1, source_target_pairs={{0,240},{4,244},{8,248},{12,252},{16,0},{20,4},{24,8},{28,12},{32,... | collective-permute-start | bytes 129032 | tf_op jit(solution)/shard_map/ppermute | solution.py:26
  161.2 8.2 %collective-permute-start.11 = (bf16[3,56,128]{2,1,0:T(8,128)(2,1)S(1)}, bf16[3,56,128]{2,1,0:T(8,128)(2,1)S(1)}, u32[]{:S(2)}, u32[]{:S(2)}) collective-permute-start(bf16[3,56,128]{2,1,0:T(8,128)(2,1)S(1)} %get-tuple-element.16), channel_id=1, source_target_pairs={{0,16},{4,20},{8,24},{12,28},{16,32},{20,36},{24,40},{28,44},{32,4... | collective-permute-start | bytes 129032 | tf_op jit(solution)/shard_map/ppermute | solution.py:26
Sparse Core Ops, SparseCore 0:
  9.2 30.8 all-gather.5
  71.8 37.3 all-gather.3

commit v8 on v5

--- a/solution.py
+++ b/solution.py
@@ -357,16 +357,14 @@
     zc = zeta_matrix(lax.dynamic_index_in_dim(halves, part // 2, 0, keepdims=False))
     pieces = jnp.transpose(screened.reshape(SLOTS, 2, 4, WIN, 128), (3, 0, 1, 2, 4))
     pieces = jnp.concatenate([pieces, pieces], axis=0)
-    pieces = pieces + message[0, 0] * 0
     line = 2 * WIN
     near_groups = [[x * line + s for s in range(line)] for x in range(ka_count // line)]
     x_groups = [[x * line + s for x in range(ka_count // line)] for s in range(line)]
     pieces = lax.all_to_all(pieces, "ka", 0, 0, axis_index_groups=near_groups, tiled=True)
     rows = jnp.transpose(pieces, (1, 2, 0, 3, 4)).reshape(SLOTS, 2, 4 * line, 128)
     w = lax.all_gather(rows, "ka", axis_index_groups=x_groups)
-    zero = rows[0, 0, 0, 0] * 0
-    ahead2 = from_behind(ahead + zero, "ka", -2)
-    behind2 = from_behind(behind + zero, "ka", 2)
+    ahead2 = from_behind(ahead, "ka", -2)
+    behind2 = from_behind(behind, "ka", 2)
     mv, mc, _ = densities((behind, here, ahead), False, zv, zc, None)
     mv, mc, words = densities((behind2, behind, here, ahead, ahead2), True, zv, zc, (mv, mc))
     order, slot_of, used = schedule(words[:, :PAIRS].reshape(TOTAL))

time: 172 us -> 170 us (0.988)
  waiting for transfers between devices: 54.1 us -> 57.1 us
  local copies, waits for them, and re-layouts: 12.2 us -> 10.1 us
  other arithmetic: 6.82 us -> 4.75 us
    ppermute x10, waiting for transfers between devices: 42.6 us -> 45.6 us  [from_behind(): return lax.ppermute(x, axis, [(i, (i + by) % count) for i in range(count)])]
    slice x2 -> x0, local copies, waits for them, and re-layouts: 1.74 us -> none  [the longest x1 1.19 us: body(): pieces = pieces + message[0, 0] * 0]
  transfers between devices with their start and end apart: 15 -> 15, of which waited for: 9 -> 9; matrix products, arithmetic and copies ran while one was open for 9% -> 7% of each run, Pallas kernels for 23% -> 24%
where the time goes in v8:
time: 170 us; the launch traced here: 169 us
  Pallas kernels  58 us (34%)
  waiting for transfers between devices  57.1 us (34%)
  starting transfers between devices  25.6 us (15%)
  between operations  13.7 us (8%)
  local copies, waits for them, and re-layouts  10.1 us (6%)
  other arithmetic  4.75 us (3%)
    ppermute x10, waiting for transfers between devices, from_behind(): return lax.ppermute(x, axis, [(i, (i + by) % count) for i in range(count)])  45.6 us
    pallas_call x2, Pallas kernels, densities(): pl.pallas_call(functools.partial(density_kernel, count, rest, steps), gri...  39.9 us
    pallas_call x1, Pallas kernels, apply_screened(): pl.pallas_call(apply_kernel, in_specs=[smem] * 4 + [pl.BlockSpec(memory_s...  16.4 us
    ppermute x10, starting transfers between devices, from_behind(): return lax.ppermute(x, axis, [(i, (i + by) % count) for i in range(count)])  13.6 us
    all_to_all x1, starting transfers between devices, body(): lax.all_to_all(pieces, 'ka', 0, 0, axis_index_groups=near_groups, tiled=T...  9.49 us
    ppermute x1, waiting for transfers between devices, body(): lax.ppermute(other, 'ga', [(0, 2), (2, 0), (1, 3), (3, 1)]).astype(f32)  9.3 us
  transfers between devices with their start and end apart: 15, of which 9 were waited for; matrix products, arithmetic and copies ran while one was open for 7% of the time, Pallas kernels for 24%

profile of v8, /device:TPU:40, one launch (start us, length us, event | category | flops | bytes accessed | tf_op | source)
XLA Modules:
  0.0 169.2 jit_solution(16417495559728418621)
XLA Ops:
  6.5 2.2 %constant_dynamic-slice_fusion.1 = bf16[1024,2,128]{2,1,0:T(2,128)(2,1)} fusion(bf16[1024,2,256]{2,1,0:T(2,128)(2,1)} %param.5, s32[]{:T(128)S(6)} %select_n.41), kind=kLoop, calls=%fused_computation.58 | loop fusion | bytes 1048580 | tf_op jit(solution)/shard_map/dynamic_slice | solution.py:355
  8.8 1.1 reshape.105
  10.0 1.1 copy.31
  11.2 9.5 %all-to-all-start = ((bf16[16,22,2,4,128]{4,3,2,1,0:T(4,128)(2,1)}), bf16[16,22,2,4,128]{4,3,2,1,0:T(4,128)(2,1)S(1)}, u32[]{:S(2)}, u32[]{:S(2)}) async-start(bf16[16,22,2,4,128]{4,3,2,1,0:T(4,128)(2,1)} %copy.31), calls=%async_computation | async-start | bytes 1441792 | tf_op jit(solution)/shard_map/all_to_all | solution.py:363
  21.0 0.7 fusion.13
  21.7 0.6 collective-permute-start
  22.3 1.5 fusion.17
  23.8 0.9 copy.41
  24.7 18.5 %collective-permute-done = bf16[112,1024]{1,0:T(8,128)(2,1)S(1)} collective-permute-done((bf16[112,1024]{1,0:T(8,128)(2,1)}, bf16[112,1024]{1,0:T(8,128)(2,1)S(1)}, u32[]{:S(2)}, u32[]{:S(2)}) %collective-permute-start) | collective-permute-done | bytes 229408 | tf_op jit(solution)/shard_map/ppermute | solution.py:26
  43.2 1.8 %collective-permute-start.1 = (bf16[2,112,1024]{2,1,0:T(8,128)(2,1)S(1)}, bf16[2,112,1024]{2,1,0:T(8,128)(2,1)S(1)}, u32[]{:S(2)}, u32[]{:S(2)}) collective-permute-start(bf16[2,112,1024]{2,1,0:T(8,128)(2,1)S(1)} %pad_maximum_fusion.1.refs_1_.refs_2_), channel_id=1, source_target_pairs={{0,8},{4,12},{8,16},{12,20},{16,24},{20,28},{24,32},{28,36},{32,40... | collective-permute-start | bytes 1376264 | tf_op jit(solution)/shard_map/ppermute | solution.py:26
  45.4 1.5 maximum_maximum_fusion.refs_3_.refs_5_
  46.9 7.9 %collective-permute-done.1.refs_0_.refs_1_ = bf16[2,112,1024]{2,1,0:T(8,128)(2,1)S(1)} collective-permute-done((bf16[2,112,1024]{2,1,0:T(8,128)(2,1)S(1)}, bf16[2,112,1024]{2,1,0:T(8,128)(2,1)S(1)}, u32[]{:S(2)}, u32[]{:S(2)}) %collective-permute-start.1) | collective-permute-done | bytes 458784 | tf_op jit(solution)/shard_map/ppermute | solution.py:26
  54.8 2.3 %collective-permute-start.2 = (bf16[2,112,1024]{2,1,0:T(8,128)(2,1)S(1)}, bf16[2,112,1024]{2,1,0:T(8,128)(2,1)S(1)}, u32[]{:S(2)}, u32[]{:S(2)}) collective-permute-start(bf16[2,112,1024]{2,1,0:T(8,128)(2,1)S(1)} %collective-permute-done.1.refs_0_.refs_1_), channel_id=1, source_target_pairs={{0,8},{4,12},{8,16},{12,20},{16,24},{20,28},{24,32},{28,36},{32,40... | collective-permute-start | bytes 1376264 | tf_op jit(solution)/shard_map/ppermute | solution.py:26
  57.0 0.5 collective-permute-done.3.refs_2_.refs_3_
  57.5 1.9 %collective-permute-start.4 = (bf16[2,112,1024]{2,1,0:T(8,128)(2,1)S(1)}, bf16[2,112,1024]{2,1,0:T(8,128)(2,1)S(1)}, u32[]{:S(2)}, u32[]{:S(2)}) collective-permute-start(bf16[2,112,1024]{2,1,0:T(8,128)(2,1)S(1)} %collective-permute-done.3.refs_2_.refs_3_), channel_id=1, source_target_pairs={{0,248},{4,252},{8,0},{12,4},{16,8},{20,12},{24,16},{28,20},{32,24... | collective-permute-start | bytes 1376264 | tf_op jit(solution)/shard_map/ppermute | solution.py:26
  59.4 1.3 copy.32
  60.7 1.4 constant_dynamic-slice_fusion
  62.4 19.8 %densities.2 = (bf16[576,16,512]{2,1,0:T(8,128)(2,1)}, bf16[576,16,256]{2,1,0:T(8,128)(2,1)}, s32[6,128]{1,0:T(8,128)}) custom-call(bf16[2,112,1024]{2,1,0:T(8,128)(2,1)S(1)} %collective-permute-done.1.refs_0_.refs_1_, bf16[2,112,1024]{2,1,0:T(8,128)(2,1)S(1)} %pad_maximum_fusion.1.refs_1_.refs_2_, ...), custom_call_target="tpu_custom_call" | custom-call | flops 14495514624 | bytes 18874368 | tf_op jit(solution)/shard_map/densities/pallas_call | solution.py:140
  82.2 20.1 %densities.3 = (bf16[576,16,512]{2,1,0:T(8,128)(2,1)}, bf16[576,16,256]{2,1,0:T(8,128)(2,1)}, s32[8,128]{1,0:T(8,128)S(1)}) custom-call(bf16[2,112,1024]{2,1,0:T(8,128)(2,1)S(1)} %collective-permute-done.2.refs_0_, bf16[2,112,1024]{2,1,0:T(8,128)(2,1)S(1)} %collective-permute-done.1.refs_0_.refs_1_, ...), custom_call_target="tpu_custom_call", output_to_operand_aliasing={{0}: (7, {}), {1}: (8, {})} | custom-call | flops 14495514624 | bytes 18874368 | tf_op jit(solution)/shard_map/densities/pallas_call | solution.py:140
  102.5 0.6 fusion.15
  103.7 0.3 select_reduce_fusion
  104.1 16.4 %apply_screened.1 = f32[4,8,3,56,128]{4,3,2,1,0:T(8,128)S(1)} custom-call(s32[960]{0:T(1024)S(1)} %broadcast_add_fusion.order_ref, s32[60]{0:T(128)S(1)} %broadcast_minimum_fusion.slot_ref, s32[1]{0:T(128)} %bitcast.12.used_ref, s32[1]{0:T(128)} %bitcast.ga_ref, bf16[576,16,512]{2,1,0:T(8,128)(2,1)} %get-tuple-element.13.mv_hbm, ...), custom_call_target="tpu_custom_call" | custom-call | flops 6000000000 | bytes 18874368 | tf_op jit(solution)/shard_map/apply_screened/pallas_call | solution.py:255
  120.7 2.1 %collective-permute-done.5 = bf16[2,8,3,56,128]{4,3,2,1,0:T(8,128)(2,1)S(1)} collective-permute-done((bf16[2,8,3,56,128]{4,3,2,1,0:T(8,128)(2,1)S(1)}, bf16[2,8,3,56,128]{4,3,2,1,0:T(8,128)(2,1)S(1)}, u32[]{:S(2)}, u32[]{:S(2)}) %collective-permute-start.5) | collective-permute-done | bytes 688160 | tf_op jit(solution)/shard_map/ppermute | solution.py:372
  122.9 2.4 %collective-permute-start.6 = (bf16[8,3,56,128]{3,2,1,0:T(8,128)(2,1)S(1)}, bf16[8,3,56,128]{3,2,1,0:T(8,128)(2,1)S(1)}, u32[]{:S(2)}, u32[]{:S(2)}) collective-permute-start(bf16[8,3,56,128]{3,2,1,0:T(8,128)(2,1)S(1)} %fusion.5), channel_id=1, source_target_pairs={{0,2},{2,0},{1,3},{3,1},{4,6},{6,4},{5,7},{7,5},{8,10},{10,8},{9,1... | collective-permute-start | bytes 1032200 | tf_op jit(solution)/shard_map/ppermute | solution.py:375
  125.3 9.3 %collective-permute-done.6 = bf16[8,3,56,128]{3,2,1,0:T(8,128)(2,1)S(1)} collective-permute-done((bf16[8,3,56,128]{3,2,1,0:T(8,128)(2,1)S(1)}, bf16[8,3,56,128]{3,2,1,0:T(8,128)(2,1)S(1)}, u32[]{:S(2)}, u32[]{:S(2)}) %collective-permute-start.6) | collective-permute-done | bytes 344096 | tf_op jit(solution)/shard_map/ppermute | solution.py:375
  135.2 3.0 %collective-permute-start.7 = (bf16[3,3,56,128]{3,2,1,0:T(8,128)(2,1)S(1)}, bf16[3,3,56,128]{3,2,1,0:T(8,128)(2,1)S(1)}, u32[]{:S(2)}, u32[]{:S(2)}) collective-permute-start(bf16[3,3,56,128]{3,2,1,0:T(8,128)(2,1)S(1)} %pad_maximum_fusion.2), channel_id=1, source_target_pairs={{0,4},{4,8},{8,12},{12,16},{16,20},{20,24},{24,28},{28,32},{32,36}... | collective-permute-start | bytes 387080 | tf_op jit(solution)/shard_map/ppermute | solution.py:26
  138.5 2.1 %collective-permute-done.9 = bf16[2,3,56,128]{3,2,1,0:T(8,128)(2,1)S(1)} collective-permute-done((bf16[2,3,56,128]{3,2,1,0:T(8,128)(2,1)S(1)}, bf16[2,3,56,128]{3,2,1,0:T(8,128)(2,1)S(1)}, u32[]{:S(2)}, u32[]{:S(2)}) %collective-permute-start.9) | collective-permute-done | bytes 86048 | tf_op jit(solution)/shard_map/ppermute | solution.py:26
  140.6 7.1 %collective-permute-done.8 = bf16[2,3,56,128]{3,2,1,0:T(8,128)(2,1)S(1)} collective-permute-done((bf16[2,3,56,128]{3,2,1,0:T(8,128)(2,1)S(1)}, bf16[2,3,56,128]{3,2,1,0:T(8,128)(2,1)S(1)}, u32[]{:S(2)}, u32[]{:S(2)}) %collective-permute-start.8) | collective-permute-done | bytes 86048 | tf_op jit(solution)/shard_map/ppermute | solution.py:26
  147.8 3.3 %collective-permute-start.10 = (f32[3,56,128]{2,1,0:T(8,128)S(1)}, f32[3,56,128]{2,1,0:T(8,128)S(1)}, u32[]{:S(2)}, u32[]{:S(2)}) collective-permute-start(f32[3,56,128]{2,1,0:T(8,128)S(1)} %get-tuple-element.19), channel_id=1, source_target_pairs={{0,240},{4,244},{8,248},{12,252},{16,0},{20,4},{24,8},{28,12},{32,... | collective-permute-start | bytes 258056 | tf_op jit(solution)/shard_map/ppermute | solution.py:26
  151.1 2.4 %collective-permute-done.10 = f32[3,56,128]{2,1,0:T(8,128)S(1)} collective-permute-done((f32[3,56,128]{2,1,0:T(8,128)S(1)}, f32[3,56,128]{2,1,0:T(8,128)S(1)}, u32[]{:S(2)}, u32[]{:S(2)}) %collective-permute-start.10) | collective-permute-done | bytes 86048 | tf_op jit(solution)/shard_map/ppermute | solution.py:26
  153.5 7.2 %collective-permute-done.11 = f32[3,56,128]{2,1,0:T(8,128)S(1)} collective-permute-done((f32[3,56,128]{2,1,0:T(8,128)S(1)}, f32[3,56,128]{2,1,0:T(8,128)S(1)}, u32[]{:S(2)}, u32[]{:S(2)}) %collective-permute-start.11) | collective-permute-done | bytes 86048 | tf_op jit(solution)/shard_map/ppermute | solution.py:26
  160.7 1.7 arrange.1
  (61 shorter events, 3.2 us)
Async XLA Ops:
  6.5 54.1 %all-gather.6.cloned.1.call-start = ((), (), s32[]{:S(2)}) async-start(), calls=%async_computation.2 | async-start | bytes 2621440 | tf_op jit(solution)/shard_map/all_gather | solution.py:356
  9.9 10.8 %copy-start.3 = (s32[6,2,6]{2,1,0:T(2,128)S(1)}, s32[6,2,6]{2,1,0:T(2,128)}, u32[]{:S(2)}) copy-start(s32[6,2,6]{2,1,0:T(2,128)} %param.7) | copy-start | bytes 868
  9.9 11.1 %copy-start.2 = (bf16[6,2,8,1024]{3,2,1,0:T(8,128)(2,1)S(1)}, bf16[6,2,8,1024]{3,2,1,0:T(8,128)(2,1)}, u32[]{:S(2)}) copy-start(bf16[6,2,8,1024]{3,2,1,0:T(8,128)(2,1)} %param.4) | copy-start | bytes 589828
  9.9 12.4 %copy-start = (bf16[1024,2,256]{2,1,0:T(2,128)(2,1)S(1)}, bf16[1024,2,256]{2,1,0:T(2,128)(2,1)}, u32[]{:S(2)}) copy-start(bf16[1024,2,256]{2,1,0:T(2,128)(2,1)} %param.5) | copy-start | bytes 3145732
  11.2 48.2 %all-to-all-start = ((bf16[16,22,2,4,128]{4,3,2,1,0:T(4,128)(2,1)}), bf16[16,22,2,4,128]{4,3,2,1,0:T(4,128)(2,1)S(1)}, u32[]{:S(2)}, u32[]{:S(2)}) async-start(bf16[16,22,2,4,128]{4,3,2,1,0:T(4,128)(2,1)} %copy.31), calls=%async_computation | async-start | bytes 1441792 | tf_op jit(solution)/shard_map/all_to_all | solution.py:363
  20.7 83.4 %all-gather.4.cloned.1.call-start = ((), (), s32[]{:S(2)}) async-start(), calls=%async_computation.1 | async-start | bytes 3604480 | tf_op jit(solution)/shard_map/all_gather | solution.py:365
  21.7 21.4 %collective-permute-start = (bf16[112,1024]{1,0:T(8,128)(2,1)}, bf16[112,1024]{1,0:T(8,128)(2,1)S(1)}, u32[]{:S(2)}, u32[]{:S(2)}) collective-permute-start(bf16[112,1024]{1,0:T(8,128)(2,1)} %get-tuple-element.33), channel_id=1, source_target_pairs={{0,252},{4,0},{8,4},{12,8},{16,12},{20,16},{24,20},{28,24},{32,28}... | collective-permute-start | bytes 688136 | tf_op jit(solution)/shard_map/ppermute | solution.py:26
  24.6 20.7 %copy-start.1 = (bf16[1024,1,256]{2,0,1:T(8,128)(2,1)S(1)}, bf16[1024,1,256]{2,0,1:T(8,128)(2,1)}, u32[]{:S(2)}) copy-start(bf16[1024,1,256]{2,0,1:T(8,128)(2,1)} %copy.41) | copy-start | bytes 1572868
  43.2 11.6 %collective-permute-start.1 = (bf16[2,112,1024]{2,1,0:T(8,128)(2,1)S(1)}, bf16[2,112,1024]{2,1,0:T(8,128)(2,1)S(1)}, u32[]{:S(2)}, u32[]{:S(2)}) collective-permute-start(bf16[2,112,1024]{2,1,0:T(8,128)(2,1)S(1)} %pad_maximum_fusion.1.refs_1_.refs_2_), channel_id=1, source_target_pairs={{0,8},{4,12},{8,16},{12,20},{16,24},{20,28},{24,32},{28,36},{32,40... | collective-permute-start | bytes 1376264 | tf_op jit(solution)/shard_map/ppermute | solution.py:26
  45.0 12.5 %collective-permute-start.3 = (bf16[2,112,1024]{2,1,0:T(8,128)(2,1)S(1)}, bf16[2,112,1024]{2,1,0:T(8,128)(2,1)S(1)}, u32[]{:S(2)}, u32[]{:S(2)}) collective-permute-start(bf16[2,112,1024]{2,1,0:T(8,128)(2,1)S(1)} %pad_maximum_fusion.1.refs_1_.refs_2_), channel_id=1, source_target_pairs={{0,248},{4,252},{8,0},{12,4},{16,8},{20,12},{24,16},{28,20},{32,24... | collective-permute-start | bytes 1376264 | tf_op jit(solution)/shard_map/ppermute | solution.py:26
  54.8 27.4 %collective-permute-start.2 = (bf16[2,112,1024]{2,1,0:T(8,128)(2,1)S(1)}, bf16[2,112,1024]{2,1,0:T(8,128)(2,1)S(1)}, u32[]{:S(2)}, u32[]{:S(2)}) collective-permute-start(bf16[2,112,1024]{2,1,0:T(8,128)(2,1)S(1)} %collective-permute-done.1.refs_0_.refs_1_), channel_id=1, source_target_pairs={{0,8},{4,12},{8,16},{12,20},{16,24},{20,28},{24,32},{28,36},{32,40... | collective-permute-start | bytes 1376264 | tf_op jit(solution)/shard_map/ppermute | solution.py:26
  57.5 24.7 %collective-permute-start.4 = (bf16[2,112,1024]{2,1,0:T(8,128)(2,1)S(1)}, bf16[2,112,1024]{2,1,0:T(8,128)(2,1)S(1)}, u32[]{:S(2)}, u32[]{:S(2)}) collective-permute-start(bf16[2,112,1024]{2,1,0:T(8,128)(2,1)S(1)} %collective-permute-done.3.refs_2_.refs_3_), channel_id=1, source_target_pairs={{0,248},{4,252},{8,0},{12,4},{16,8},{20,12},{24,16},{28,20},{32,24... | collective-permute-start | bytes 1376264 | tf_op jit(solution)/shard_map/ppermute | solution.py:26
  120.6 2.2 %collective-permute-start.5 = (bf16[2,8,3,56,128]{4,3,2,1,0:T(8,128)(2,1)S(1)}, bf16[2,8,3,56,128]{4,3,2,1,0:T(8,128)(2,1)S(1)}, u32[]{:S(2)}, u32[]{:S(2)}) collective-permute-start(bf16[2,8,3,56,128]{4,3,2,1,0:T(8,128)(2,1)S(1)} %slice.196), channel_id=1, source_target_pairs={{0,1},{1,0},{2,3},{3,2},{4,5},{5,4},{6,7},{7,6},{8,9},{9,8},{10,11... | collective-permute-start | bytes 2064392 | tf_op jit(solution)/shard_map/ppermute | solution.py:372
  122.9 11.7 %collective-permute-start.6 = (bf16[8,3,56,128]{3,2,1,0:T(8,128)(2,1)S(1)}, bf16[8,3,56,128]{3,2,1,0:T(8,128)(2,1)S(1)}, u32[]{:S(2)}, u32[]{:S(2)}) collective-permute-start(bf16[8,3,56,128]{3,2,1,0:T(8,128)(2,1)S(1)} %fusion.5), channel_id=1, source_target_pairs={{0,2},{2,0},{1,3},{3,1},{4,6},{6,4},{5,7},{7,5},{8,10},{10,8},{9,1... | collective-permute-start | bytes 1032200 | tf_op jit(solution)/shard_map/ppermute | solution.py:375
  134.9 5.7 %collective-permute-start.9 = (bf16[2,3,56,128]{3,2,1,0:T(8,128)(2,1)S(1)}, bf16[2,3,56,128]{3,2,1,0:T(8,128)(2,1)S(1)}, u32[]{:S(2)}, u32[]{:S(2)}) collective-permute-start(bf16[2,3,56,128]{3,2,1,0:T(8,128)(2,1)S(1)} %pad_maximum_fusion.4), channel_id=1, source_target_pairs={{0,252},{4,0},{8,4},{12,8},{16,12},{20,16},{24,20},{28,24},{32,28}... | collective-permute-start | bytes 258056 | tf_op jit(solution)/shard_map/ppermute | solution.py:26
  135.2 12.4 %collective-permute-start.7 = (bf16[3,3,56,128]{3,2,1,0:T(8,128)(2,1)S(1)}, bf16[3,3,56,128]{3,2,1,0:T(8,128)(2,1)S(1)}, u32[]{:S(2)}, u32[]{:S(2)}) collective-permute-start(bf16[3,3,56,128]{3,2,1,0:T(8,128)(2,1)S(1)} %pad_maximum_fusion.2), channel_id=1, source_target_pairs={{0,4},{4,8},{8,12},{12,16},{16,20},{20,24},{24,28},{28,32},{32,36}... | collective-permute-start | bytes 387080 | tf_op jit(solution)/shard_map/ppermute | solution.py:26
  138.2 9.4 %collective-permute-start.8 = (bf16[2,3,56,128]{3,2,1,0:T(8,128)(2,1)S(1)}, bf16[2,3,56,128]{3,2,1,0:T(8,128)(2,1)S(1)}, u32[]{:S(2)}, u32[]{:S(2)}) collective-permute-start(bf16[2,3,56,128]{3,2,1,0:T(8,128)(2,1)S(1)} %pad_maximum_fusion.3), channel_id=1, source_target_pairs={{0,8},{4,12},{8,16},{12,20},{16,24},{20,28},{24,32},{28,36},{32,40... | collective-permute-start | bytes 258056 | tf_op jit(solution)/shard_map/ppermute | solution.py:26
  147.8 5.7 %collective-permute-start.10 = (f32[3,56,128]{2,1,0:T(8,128)S(1)}, f32[3,56,128]{2,1,0:T(8,128)S(1)}, u32[]{:S(2)}, u32[]{:S(2)}) collective-permute-start(f32[3,56,128]{2,1,0:T(8,128)S(1)} %get-tuple-element.19), channel_id=1, source_target_pairs={{0,240},{4,244},{8,248},{12,252},{16,0},{20,4},{24,8},{28,12},{32,... | collective-permute-start | bytes 258056 | tf_op jit(solution)/shard_map/ppermute | solution.py:26
  151.0 9.6 %collective-permute-start.11 = (f32[3,56,128]{2,1,0:T(8,128)S(1)}, f32[3,56,128]{2,1,0:T(8,128)S(1)}, u32[]{:S(2)}, u32[]{:S(2)}) collective-permute-start(f32[3,56,128]{2,1,0:T(8,128)S(1)} %get-tuple-element.20), channel_id=1, source_target_pairs={{0,16},{4,20},{8,24},{12,28},{16,32},{20,36},{24,40},{28,44},{32,4... | collective-permute-start | bytes 258056 | tf_op jit(solution)/shard_map/ppermute | solution.py:26
Sparse Core Ops, SparseCore 0:
  9.2 40.3 all-gather.5
  60.8 40.2 all-gather.3
